TPU v7x, 128 devices: a whole 4x4x4 slice. The times are simulated.
128 devices in a mesh: row: 16 (over y, x_hi, core), col: 8 (over x_lo, z).
Axes of the slice: x: 4 (x_hi: 2, x_lo: 2; x = x_hi * 2 + x_lo), y: 4, z: 4, core: 2. Of those that a mesh axis runs over, the one named last changes fastest.
Arguments:
- inputs: bfloat16 [512, 12288], P('col', 'row'), may hold values from -6 to 6
- cotangent: bfloat16 [512, 12288], P('col', 'row'), may hold values from -6 to 6
- weight_in: bfloat16 [12288, 24576], P('row', 'col'), may hold values from -0.0546875 to 0.0546875
- weight_out: bfloat16 [24576, 12288], P('col', 'row'), may hold values from -0.0390625 to 0.0390625
Outputs:
- weight_in_grad: bfloat16 [12288, 24576], P('row', 'col')
- weight_out_grad: bfloat16 [24576, 12288], P('col', 'row')
- inputs_grad: bfloat16 [512, 12288], P('col', 'row')
All inputs are finite; a program needn't handle non-finite values.
Results may differ from a plain program's by a relative error of at most 0.005.
Values may be sent and summed in bfloat16 or wider, within the bound.
No kernel may reach another device: no remote copies, remote signals or barrier semaphores. Data moves between devices by JAX's collectives and lax.ppermute only.
A program may use at most 128 MiB of HBM per device.

v0:
```python
import math

import jax
import jax.numpy as jnp
from jax import lax
from jax.sharding import PartitionSpec as P


def gelu_value(v):
    inner = math.sqrt(2.0 / math.pi) * (v + 0.044715 * v * v * v)
    return 0.5 * v * (1.0 + jnp.tanh(inner))


def gelu_slope(v):
    coeff = math.sqrt(2.0 / math.pi)
    tanh_part = jnp.tanh(coeff * (v + 0.044715 * v * v * v))
    return 0.5 * (1.0 + tanh_part) + 0.5 * v * (1.0 - tanh_part * tanh_part) * coeff * (
        1.0 + 3.0 * 0.044715 * v * v
    )


def on_device(inputs, cotangent, weight_in, weight_out):
    inputs_all, cotangent_all = (
        lax.all_gather(inputs, "col", axis=0, tiled=True),
        lax.all_gather(cotangent, "col", axis=0, tiled=True),
    )
    per_row = inputs_all.shape[0] // lax.axis_size("row")
    pre_full = lax.psum(jnp.dot(inputs_all, weight_in, preferred_element_type=jnp.float32), "row")
    pre = lax.dynamic_slice_in_dim(pre_full, lax.axis_index("row") * per_row, per_row, 0)
    act_all = gelu_value(pre_full).astype(jnp.bfloat16)
    act_grad = lax.psum_scatter(
        lax.dot_general(
            cotangent_all, weight_out, (((1,), (1,)), ((), ())), preferred_element_type=jnp.float32
        ),
        "row",
        scatter_dimension=0,
        tiled=True,
    )
    pre_grad = (act_grad * gelu_slope(pre)).astype(jnp.bfloat16)
    weight_out_grad = lax.dot_general(
        act_all, cotangent_all, (((0,), (0,)), ((), ())), preferred_element_type=jnp.float32
    ).astype(jnp.bfloat16)
    grad_all = lax.all_gather(pre_grad, "row", axis=0, tiled=True)
    weight_total = lax.dot_general(
        inputs_all, grad_all, (((0,), (0,)), ((), ())), preferred_element_type=jnp.float32
    )
    input_partial = lax.dot_general(
        grad_all, weight_in, (((1,), (1,)), ((), ())), preferred_element_type=jnp.float32
    )
    weight_in_grad = weight_total.astype(jnp.bfloat16)
    inputs_grad = lax.psum_scatter(input_partial, "col", scatter_dimension=0, tiled=True).astype(
        jnp.bfloat16
    )
    return (weight_in_grad, weight_out_grad, inputs_grad)


def solution(mesh):
    return jax.shard_map(
        on_device,
        mesh=mesh,
        in_specs=(P("col", "row"), P("col", "row"), P("row", "col"), P("col", "row")),
        out_specs=(P("row", "col"), P("col", "row"), P("col", "row")),
        check_vma=False,
    )
```

profile of v0, /device:TPU:0, one launch (start us, length us, event | category | flops | bytes accessed | tf_op | source)
XLA Modules:
  0.0 418.1 jit_solution(11808330580543765945)
XLA Ops:
  7.2 0.0 all-reduce.2.cloned.1.call-start
  7.2 31.2 %all_gather.10 = bf16[512,768]{1,0:T(8,128)(2,1)S(1)} all-gather(bf16[64,768]{1,0:T(8,128)(2,1)} %param.4), channel_id=1, replica_groups=mesh['row'=16,'col'=8] {'col'}, dimensions={0}, use_global_device_ids=true | all-gather | bytes 884736 | tf_op jit(solution)/shard_map/all_gather | solution.py:24
  38.5 6.8 %fusion.23 = f32[512,3072]{1,0:T(8,128)} fusion(bf16[512,768]{1,0:T(8,128)(2,1)S(1)} %all_gather.10, bf16[768,3072]{1,0:T(8,128)(2,1)} %param.6), kind=kOutput, calls=%fused_computation.27 | convolution fusion | flops 2415919104 | bytes 11796480 | tf_op jit(solution)/shard_map/dot_general | solution.py:28
  45.2 0.0 copy-start
  45.2 0.0 all-reduce.2.cloned.1.call-update
  45.2 0.0 reduce-scatter.3.cloned.1.call-start
  45.3 0.8 copy-done
  46.1 30.9 %all_gather.9 = bf16[512,768]{1,0:T(8,128)(2,1)S(1)} all-gather(bf16[64,768]{1,0:T(8,128)(2,1)S(1)} %copy-done), channel_id=1, replica_groups=mesh['row'=16,'col'=8] {'col'}, dimensions={0}, use_global_device_ids=true | all-gather | bytes 884736 | tf_op jit(solution)/shard_map/all_gather | solution.py:25
  77.0 6.9 %fusion.22 = f32[512,3072]{1,0:T(8,128)} fusion(bf16[512,768]{1,0:T(8,128)(2,1)S(1)} %all_gather.9, bf16[3072,768]{1,0:T(8,128)(2,1)} %param.7), kind=kOutput, calls=%fused_computation.26 | convolution fusion | flops 2415919104 | bytes 11796480 | tf_op jit(solution)/shard_map/dot_general | solution.py:32
  83.9 0.0 reduce-scatter.3.cloned.1.call-update
  83.9 0.0 all-gather.2.cloned.1.call-start
  84.0 133.5 %all-reduce.2.cloned.1.call-done = f32[512,3072]{1,0:T(8,128)} async-done(((f32[512,3072]{1,0:T(8,128)}), f32[512,3072]{1,0:T(8,128)}) %all-reduce.2.cloned.1.call-update) | async-done | bytes 6291472 | tf_op jit(solution)/shard_map/psum | solution.py:28
  217.4 92.5 %reduce-scatter.3.cloned.1.call-done = f32[32,3072]{1,0:T(8,128)} async-done(((f32[512,3072]{1,0:T(8,128)}), f32[32,3072]{1,0:T(8,128)}) %reduce-scatter.3.cloned.1.call-update) | async-done | bytes 393232 | tf_op jit(solution)/shard_map/reduce_scatter | solution.py:31
  309.9 2.0 fusion.17
  312.0 0.0 all-gather.2.cloned.1.call-update
  312.0 0.0 reduce-scatter.5.cloned.1.call-start
  312.1 50.7 %all-gather.2.cloned.1.call-done = bf16[512,3072]{1,0:T(8,128)(2,1)} async-done(((bf16[32,3072]{1,0:T(8,128)(2,1)}), bf16[512,3072]{1,0:T(8,128)(2,1)}) %all-gather.2.cloned.1.call-update) | async-done | bytes 3145744 | tf_op jit(solution)/shard_map/all_gather | solution.py:43
  362.8 7.1 %fusion.24 = f32[512,768]{1,0:T(8,128)} fusion(bf16[512,3072]{1,0:T(8,128)(2,1)} %all-gather.2.cloned.1.call-done, bf16[768,3072]{1,0:T(8,128)(2,1)} %param.6), kind=kOutput, calls=%fused_computation.28 | convolution fusion | flops 2415919104 | bytes 9437184 | tf_op jit(solution)/shard_map/dot_general | solution.py:47
  369.9 0.0 reduce-scatter.5.cloned.1.call-update
  369.9 0.0 copy-start.1
  369.9 8.5 %convolution_convert_fusion = bf16[3072,768]{1,0:T(8,128)(2,1)} fusion(bf16[512,768]{1,0:T(8,128)(2,1)S(1)} %all_gather.9, f32[512,3072]{1,0:T(8,128)} %all-reduce.2.cloned.1.call-done), kind=kOutput, calls=%fused_computation.6 | convolution fusion | flops 2432434176 | bytes 11796480 | tf_op jit(solution)/shard_map/dot_general | solution.py:40
  378.4 0.0 copy-done.1
  378.4 4.3 %fusion.5 = bf16[768,3072]{0,1:T(8,128)(2,1)} fusion(bf16[512,3072]{1,0:T(8,128)(2,1)S(1)} %copy-done.1, bf16[512,768]{1,0:T(8,128)(2,1)S(1)} %all_gather.10), kind=kOutput, calls=%fused_computation.8 | convolution fusion | flops 2418278400 | bytes 8650752 | tf_op jit(solution)/shard_map/dot_general | solution.py:44
  382.7 6.6 %copy.7 = bf16[768,3072]{1,0:T(8,128)(2,1)} copy(bf16[768,3072]{0,1:T(8,128)(2,1)} %fusion.5) | data formatting | bytes 9437184
  389.3 20.6 %reduce-scatter.5.cloned.1.call-done = f32[64,768]{1,0:T(8,128)} async-done(((f32[512,768]{1,0:T(8,128)}), f32[64,768]{1,0:T(8,128)}) %reduce-scatter.5.cloned.1.call-update) | async-done | bytes 196624 | tf_op jit(solution)/shard_map/reduce_scatter | solution.py:51
  410.0 1.6 convert_element_type.23
Async XLA Ops:
  7.2 210.3 %all-reduce.2.cloned.1.call-start = ((), (), s32[]{:S(2)}) async-start(), calls=%async_computation.3 | async-start | bytes 12582912 | tf_op jit(solution)/shard_map/psum | solution.py:28
  45.2 0.9 copy-start
  45.2 264.7 %reduce-scatter.3.cloned.1.call-start = ((), (), s32[]{:S(2)}) async-start(), calls=%async_computation.2 | async-start | bytes 6684672 | tf_op jit(solution)/shard_map/reduce_scatter | solution.py:31
  83.9 278.9 %all-gather.2.cloned.1.call-start = ((), (), s32[]{:S(2)}) async-start(), calls=%async_computation.4 | async-start | bytes 3342336 | tf_op jit(solution)/shard_map/all_gather | solution.py:43
  312.0 98.0 %reduce-scatter.5.cloned.1.call-start = ((), (), s32[]{:S(2)}) async-start(), calls=%async_computation.5 | async-start | bytes 1769472 | tf_op jit(solution)/shard_map/reduce_scatter | solution.py:51
  369.9 8.5 %copy-start.1 = (bf16[512,3072]{1,0:T(8,128)(2,1)S(1)}, bf16[512,3072]{1,0:T(8,128)(2,1)}, u32[]{:S(2)}) copy-start(bf16[512,3072]{1,0:T(8,128)(2,1)} %all-gather.2.cloned.1.call-done) | copy-start | bytes 9437188
Sparse Core Ops, SparseCore 0:
  45.4 172.0 all-reduce.1
  221.6 88.2 reduce-scatter.2
  313.3 49.4 all-gather.1
  370.0 39.9 reduce-scatter.4
where the time goes:
time: 419 us; the launch traced here: 418 us
  waiting for transfers between devices  297 us (71%)
  blocking collectives  62.1 us (15%)
  matrix products  33.5 us (8%)
  between operations  13.8 us (3%)
  local copies, waits for them, and re-layouts  7.45 us (2%)
    psum x1, waiting for transfers between devices, on_device(): lax.psum(jnp.dot(inputs_all, weight_in, preferred_element_type=jnp.float3...  133 us
    reduce_scatter x1, waiting for transfers between devices, on_device(): lax.psum_scatter(lax.dot_general(cotangent_all, weight_out, (((1,), (1,))...  92.5 us
    all_gather x1, waiting for transfers between devices, on_device(): grad_all = lax.all_gather(pre_grad, 'row', axis=0, tiled=True)  50.7 us
    all_gather x1, blocking collectives, on_device(): lax.all_gather(inputs, 'col', axis=0, tiled=True)  31.2 us
    all_gather x1, blocking collectives, on_device(): lax.all_gather(cotangent, 'col', axis=0, tiled=True)  30.9 us
    reduce_scatter x1, waiting for transfers between devices, on_device(): lax.psum_scatter(input_partial, 'col', scatter_dimension=0, tiled=True)  20.6 us
    dot_general x1, matrix products, on_device(): lax.dot_general(act_all, cotangent_all, (((0,), (0,)), ((), ())), preferr...  8.47 us
  transfers between devices with their start and end apart: 4, of which 4 were waited for; matrix products, arithmetic and copies ran while one was open for 6% of the time, Pallas kernels for 0%

commit v1 on v0

v1 whole, which is shorter than its diff:
```python
import math

import jax
import jax.numpy as jnp
from jax import lax
from jax.sharding import PartitionSpec as P

ROW = [(y, x, c) for y in range(4) for x in range(2) for c in range(2)]
COL = [(x, z) for x in range(2) for z in range(4)]


def at_row(y, x, c):
    return ((y % 4) * 2 + x % 2) * 2 + c % 2


def at_col(x, z):
    return (x % 2) * 4 + z % 4


def from_row(a, dy, dx, dc):
    return lax.ppermute(a, "row", [(at_row(y + dy, x + dx, c + dc), at_row(y, x, c)) for y, x, c in ROW])


def from_col(a, dx, dz):
    return lax.ppermute(a, "col", [(at_col(x + dx, z + dz), at_col(x, z)) for x, z in COL])


def gelu_value(v):
    inner = math.sqrt(2.0 / math.pi) * (v + 0.044715 * v * v * v)
    return 0.5 * v * (1.0 + jnp.tanh(inner))


def gelu_slope(v):
    coeff = math.sqrt(2.0 / math.pi)
    tanh_part = jnp.tanh(coeff * (v + 0.044715 * v * v * v))
    return 0.5 * (1.0 + tanh_part) + 0.5 * v * (1.0 - tanh_part * tanh_part) * coeff * (
        1.0 + 3.0 * 0.044715 * v * v
    )


def f32(a):
    return a.astype(jnp.float32)


def bf16(a):
    return a.astype(jnp.bfloat16)


def sum_y(part):
    sent = bf16(part)
    got = [from_row(sent[dy], -dy, 0, 0) for dy in (1, 3, 2)]
    return part[0] + f32(got[0]) + f32(got[1]) + f32(got[2])


def sum_x(part):
    return part[0] + f32(from_row(bf16(part[1]), 0, 1, 0))


def sum_core(part):
    return part[0] + f32(from_row(bf16(part[1]), 0, 0, 1))


def sum_row(part, y_first):
    n = part.shape[1]
    pair = sum_core(part.reshape(2, -1, n))
    if y_first:
        one = sum_y(pair.reshape(4, -1, n))
        return sum_x(one.reshape(2, -1, n))
    pair = pair.reshape(4, 2, -1, n)
    one = sum_x(jnp.stack([pair[:, 0], pair[:, 1]]))
    return sum_y(one)


def gather_row(own, y_first):
    t, n = own.shape
    if y_first:
        ys = jnp.stack([own] + [from_row(own, dy, 0, 0) for dy in (1, 2, 3)])
        both = jnp.stack([ys, from_row(ys, 0, 1, 0)], 1)
    else:
        xs = jnp.stack([own, from_row(own, 0, 1, 0)])
        both = jnp.stack([xs] + [from_row(xs, dy, 0, 0) for dy in (1, 2, 3)])
    half = both.reshape(8 * t, n)
    return jnp.concatenate([half, from_row(half, 0, 0, 1)])


def gather_col(own, direct):
    if direct:
        got = [from_col(own, dx, dz) if (dx or dz) else own for dz in range(4) for dx in range(2)]
        return jnp.concatenate(got)
    pair = jnp.concatenate([own, from_col(own, 1, 0)])
    return jnp.concatenate([pair] + [from_col(pair, 0, dz) for dz in (1, 2, 3)])


def on_device(inputs, cotangent, weight_in, weight_out):
    row = lax.axis_index("row")
    y, x, c = row // 4, (row // 2) % 2, row % 2
    rel = jnp.arange(512)
    dc, dy, dx, t = rel // 256, (rel // 64) % 4, (rel // 32) % 2, rel % 32
    order = ((((c + dc) % 2) * 4 + (y + dy) % 4) * 2 + (x + dx) % 2) * 32 + t
    to_rel = (order[:, None] == rel[None, :]).astype(jnp.bfloat16)

    def arranged(a):
        return jnp.dot(to_rel, a, preferred_element_type=jnp.float32).astype(jnp.bfloat16)

    inputs_all = arranged(gather_col(inputs, True))
    cotangent_all = arranged(gather_col(cotangent, False))
    pre = sum_row(jnp.dot(inputs_all, weight_in, preferred_element_type=jnp.float32), True)
    act = bf16(gelu_value(pre))
    act_grad = sum_row(
        lax.dot_general(
            cotangent_all, weight_out, (((1,), (1,)), ((), ())), preferred_element_type=jnp.float32
        ),
        False,
    )
    pre_grad = bf16(act_grad * gelu_slope(pre))
    act_all = gather_row(act, False)
    weight_out_grad = bf16(
        lax.dot_general(
            act_all, cotangent_all, (((0,), (0,)), ((), ())), preferred_element_type=jnp.float32
        )
    )
    grad_all = gather_row(pre_grad, True)
    input_partial = lax.dot_general(
        grad_all, weight_in, (((1,), (1,)), ((), ())), preferred_element_type=jnp.float32
    )
    weight_in_grad = bf16(
        lax.dot_general(
            inputs_all, grad_all, (((0,), (0,)), ((), ())), preferred_element_type=jnp.float32
        )
    )
    back = lax.dot_general(
        to_rel, bf16(input_partial), (((0,), (0,)), ((), ())), preferred_element_type=jnp.float32
    )
    blocks = back.reshape(4, 2, 64, -1)
    sent = bf16(blocks)
    total = blocks[0, 0]
    for dz in range(4):
        for dx in range(2):
            if dz or dx:
                total = total + f32(from_col(sent[dz, dx], dx, -dz))
    return (weight_in_grad, weight_out_grad, bf16(total))


def solution(mesh):
    return jax.shard_map(
        on_device,
        mesh=mesh,
        in_specs=(P("col", "row"), P("col", "row"), P("row", "col"), P("col", "row")),
        out_specs=(P("row", "col"), P("col", "row"), P("col", "row")),
        check_vma=False,
    )
```

time: 419 us -> 182 us (0.43)
  waiting for transfers between devices: 297 us -> 91.6 us
  blocking collectives: 62.1 us -> 0 us
  starting transfers between devices: 0.16 us -> 53.6 us
  between operations: 13.8 us -> 1.03 us
  matrix products: 33.5 us -> 27.9 us
  local copies, waits for them, and re-layouts: 7.45 us -> 2.48 us
    psum x1 -> x0, waiting for transfers between devices: 133 us -> none  [on_device(): lax.psum(jnp.dot(inputs_all, weight_in, preferred_element_type=jnp.float3...]
    reduce_scatter x2 -> x0, waiting for transfers between devices: 113 us -> none  [the longest x1 92.5 us: on_device(): lax.psum_scatter(lax.dot_general(cotangent_all, weight_out, (((1,), (1,))...]
    ppermute x0 -> x38, waiting for transfers between devices: none -> 91.6 us  [the longest x20 68 us: from_row(): lax.ppermute(a, 'row', [(at_row(y + dy, x + dx, c + dc), at_row(y, x, c))...]
    all_gather x2 -> x0, blocking collectives: 62.1 us -> none  [the longest x1 31.2 us: on_device(): lax.all_gather(inputs, 'col', axis=0, tiled=True)]
    ppermute x0 -> x38, starting transfers between devices: none -> 53.6 us  [the longest x20 27.5 us: from_row(): lax.ppermute(a, 'row', [(at_row(y + dy, x + dx, c + dc), at_row(y, x, c))...]
    all_gather x1 -> x0, waiting for transfers between devices: 50.7 us -> none  [on_device(): grad_all = lax.all_gather(pre_grad, 'row', axis=0, tiled=True)]
    unnamed x5 -> x24, local copies, waits for them, and re-layouts: 7.45 us -> 1.63 us
    dot_general x1, matrix products: 6.88 us -> 2.64 us  [on_device(): lax.dot_general(cotangent_all, weight_out, (((1,), (1,)), ((), ())), pref...]
  transfers between devices with their start and end apart: 4 -> 38, of which waited for: 4 -> 18; matrix products, arithmetic and copies ran while one was open for 6% -> 18% of each run, Pallas kernels for 0% -> 0%
where the time goes in v1:
time: 182 us; the launch traced here: 181 us
  waiting for transfers between devices  91.6 us (50%)
  starting transfers between devices  53.6 us (29%)
  matrix products  27.9 us (15%)
  other arithmetic  4.31 us (2%)
  local copies, waits for them, and re-layouts  2.48 us (1%)
    ppermute x20, waiting for transfers between devices, from_row(): lax.ppermute(a, 'row', [(at_row(y + dy, x + dx, c + dc), at_row(y, x, c))...  68 us
    ppermute x20, starting transfers between devices, from_row(): lax.ppermute(a, 'row', [(at_row(y + dy, x + dx, c + dc), at_row(y, x, c))...  27.5 us
    ppermute x18, starting transfers between devices, from_col(): lax.ppermute(a, 'col', [(at_col(x + dx, z + dz), at_col(x, z)) for x, z i...  26.1 us
    ppermute x18, waiting for transfers between devices, from_col(): lax.ppermute(a, 'col', [(at_col(x + dx, z + dz), at_col(x, z)) for x, z i...  23.6 us
    dot_general x1, matrix products, on_device(): lax.dot_general(act_all, cotangent_all, (((0,), (0,)), ((), ())), preferr...  6.74 us
    dot_general x1, matrix products, on_device(): lax.dot_general(to_rel, bf16(input_partial), (((0,), (0,)), ((), ())), pr...  6.45 us
    dot_general x1, matrix products, on_device(): lax.dot_general(inputs_all, grad_all, (((0,), (0,)), ((), ())), preferred...  5.7 us
    dot_general x1, matrix products, on_device(): jnp.dot(inputs_all, weight_in, preferred_element_type=jnp.float32)  5.09 us
  transfers between devices with their start and end apart: 38, of which 18 were waited for; matrix products, arithmetic and copies ran while one was open for 18% of the time, Pallas kernels for 0%

profile of v1, /device:TPU:0, one launch (start us, length us, event | category | flops | bytes accessed | tf_op | source)
XLA Modules:
  0.0 180.9 jit_solution(18295064383841166149)
XLA Ops:
  0.6 2.1 %collective-permute-start.5 = (bf16[64,768]{1,0:T(8,128)(2,1)}, bf16[64,768]{1,0:T(8,128)(2,1)S(1)}, u32[]{:S(2)}, u32[]{:S(2)}) collective-permute-start(bf16[64,768]{1,0:T(8,128)(2,1)} %param.4), channel_id=1, source_target_pairs={{3,0},{0,1},{1,2},{2,3},{7,4},{4,5},{5,6},{6,7},{11,8},{8,9},{9,10... | collective-permute-start | bytes 294920 | tf_op jit(solution)/shard_map/ppermute | solution.py:25
  2.7 4.5 %collective-permute-start.4 = (bf16[64,768]{1,0:T(8,128)(2,1)}, bf16[64,768]{1,0:T(8,128)(2,1)S(1)}, u32[]{:S(2)}, u32[]{:S(2)}) collective-permute-start(bf16[64,768]{1,0:T(8,128)(2,1)} %param.4), channel_id=1, source_target_pairs={{6,0},{7,1},{4,2},{5,3},{2,4},{3,5},{0,6},{1,7},{14,8},{15,9},{12,... | collective-permute-start | bytes 294920 | tf_op jit(solution)/shard_map/ppermute | solution.py:25
  7.2 2.1 %collective-permute-start.2 = (bf16[64,768]{1,0:T(8,128)(2,1)}, bf16[64,768]{1,0:T(8,128)(2,1)S(1)}, u32[]{:S(2)}, u32[]{:S(2)}) collective-permute-start(bf16[64,768]{1,0:T(8,128)(2,1)} %param.4), channel_id=1, source_target_pairs={{5,0},{6,1},{7,2},{4,3},{1,4},{2,5},{3,6},{0,7},{13,8},{14,9},{15,... | collective-permute-start | bytes 294920 | tf_op jit(solution)/shard_map/ppermute | solution.py:25
  9.3 1.5 collective-permute-start
  10.8 0.9 constant_dynamic-update-slice_fusion.7
  11.8 3.3 %collective-permute-done = bf16[64,768]{1,0:T(8,128)(2,1)S(1)} collective-permute-done((bf16[64,768]{1,0:T(8,128)(2,1)}, bf16[64,768]{1,0:T(8,128)(2,1)S(1)}, u32[]{:S(2)}, u32[]{:S(2)}) %collective-permute-start) | collective-permute-done | bytes 98336 | tf_op jit(solution)/shard_map/ppermute | solution.py:25
  15.1 1.7 collective-permute-start.1
  16.8 3.1 %collective-permute-done.1 = bf16[64,768]{1,0:T(8,128)(2,1)S(1)} collective-permute-done((bf16[64,768]{1,0:T(8,128)(2,1)}, bf16[64,768]{1,0:T(8,128)(2,1)S(1)}, u32[]{:S(2)}, u32[]{:S(2)}) %collective-permute-start.1) | collective-permute-done | bytes 98336 | tf_op jit(solution)/shard_map/ppermute | solution.py:25
  20.3 1.1 collective-permute-start.7
  21.5 5.4 %collective-permute-done.6 = bf16[64,768]{1,0:T(8,128)(2,1)S(1)} collective-permute-done((bf16[64,768]{1,0:T(8,128)(2,1)}, bf16[64,768]{1,0:T(8,128)(2,1)S(1)}, u32[]{:S(2)}, u32[]{:S(2)}) %collective-permute-start.6) | collective-permute-done | bytes 98336 | tf_op jit(solution)/shard_map/ppermute | solution.py:25
  27.6 5.1 %fusion.64 = f32[512,3072]{1,0:T(8,128)S(1)} fusion(bf16[512,768]{1,0:T(8,128)(2,1)S(1)} %convolution_convert_fusion.3, bf16[768,3072]{1,0:T(8,128)(2,1)} %param.6), kind=kOutput, calls=%fused_computation.137 | convolution fusion | flops 2415919104 | bytes 11796480 | tf_op jit(solution)/shard_map/dot_general | solution.py:107
  33.6 1.7 collective-permute-start.8
  35.4 0.9 collective-permute-start.10
  36.3 5.2 %collective-permute-done.8 = bf16[128,768]{1,0:T(8,128)(2,1)S(1)} collective-permute-done((bf16[128,768]{1,0:T(8,128)(2,1)S(1)}, bf16[128,768]{1,0:T(8,128)(2,1)S(1)}, u32[]{:S(2)}, u32[]{:S(2)}) %collective-permute-start.8) | collective-permute-done | bytes 196640 | tf_op jit(solution)/shard_map/ppermute | solution.py:25
  41.5 3.2 %collective-permute-done.9 = bf16[128,768]{1,0:T(8,128)(2,1)S(1)} collective-permute-done((bf16[128,768]{1,0:T(8,128)(2,1)S(1)}, bf16[128,768]{1,0:T(8,128)(2,1)S(1)}, u32[]{:S(2)}, u32[]{:S(2)}) %collective-permute-start.9) | collective-permute-done | bytes 196640 | tf_op jit(solution)/shard_map/ppermute | solution.py:25
  44.7 2.5 %collective-permute-done.10 = bf16[128,768]{1,0:T(8,128)(2,1)S(1)} collective-permute-done((bf16[128,768]{1,0:T(8,128)(2,1)S(1)}, bf16[128,768]{1,0:T(8,128)(2,1)S(1)}, u32[]{:S(2)}, u32[]{:S(2)}) %collective-permute-start.10) | collective-permute-done | bytes 196640 | tf_op jit(solution)/shard_map/ppermute | solution.py:25
  47.9 2.6 %fusion.63 = f32[512,3072]{1,0:T(8,128)S(1)} fusion(bf16[512,768]{1,0:T(8,128)(2,1)S(1)} %convolution_convert_fusion.2, bf16[3072,768]{1,0:T(8,128)(2,1)S(1)} %bitcast.100), kind=kOutput, calls=%fused_computation.136 | convolution fusion | flops 2415919104 | bytes 11796480 | tf_op jit(solution)/shard_map/dot_general | solution.py:110
  51.6 1.6 collective-permute-start.17
  53.3 2.9 %collective-permute-start.19 = (bf16[64,3072]{1,0:T(8,128)(2,1)S(1)}, bf16[64,3072]{1,0:T(8,128)(2,1)S(1)}, u32[]{:S(2)}, u32[]{:S(2)}) collective-permute-start(bf16[64,3072]{1,0:T(8,128)(2,1)S(1)} %get-tuple-element.8), channel_id=1, source_target_pairs={{64,0},{72,8},{80,16},{88,24},{96,32},{104,40},{112,48},{120,56},{... | collective-permute-start | bytes 1179656 | tf_op jit(solution)/shard_map/ppermute | solution.py:21
  56.2 1.3 collective-permute-start.18
  58.0 2.8 %collective-permute-start.12 = (bf16[4,32,3072]{2,1,0:T(8,128)(2,1)S(1)}, bf16[4,32,3072]{2,1,0:T(8,128)(2,1)S(1)}, u32[]{:S(2)}, u32[]{:S(2)}) collective-permute-start(bf16[4,32,3072]{2,1,0:T(8,128)(2,1)S(1)} %fusion.7), channel_id=1, source_target_pairs={{16,0},{24,8},{0,16},{8,24},{48,32},{56,40},{32,48},{40,56},{80,64... | collective-permute-start | bytes 2359304 | tf_op jit(solution)/shard_map/ppermute | solution.py:21
  60.8 3.6 %collective-permute-done.17 = bf16[64,3072]{1,0:T(8,128)(2,1)S(1)} collective-permute-done((bf16[64,3072]{1,0:T(8,128)(2,1)S(1)}, bf16[64,3072]{1,0:T(8,128)(2,1)S(1)}, u32[]{:S(2)}, u32[]{:S(2)}) %collective-permute-start.17) | collective-permute-done | bytes 393248 | tf_op jit(solution)/shard_map/ppermute | solution.py:21
  64.5 9.6 %collective-permute-done.19 = bf16[64,3072]{1,0:T(8,128)(2,1)S(1)} collective-permute-done((bf16[64,3072]{1,0:T(8,128)(2,1)S(1)}, bf16[64,3072]{1,0:T(8,128)(2,1)S(1)}, u32[]{:S(2)}, u32[]{:S(2)}) %collective-permute-start.19) | collective-permute-done | bytes 393248 | tf_op jit(solution)/shard_map/ppermute | solution.py:21
  74.3 2.8 %collective-permute-start.20 = (bf16[32,3072]{1,0:T(8,128)(2,1)S(1)}, bf16[32,3072]{1,0:T(8,128)(2,1)S(1)}, u32[]{:S(2)}, u32[]{:S(2)}) collective-permute-start(bf16[32,3072]{1,0:T(8,128)(2,1)S(1)} %slice.187), channel_id=1, source_target_pairs={{16,0},{24,8},{0,16},{8,24},{48,32},{56,40},{32,48},{40,56},{80,64... | collective-permute-start | bytes 589832 | tf_op jit(solution)/shard_map/ppermute | solution.py:21
  77.1 2.0 %collective-permute-done.12 = bf16[4,32,3072]{2,1,0:T(8,128)(2,1)S(1)} collective-permute-done((bf16[4,32,3072]{2,1,0:T(8,128)(2,1)S(1)}, bf16[4,32,3072]{2,1,0:T(8,128)(2,1)S(1)}, u32[]{:S(2)}, u32[]{:S(2)}) %collective-permute-start.12) | collective-permute-done | bytes 786464 | tf_op jit(solution)/shard_map/ppermute | solution.py:21
  80.2 1.1 collective-permute-start.15
  81.3 1.6 collective-permute-start.14
  83.0 7.8 %collective-permute-done.13 = bf16[32,3072]{1,0:T(8,128)(2,1)S(1)} collective-permute-done((bf16[32,3072]{1,0:T(8,128)(2,1)S(1)}, bf16[32,3072]{1,0:T(8,128)(2,1)S(1)}, u32[]{:S(2)}, u32[]{:S(2)}) %collective-permute-start.13) | collective-permute-done | bytes 196640 | tf_op jit(solution)/shard_map/ppermute | solution.py:21
  91.2 0.8 collective-permute-start.23
  92.0 3.4 %collective-permute-start.22 = (bf16[32,3072]{1,0:T(8,128)(2,1)S(1)}, bf16[32,3072]{1,0:T(8,128)(2,1)S(1)}, u32[]{:S(2)}, u32[]{:S(2)}) collective-permute-start(bf16[32,3072]{1,0:T(8,128)(2,1)S(1)} %get-tuple-element.11), channel_id=1, source_target_pairs={{64,0},{72,8},{80,16},{88,24},{96,32},{104,40},{112,48},{120,56},{... | collective-permute-start | bytes 589832 | tf_op jit(solution)/shard_map/ppermute | solution.py:21
  95.4 3.5 %collective-permute-done.23 = bf16[32,3072]{1,0:T(8,128)(2,1)S(1)} collective-permute-done((bf16[32,3072]{1,0:T(8,128)(2,1)S(1)}, bf16[32,3072]{1,0:T(8,128)(2,1)S(1)}, u32[]{:S(2)}, u32[]{:S(2)}) %collective-permute-start.23) | collective-permute-done | bytes 196640 | tf_op jit(solution)/shard_map/ppermute | solution.py:21
  98.8 5.0 %collective-permute-done.22 = bf16[32,3072]{1,0:T(8,128)(2,1)S(1)} collective-permute-done((bf16[32,3072]{1,0:T(8,128)(2,1)S(1)}, bf16[32,3072]{1,0:T(8,128)(2,1)S(1)}, u32[]{:S(2)}, u32[]{:S(2)}) %collective-permute-start.22) | collective-permute-done | bytes 196640 | tf_op jit(solution)/shard_map/ppermute | solution.py:21
  104.0 2.7 %collective-permute-start.24 = (bf16[4,32,3072]{2,1,0:T(8,128)(2,1)S(1)}, bf16[4,32,3072]{2,1,0:T(8,128)(2,1)S(1)}, u32[]{:S(2)}, u32[]{:S(2)}) collective-permute-start(bf16[4,32,3072]{2,1,0:T(8,128)(2,1)S(1)} %get-tuple-element.20), channel_id=1, source_target_pairs={{16,0},{24,8},{0,16},{8,24},{48,32},{56,40},{32,48},{40,56},{80,64... | collective-permute-start | bytes 2359304 | tf_op jit(solution)/shard_map/ppermute | solution.py:21
  106.7 0.9 collective-permute-start.26
  107.6 18.1 %collective-permute-done.24 = bf16[4,32,3072]{2,1,0:T(8,128)(2,1)S(1)} collective-permute-done((bf16[4,32,3072]{2,1,0:T(8,128)(2,1)S(1)}, bf16[4,32,3072]{2,1,0:T(8,128)(2,1)S(1)}, u32[]{:S(2)}, u32[]{:S(2)}) %collective-permute-start.24) | collective-permute-done | bytes 786464 | tf_op jit(solution)/shard_map/ppermute | solution.py:21
  126.0 1.8 collective-permute-done.26
  128.0 3.6 %collective-permute-start.27 = (bf16[2,32,3072]{2,1,0:T(8,128)(2,1)S(1)}, bf16[2,32,3072]{2,1,0:T(8,128)(2,1)S(1)}, u32[]{:S(2)}, u32[]{:S(2)}) collective-permute-start(bf16[2,32,3072]{2,1,0:T(8,128)(2,1)S(1)} %get-tuple-element.25), channel_id=1, source_target_pairs={{32,0},{40,8},{48,16},{56,24},{64,32},{72,40},{80,48},{88,56},{96,... | collective-permute-start | bytes 1179656 | tf_op jit(solution)/shard_map/ppermute | solution.py:21
  132.3 9.2 %collective-permute-done.28 = bf16[2,32,3072]{2,1,0:T(8,128)(2,1)S(1)} collective-permute-done((bf16[2,32,3072]{2,1,0:T(8,128)(2,1)S(1)}, bf16[2,32,3072]{2,1,0:T(8,128)(2,1)S(1)}, u32[]{:S(2)}, u32[]{:S(2)}) %collective-permute-start.28) | collective-permute-done | bytes 393248 | tf_op jit(solution)/shard_map/ppermute | solution.py:21
  141.5 7.3 %collective-permute-done.27 = bf16[2,32,3072]{2,1,0:T(8,128)(2,1)S(1)} collective-permute-done((bf16[2,32,3072]{2,1,0:T(8,128)(2,1)S(1)}, bf16[2,32,3072]{2,1,0:T(8,128)(2,1)S(1)}, u32[]{:S(2)}, u32[]{:S(2)}) %collective-permute-start.27) | collective-permute-done | bytes 393248 | tf_op jit(solution)/shard_map/ppermute | solution.py:21
  148.8 1.3 pad_maximum_fusion.4
  150.2 6.4 %fusion.6 = f32[512,768]{1,0:T(8,128)S(1)} fusion(bf16[768,3072]{1,0:T(8,128)(2,1)} %param.6, bf16[256,3072]{1,0:T(8,128)(2,1)} %collective-permute-done.25, bf16[256,3072]{1,0:T(8,128)(2,1)S(1)} %bitcast.87, s32[512]{0:T(512)S(1)} %fusion.40), kind=kOutput, calls=%fused_computation.19 | convolution fusion | flops 2825519104 | bytes 9439232 | tf_op jit(solution)/shard_map/dot_general | solution.py:131
  157.3 1.9 %collective-permute-start.37 = (bf16[64,768]{1,0:T(8,128)(2,1)S(1)}, bf16[64,768]{1,0:T(8,128)(2,1)S(1)}, u32[]{:S(2)}, u32[]{:S(2)}) collective-permute-start(bf16[64,768]{1,0:T(8,128)(2,1)S(1)} %get-tuple-element.13), channel_id=1, source_target_pairs={{5,0},{6,1},{7,2},{4,3},{1,4},{2,5},{3,6},{0,7},{13,8},{14,9},{15,... | collective-permute-start | bytes 294920 | tf_op jit(solution)/shard_map/ppermute | solution.py:25
  159.2 6.7 %convolution_convert_fusion = bf16[3072,768]{1,0:T(8,128)(2,1)} fusion(bf16[512,768]{1,0:T(8,128)(2,1)S(1)} %copy-done.4, bf16[256,3072]{1,0:T(8,128)(2,1)} %collective-permute-done.30, bf16[256,3072]{1,0:T(8,128)(2,1)} %bitcast.20), kind=kOutput, calls=%fused_computation | convolution fusion | flops 2424569856 | bytes 8650752 | tf_op jit(solution)/shard_map/dot_general | solution.py:118
  166.2 2.9 %collective-permute-start.35 = (bf16[64,768]{1,0:T(8,128)(2,1)S(1)}, bf16[64,768]{1,0:T(8,128)(2,1)S(1)}, u32[]{:S(2)}, u32[]{:S(2)}) collective-permute-start(bf16[64,768]{1,0:T(8,128)(2,1)S(1)} %get-tuple-element.15), channel_id=1, source_target_pairs={{6,0},{7,1},{4,2},{5,3},{2,4},{3,5},{0,6},{1,7},{14,8},{15,9},{12,... | collective-permute-start | bytes 294920 | tf_op jit(solution)/shard_map/ppermute | solution.py:25
  169.6 2.8 %collective-permute-start.33 = (bf16[64,768]{1,0:T(8,128)(2,1)S(1)}, bf16[64,768]{1,0:T(8,128)(2,1)S(1)}, u32[]{:S(2)}, u32[]{:S(2)}) collective-permute-start(bf16[64,768]{1,0:T(8,128)(2,1)S(1)} %get-tuple-element.17), channel_id=1, source_target_pairs={{7,0},{4,1},{5,2},{6,3},{3,4},{0,5},{1,6},{2,7},{15,8},{12,9},{13,... | collective-permute-start | bytes 294920 | tf_op jit(solution)/shard_map/ppermute | solution.py:25
  172.4 1.1 collective-permute-start.32
  173.6 5.7 %convolution_convert_fusion.1 = bf16[768,3072]{1,0:T(8,128)(2,1)} fusion(bf16[512,768]{1,0:T(8,128)(2,1)S(1)} %copy-done.1, bf16[256,3072]{1,0:T(8,128)(2,1)} %collective-permute-done.25, bf16[256,3072]{1,0:T(8,128)(2,1)S(1)} %bitcast.88), kind=kOutput, calls=%fused_computation.1 | convolution fusion | flops 2424569856 | bytes 8650752 | tf_op jit(solution)/shard_map/dot_general | solution.py:127
  179.3 0.8 collective-permute-done.32
  (83 shorter events, 9.4 us)
Async XLA Ops:
  0.6 20.8 %collective-permute-start.5 = (bf16[64,768]{1,0:T(8,128)(2,1)}, bf16[64,768]{1,0:T(8,128)(2,1)S(1)}, u32[]{:S(2)}, u32[]{:S(2)}) collective-permute-start(bf16[64,768]{1,0:T(8,128)(2,1)} %param.4), channel_id=1, source_target_pairs={{3,0},{0,1},{1,2},{2,3},{7,4},{4,5},{5,6},{6,7},{11,8},{8,9},{9,10... | collective-permute-start | bytes 294920 | tf_op jit(solution)/shard_map/ppermute | solution.py:25
  2.7 18.7 %collective-permute-start.4 = (bf16[64,768]{1,0:T(8,128)(2,1)}, bf16[64,768]{1,0:T(8,128)(2,1)S(1)}, u32[]{:S(2)}, u32[]{:S(2)}) collective-permute-start(bf16[64,768]{1,0:T(8,128)(2,1)} %param.4), channel_id=1, source_target_pairs={{6,0},{7,1},{4,2},{5,3},{2,4},{3,5},{0,6},{1,7},{14,8},{15,9},{12,... | collective-permute-start | bytes 294920 | tf_op jit(solution)/shard_map/ppermute | solution.py:25
  7.2 14.2 %collective-permute-start.3 = (bf16[64,768]{1,0:T(8,128)(2,1)}, bf16[64,768]{1,0:T(8,128)(2,1)S(1)}, u32[]{:S(2)}, u32[]{:S(2)}) collective-permute-start(bf16[64,768]{1,0:T(8,128)(2,1)} %param.4), channel_id=1, source_target_pairs={{2,0},{3,1},{0,2},{1,3},{6,4},{7,5},{4,6},{5,7},{10,8},{11,9},{8,1... | collective-permute-start | bytes 294920 | tf_op jit(solution)/shard_map/ppermute | solution.py:25
  7.2 13.0 %collective-permute-start.2 = (bf16[64,768]{1,0:T(8,128)(2,1)}, bf16[64,768]{1,0:T(8,128)(2,1)S(1)}, u32[]{:S(2)}, u32[]{:S(2)}) collective-permute-start(bf16[64,768]{1,0:T(8,128)(2,1)} %param.4), channel_id=1, source_target_pairs={{5,0},{6,1},{7,2},{4,3},{1,4},{2,5},{3,6},{0,7},{13,8},{14,9},{15,... | collective-permute-start | bytes 294920 | tf_op jit(solution)/shard_map/ppermute | solution.py:25
  9.3 5.8 %collective-permute-start = (bf16[64,768]{1,0:T(8,128)(2,1)}, bf16[64,768]{1,0:T(8,128)(2,1)S(1)}, u32[]{:S(2)}, u32[]{:S(2)}) collective-permute-start(bf16[64,768]{1,0:T(8,128)(2,1)} %param.4), channel_id=1, source_target_pairs={{4,0},{5,1},{6,2},{7,3},{0,4},{1,5},{2,6},{3,7},{12,8},{13,9},{14,... | collective-permute-start | bytes 294920 | tf_op jit(solution)/shard_map/ppermute | solution.py:25
  15.1 4.8 %collective-permute-start.1 = (bf16[64,768]{1,0:T(8,128)(2,1)}, bf16[64,768]{1,0:T(8,128)(2,1)S(1)}, u32[]{:S(2)}, u32[]{:S(2)}) collective-permute-start(bf16[64,768]{1,0:T(8,128)(2,1)} %param.4), channel_id=1, source_target_pairs={{1,0},{2,1},{3,2},{0,3},{5,4},{6,5},{7,6},{4,7},{9,8},{10,9},{11,1... | collective-permute-start | bytes 294920 | tf_op jit(solution)/shard_map/ppermute | solution.py:25
  19.9 6.9 %collective-permute-start.6 = (bf16[64,768]{1,0:T(8,128)(2,1)}, bf16[64,768]{1,0:T(8,128)(2,1)S(1)}, u32[]{:S(2)}, u32[]{:S(2)}) collective-permute-start(bf16[64,768]{1,0:T(8,128)(2,1)} %param.4), channel_id=1, source_target_pairs={{7,0},{4,1},{5,2},{6,3},{3,4},{0,5},{1,6},{2,7},{15,8},{12,9},{13,... | collective-permute-start | bytes 294920 | tf_op jit(solution)/shard_map/ppermute | solution.py:25
  20.3 13.3 %collective-permute-start.7 = (bf16[64,768]{1,0:T(8,128)(2,1)}, bf16[64,768]{1,0:T(8,128)(2,1)S(1)}, u32[]{:S(2)}, u32[]{:S(2)}) collective-permute-start(bf16[64,768]{1,0:T(8,128)(2,1)} %param.5), channel_id=1, source_target_pairs={{4,0},{5,1},{6,2},{7,3},{0,4},{1,5},{2,6},{3,7},{12,8},{13,9},{14,... | collective-permute-start | bytes 294920 | tf_op jit(solution)/shard_map/ppermute | solution.py:25
  26.9 21.0 %slice-start = ((s8[4718592]{0:T(1024)(128)(4,1)}), s8[4194304]{0:T(1024)(128)(4,1)S(1)}, s32[]{:S(2)}) async-start(s8[4718592]{0:T(1024)(128)(4,1)} %bitcast.99), calls=%async_computation | async-start | bytes 8388608
  27.5 5.1 %copy-start = (bf16[512,768]{1,0:T(8,128)(2,1)}, bf16[512,768]{1,0:T(8,128)(2,1)S(1)}, u32[]{:S(2)}) copy-start(bf16[512,768]{1,0:T(8,128)(2,1)S(1)} %convolution_convert_fusion.3) | copy-start | bytes 2359300
  27.5 20.4 %slice-start.1 = ((s8[4718592]{0:T(1024)(128)(4,1)}), s8[524288]{0:T(1024)(128)(4,1)S(1)}, s32[]{:S(2)}) async-start(s8[4718592]{0:T(1024)(128)(4,1)} %bitcast.99), calls=%async_computation.1 | async-start | bytes 1048576
  32.7 0.9 copy-start.2
  32.9 18.0 %collective-permute-start.16 = (bf16[256,3072]{1,0:T(8,128)(2,1)S(1)}, bf16[256,3072]{1,0:T(8,128)(2,1)S(1)}, u32[]{:S(2)}, u32[]{:S(2)}) collective-permute-start(bf16[256,3072]{1,0:T(8,128)(2,1)S(1)} %slice.185), channel_id=1, source_target_pairs={{8,0},{0,8},{24,16},{16,24},{40,32},{32,40},{56,48},{48,56},{72,64... | collective-permute-start | bytes 4718600 | tf_op jit(solution)/shard_map/ppermute | solution.py:21
  33.6 7.8 %collective-permute-start.8 = (bf16[128,768]{1,0:T(8,128)(2,1)S(1)}, bf16[128,768]{1,0:T(8,128)(2,1)S(1)}, u32[]{:S(2)}, u32[]{:S(2)}) collective-permute-start(bf16[128,768]{1,0:T(8,128)(2,1)S(1)} %get-tuple-element.26), channel_id=1, source_target_pairs={{1,0},{2,1},{3,2},{0,3},{5,4},{6,5},{7,6},{4,7},{9,8},{10,9},{11,1... | collective-permute-start | bytes 589832 | tf_op jit(solution)/shard_map/ppermute | solution.py:25
  35.4 9.3 %collective-permute-start.9 = (bf16[128,768]{1,0:T(8,128)(2,1)S(1)}, bf16[128,768]{1,0:T(8,128)(2,1)S(1)}, u32[]{:S(2)}, u32[]{:S(2)}) collective-permute-start(bf16[128,768]{1,0:T(8,128)(2,1)S(1)} %get-tuple-element.26), channel_id=1, source_target_pairs={{2,0},{3,1},{0,2},{1,3},{6,4},{7,5},{4,6},{5,7},{10,8},{11,9},{8,1... | collective-permute-start | bytes 589832 | tf_op jit(solution)/shard_map/ppermute | solution.py:25
  35.4 11.9 %collective-permute-start.10 = (bf16[128,768]{1,0:T(8,128)(2,1)S(1)}, bf16[128,768]{1,0:T(8,128)(2,1)S(1)}, u32[]{:S(2)}, u32[]{:S(2)}) collective-permute-start(bf16[128,768]{1,0:T(8,128)(2,1)S(1)} %get-tuple-element.26), channel_id=1, source_target_pairs={{3,0},{0,1},{1,2},{2,3},{7,4},{4,5},{5,6},{6,7},{11,8},{8,9},{9,10... | collective-permute-start | bytes 589832 | tf_op jit(solution)/shard_map/ppermute | solution.py:25
  47.9 2.7 %copy-start.3 = (bf16[512,768]{1,0:T(8,128)(2,1)}, bf16[512,768]{1,0:T(8,128)(2,1)S(1)}, u32[]{:S(2)}) copy-start(bf16[512,768]{1,0:T(8,128)(2,1)S(1)} %convolution_convert_fusion.2) | copy-start | bytes 2359300
  50.8 6.7 %collective-permute-start.11 = (bf16[256,3072]{1,0:T(8,128)(2,1)S(1)}, bf16[256,3072]{1,0:T(8,128)(2,1)S(1)}, u32[]{:S(2)}, u32[]{:S(2)}) collective-permute-start(bf16[256,3072]{1,0:T(8,128)(2,1)S(1)} %slice.186), channel_id=1, source_target_pairs={{8,0},{0,8},{24,16},{16,24},{40,32},{32,40},{56,48},{48,56},{72,64... | collective-permute-start | bytes 4718600 | tf_op jit(solution)/shard_map/ppermute | solution.py:21
  51.6 12.8 %collective-permute-start.17 = (bf16[64,3072]{1,0:T(8,128)(2,1)S(1)}, bf16[64,3072]{1,0:T(8,128)(2,1)S(1)}, u32[]{:S(2)}, u32[]{:S(2)}) collective-permute-start(bf16[64,3072]{1,0:T(8,128)(2,1)S(1)} %get-tuple-element.7), channel_id=1, source_target_pairs={{96,0},{104,8},{112,16},{120,24},{0,32},{8,40},{16,48},{24,56},{32... | collective-permute-start | bytes 1179656 | tf_op jit(solution)/shard_map/ppermute | solution.py:21
  53.3 20.8 %collective-permute-start.19 = (bf16[64,3072]{1,0:T(8,128)(2,1)S(1)}, bf16[64,3072]{1,0:T(8,128)(2,1)S(1)}, u32[]{:S(2)}, u32[]{:S(2)}) collective-permute-start(bf16[64,3072]{1,0:T(8,128)(2,1)S(1)} %get-tuple-element.8), channel_id=1, source_target_pairs={{64,0},{72,8},{80,16},{88,24},{96,32},{104,40},{112,48},{120,56},{... | collective-permute-start | bytes 1179656 | tf_op jit(solution)/shard_map/ppermute | solution.py:21
  56.2 17.9 %collective-permute-start.18 = (bf16[64,3072]{1,0:T(8,128)(2,1)S(1)}, bf16[64,3072]{1,0:T(8,128)(2,1)S(1)}, u32[]{:S(2)}, u32[]{:S(2)}) collective-permute-start(bf16[64,3072]{1,0:T(8,128)(2,1)S(1)} %get-tuple-element.9), channel_id=1, source_target_pairs={{32,0},{40,8},{48,16},{56,24},{64,32},{72,40},{80,48},{88,56},{96,... | collective-permute-start | bytes 1179656 | tf_op jit(solution)/shard_map/ppermute | solution.py:21
  58.0 21.1 %collective-permute-start.12 = (bf16[4,32,3072]{2,1,0:T(8,128)(2,1)S(1)}, bf16[4,32,3072]{2,1,0:T(8,128)(2,1)S(1)}, u32[]{:S(2)}, u32[]{:S(2)}) collective-permute-start(bf16[4,32,3072]{2,1,0:T(8,128)(2,1)S(1)} %fusion.7), channel_id=1, source_target_pairs={{16,0},{24,8},{0,16},{8,24},{48,32},{56,40},{32,48},{40,56},{80,64... | collective-permute-start | bytes 2359304 | tf_op jit(solution)/shard_map/ppermute | solution.py:21
  74.3 8.7 %collective-permute-start.20 = (bf16[32,3072]{1,0:T(8,128)(2,1)S(1)}, bf16[32,3072]{1,0:T(8,128)(2,1)S(1)}, u32[]{:S(2)}, u32[]{:S(2)}) collective-permute-start(bf16[32,3072]{1,0:T(8,128)(2,1)S(1)} %slice.187), channel_id=1, source_target_pairs={{16,0},{24,8},{0,16},{8,24},{48,32},{56,40},{32,48},{40,56},{80,64... | collective-permute-start | bytes 589832 | tf_op jit(solution)/shard_map/ppermute | solution.py:21
  79.4 11.3 %collective-permute-start.13 = (bf16[32,3072]{1,0:T(8,128)(2,1)S(1)}, bf16[32,3072]{1,0:T(8,128)(2,1)S(1)}, u32[]{:S(2)}, u32[]{:S(2)}) collective-permute-start(bf16[32,3072]{1,0:T(8,128)(2,1)S(1)} %get-tuple-element.21), channel_id=1, source_target_pairs={{96,0},{104,8},{112,16},{120,24},{0,32},{8,40},{16,48},{24,56},{32... | collective-permute-start | bytes 589832 | tf_op jit(solution)/shard_map/ppermute | solution.py:21
  80.2 10.6 %collective-permute-start.15 = (bf16[32,3072]{1,0:T(8,128)(2,1)S(1)}, bf16[32,3072]{1,0:T(8,128)(2,1)S(1)}, u32[]{:S(2)}, u32[]{:S(2)}) collective-permute-start(bf16[32,3072]{1,0:T(8,128)(2,1)S(1)} %get-tuple-element.22), channel_id=1, source_target_pairs={{64,0},{72,8},{80,16},{88,24},{96,32},{104,40},{112,48},{120,56},{... | collective-permute-start | bytes 589832 | tf_op jit(solution)/shard_map/ppermute | solution.py:21
  81.3 9.5 %collective-permute-start.14 = (bf16[32,3072]{1,0:T(8,128)(2,1)S(1)}, bf16[32,3072]{1,0:T(8,128)(2,1)S(1)}, u32[]{:S(2)}, u32[]{:S(2)}) collective-permute-start(bf16[32,3072]{1,0:T(8,128)(2,1)S(1)} %get-tuple-element.23), channel_id=1, source_target_pairs={{32,0},{40,8},{48,16},{56,24},{64,32},{72,40},{80,48},{88,56},{96,... | collective-permute-start | bytes 589832 | tf_op jit(solution)/shard_map/ppermute | solution.py:21
  91.2 7.6 %collective-permute-start.23 = (bf16[32,3072]{1,0:T(8,128)(2,1)S(1)}, bf16[32,3072]{1,0:T(8,128)(2,1)S(1)}, u32[]{:S(2)}, u32[]{:S(2)}) collective-permute-start(bf16[32,3072]{1,0:T(8,128)(2,1)S(1)} %get-tuple-element.11), channel_id=1, source_target_pairs={{96,0},{104,8},{112,16},{120,24},{0,32},{8,40},{16,48},{24,56},{32... | collective-permute-start | bytes 589832 | tf_op jit(solution)/shard_map/ppermute | solution.py:21
  92.0 11.8 %collective-permute-start.22 = (bf16[32,3072]{1,0:T(8,128)(2,1)S(1)}, bf16[32,3072]{1,0:T(8,128)(2,1)S(1)}, u32[]{:S(2)}, u32[]{:S(2)}) collective-permute-start(bf16[32,3072]{1,0:T(8,128)(2,1)S(1)} %get-tuple-element.11), channel_id=1, source_target_pairs={{64,0},{72,8},{80,16},{88,24},{96,32},{104,40},{112,48},{120,56},{... | collective-permute-start | bytes 589832 | tf_op jit(solution)/shard_map/ppermute | solution.py:21
  95.4 8.5 %collective-permute-start.21 = (bf16[32,3072]{1,0:T(8,128)(2,1)S(1)}, bf16[32,3072]{1,0:T(8,128)(2,1)S(1)}, u32[]{:S(2)}, u32[]{:S(2)}) collective-permute-start(bf16[32,3072]{1,0:T(8,128)(2,1)S(1)} %get-tuple-element.11), channel_id=1, source_target_pairs={{32,0},{40,8},{48,16},{56,24},{64,32},{72,40},{80,48},{88,56},{96,... | collective-permute-start | bytes 589832 | tf_op jit(solution)/shard_map/ppermute | solution.py:21
  104.0 21.7 %collective-permute-start.24 = (bf16[4,32,3072]{2,1,0:T(8,128)(2,1)S(1)}, bf16[4,32,3072]{2,1,0:T(8,128)(2,1)S(1)}, u32[]{:S(2)}, u32[]{:S(2)}) collective-permute-start(bf16[4,32,3072]{2,1,0:T(8,128)(2,1)S(1)} %get-tuple-element.20), channel_id=1, source_target_pairs={{16,0},{24,8},{0,16},{8,24},{48,32},{56,40},{32,48},{40,56},{80,64... | collective-permute-start | bytes 2359304 | tf_op jit(solution)/shard_map/ppermute | solution.py:21
  106.7 21.1 %collective-permute-start.26 = (bf16[32,3072]{1,0:T(8,128)(2,1)S(1)}, bf16[32,3072]{1,0:T(8,128)(2,1)S(1)}, u32[]{:S(2)}, u32[]{:S(2)}) collective-permute-start(bf16[32,3072]{1,0:T(8,128)(2,1)S(1)} %get-tuple-element.10), channel_id=1, source_target_pairs={{16,0},{24,8},{0,16},{8,24},{48,32},{56,40},{32,48},{40,56},{80,64... | collective-permute-start | bytes 589832 | tf_op jit(solution)/shard_map/ppermute | solution.py:21
  126.0 24.2 %collective-permute-start.25 = (bf16[256,3072]{1,0:T(8,128)(2,1)S(1)}, bf16[256,3072]{1,0:T(8,128)(2,1)}, u32[]{:S(2)}, u32[]{:S(2)}) collective-permute-start(bf16[256,3072]{1,0:T(8,128)(2,1)S(1)} %bitcast.86), channel_id=1, source_target_pairs={{8,0},{0,8},{24,16},{16,24},{40,32},{32,40},{56,48},{48,56},{72,64... | collective-permute-start | bytes 4718600 | tf_op jit(solution)/shard_map/ppermute | solution.py:21
  127.9 13.7 %collective-permute-start.28 = (bf16[2,32,3072]{2,1,0:T(8,128)(2,1)S(1)}, bf16[2,32,3072]{2,1,0:T(8,128)(2,1)S(1)}, u32[]{:S(2)}, u32[]{:S(2)}) collective-permute-start(bf16[2,32,3072]{2,1,0:T(8,128)(2,1)S(1)} %get-tuple-element.25), channel_id=1, source_target_pairs={{64,0},{72,8},{80,16},{88,24},{96,32},{104,40},{112,48},{120,56},{... | collective-permute-start | bytes 1179656 | tf_op jit(solution)/shard_map/ppermute | solution.py:21
  128.0 20.9 %collective-permute-start.27 = (bf16[2,32,3072]{2,1,0:T(8,128)(2,1)S(1)}, bf16[2,32,3072]{2,1,0:T(8,128)(2,1)S(1)}, u32[]{:S(2)}, u32[]{:S(2)}) collective-permute-start(bf16[2,32,3072]{2,1,0:T(8,128)(2,1)S(1)} %get-tuple-element.25), channel_id=1, source_target_pairs={{32,0},{40,8},{48,16},{56,24},{64,32},{72,40},{80,48},{88,56},{96,... | collective-permute-start | bytes 1179656 | tf_op jit(solution)/shard_map/ppermute | solution.py:21
  131.5 17.3 %collective-permute-start.29 = (bf16[2,32,3072]{2,1,0:T(8,128)(2,1)S(1)}, bf16[2,32,3072]{2,1,0:T(8,128)(2,1)S(1)}, u32[]{:S(2)}, u32[]{:S(2)}) collective-permute-start(bf16[2,32,3072]{2,1,0:T(8,128)(2,1)S(1)} %get-tuple-element.25), channel_id=1, source_target_pairs={{96,0},{104,8},{112,16},{120,24},{0,32},{8,40},{16,48},{24,56},{32... | collective-permute-start | bytes 1179656 | tf_op jit(solution)/shard_map/ppermute | solution.py:21
  150.1 9.1 %collective-permute-start.30 = (bf16[256,3072]{1,0:T(8,128)(2,1)}, bf16[256,3072]{1,0:T(8,128)(2,1)}, u32[]{:S(2)}, u32[]{:S(2)}) collective-permute-start(bf16[256,3072]{1,0:T(8,128)(2,1)} %bitcast.20), channel_id=1, source_target_pairs={{8,0},{0,8},{24,16},{16,24},{40,32},{32,40},{56,48},{48,56},{72,64... | collective-permute-start | bytes 4718600 | tf_op jit(solution)/shard_map/ppermute | solution.py:21
  156.6 2.6 %copy-start.4 = (bf16[512,768]{1,0:T(8,128)(2,1)S(1)}, bf16[512,768]{1,0:T(8,128)(2,1)}, u32[]{:S(2)}) copy-start(bf16[512,768]{1,0:T(8,128)(2,1)} %copy-done.3) | copy-start | bytes 2359300
  156.8 12.8 %collective-permute-start.31 = (bf16[64,768]{1,0:T(8,128)(2,1)S(1)}, bf16[64,768]{1,0:T(8,128)(2,1)S(1)}, u32[]{:S(2)}, u32[]{:S(2)}) collective-permute-start(bf16[64,768]{1,0:T(8,128)(2,1)S(1)} %get-tuple-element.12), channel_id=1, source_target_pairs={{4,0},{5,1},{6,2},{7,3},{0,4},{1,5},{2,6},{3,7},{12,8},{13,9},{14,... | collective-permute-start | bytes 294920 | tf_op jit(solution)/shard_map/ppermute | solution.py:25
  157.3 16.2 %copy-start.1 = (bf16[512,768]{1,0:T(8,128)(2,1)S(1)}, bf16[512,768]{1,0:T(8,128)(2,1)}, u32[]{:S(2)}) copy-start(bf16[512,768]{1,0:T(8,128)(2,1)} %copy-done) | copy-start | bytes 2359300
  157.3 15.1 %collective-permute-start.37 = (bf16[64,768]{1,0:T(8,128)(2,1)S(1)}, bf16[64,768]{1,0:T(8,128)(2,1)S(1)}, u32[]{:S(2)}, u32[]{:S(2)}) collective-permute-start(bf16[64,768]{1,0:T(8,128)(2,1)S(1)} %get-tuple-element.13), channel_id=1, source_target_pairs={{5,0},{6,1},{7,2},{4,3},{1,4},{2,5},{3,6},{0,7},{13,8},{14,9},{15,... | collective-permute-start | bytes 294920 | tf_op jit(solution)/shard_map/ppermute | solution.py:25
  166.0 13.3 %collective-permute-start.36 = (bf16[64,768]{1,0:T(8,128)(2,1)S(1)}, bf16[64,768]{1,0:T(8,128)(2,1)S(1)}, u32[]{:S(2)}, u32[]{:S(2)}) collective-permute-start(bf16[64,768]{1,0:T(8,128)(2,1)S(1)} %get-tuple-element.14), channel_id=1, source_target_pairs={{1,0},{2,1},{3,2},{0,3},{5,4},{6,5},{7,6},{4,7},{9,8},{10,9},{11,1... | collective-permute-start | bytes 294920 | tf_op jit(solution)/shard_map/ppermute | solution.py:25
  166.2 13.1 %collective-permute-start.35 = (bf16[64,768]{1,0:T(8,128)(2,1)S(1)}, bf16[64,768]{1,0:T(8,128)(2,1)S(1)}, u32[]{:S(2)}, u32[]{:S(2)}) collective-permute-start(bf16[64,768]{1,0:T(8,128)(2,1)S(1)} %get-tuple-element.15), channel_id=1, source_target_pairs={{6,0},{7,1},{4,2},{5,3},{2,4},{3,5},{0,6},{1,7},{14,8},{15,9},{12,... | collective-permute-start | bytes 294920 | tf_op jit(solution)/shard_map/ppermute | solution.py:25
  169.1 10.2 %collective-permute-start.34 = (bf16[64,768]{1,0:T(8,128)(2,1)S(1)}, bf16[64,768]{1,0:T(8,128)(2,1)S(1)}, u32[]{:S(2)}, u32[]{:S(2)}) collective-permute-start(bf16[64,768]{1,0:T(8,128)(2,1)S(1)} %get-tuple-element.16), channel_id=1, source_target_pairs={{2,0},{3,1},{0,2},{1,3},{6,4},{7,5},{4,6},{5,7},{10,8},{11,9},{8,1... | collective-permute-start | bytes 294920 | tf_op jit(solution)/shard_map/ppermute | solution.py:25
  169.6 9.7 %collective-permute-start.33 = (bf16[64,768]{1,0:T(8,128)(2,1)S(1)}, bf16[64,768]{1,0:T(8,128)(2,1)S(1)}, u32[]{:S(2)}, u32[]{:S(2)}) collective-permute-start(bf16[64,768]{1,0:T(8,128)(2,1)S(1)} %get-tuple-element.17), channel_id=1, source_target_pairs={{7,0},{4,1},{5,2},{6,3},{3,4},{0,5},{1,6},{2,7},{15,8},{12,9},{13,... | collective-permute-start | bytes 294920 | tf_op jit(solution)/shard_map/ppermute | solution.py:25
  172.4 7.7 %collective-permute-start.32 = (bf16[64,768]{1,0:T(8,128)(2,1)S(1)}, bf16[64,768]{1,0:T(8,128)(2,1)S(1)}, u32[]{:S(2)}, u32[]{:S(2)}) collective-permute-start(bf16[64,768]{1,0:T(8,128)(2,1)S(1)} %get-tuple-element.18), channel_id=1, source_target_pairs={{3,0},{0,1},{1,2},{2,3},{7,4},{4,5},{5,6},{6,7},{11,8},{8,9},{9,10... | collective-permute-start | bytes 294920 | tf_op jit(solution)/shard_map/ppermute | solution.py:25

commit v2 on v0

v2 whole, which is shorter than its diff:
```python
import functools
import math

import jax
import jax.numpy as jnp
from jax import lax
from jax.experimental import pallas as pl
from jax.experimental.pallas import tpu as pltpu
from jax.sharding import PartitionSpec as P

ROW = [(y, x, c) for y in range(4) for x in range(2) for c in range(2)]
COL = [(x, z) for x in range(2) for z in range(4)]
MIB = 1 << 20
COST = pl.CostEstimate(flops=1, bytes_accessed=1, transcendentals=0)


def at_row(y, x, c):
    return ((y % 4) * 2 + x % 2) * 2 + c % 2


def at_col(x, z):
    return (x % 2) * 4 + z % 4


def from_row(a, dy, dx, dc):
    return lax.ppermute(a, "row", [(at_row(y + dy, x + dx, c + dc), at_row(y, x, c)) for y, x, c in ROW])


def from_col(a, dx, dz):
    return lax.ppermute(a, "col", [(at_col(x + dx, z + dz), at_col(x, z)) for x, z in COL])


def gelu_value(v):
    inner = math.sqrt(2.0 / math.pi) * (v + 0.044715 * v * v * v)
    return 0.5 * v * (1.0 + jnp.tanh(inner))


def gelu_slope(v):
    coeff = math.sqrt(2.0 / math.pi)
    tanh_part = jnp.tanh(coeff * (v + 0.044715 * v * v * v))
    return 0.5 * (1.0 + tanh_part) + 0.5 * v * (1.0 - tanh_part * tanh_part) * coeff * (
        1.0 + 3.0 * 0.044715 * v * v
    )


def f32(a):
    return a.astype(jnp.float32)


def bf16(a):
    return a.astype(jnp.bfloat16)


def contract(a, b, da, db):
    return lax.dot_general(a, b, (((da,), (db,)), ((), ())), preferred_element_type=jnp.float32)


VMEM = pl.BlockSpec(memory_space=pltpu.VMEM)
SMEM = pl.BlockSpec(memory_space=pltpu.SMEM)
TILE = 512


def params(mib):
    return pltpu.CompilerParams(vmem_limit_bytes=mib * MIB)


def loaded(first, second):
    def body(first_ref, second_ref, first_out, second_out, sems):
        copies = [
            pltpu.make_async_copy(first_ref, first_out, sems.at[0]),
            pltpu.make_async_copy(second_ref, second_out, sems.at[1]),
        ]
        for copy in copies:
            copy.start()
        for copy in copies:
            copy.wait()

    return pl.pallas_call(
        body,
        in_specs=[pl.BlockSpec(memory_space=pl.ANY)] * 2,
        out_specs=[VMEM] * 2,
        out_shape=[pltpu.VMEM(first.shape, first.dtype), pltpu.VMEM(second.shape, second.dtype)],
        scratch_shapes=[pltpu.SemaphoreType.DMA((2,))],
        compiler_params=params(16),
        cost_estimate=COST,
    )(pltpu.with_memory_space_constraint(first, pltpu.HBM), pltpu.with_memory_space_constraint(second, pltpu.HBM))


def project(tokens, weight, place, hidden_dim):
    rows, k = tokens.shape
    hidden = weight.shape[hidden_dim]
    half = rows // 2

    def body(place_ref, tokens_ref, weight_ref, keep_ref, send_ref, placed_ref):
        for b in range(rows // 16):
            start = pl.multiple_of(place_ref[b] * 16, 16)
            placed_ref[pl.ds(16 * b, 16), :] = tokens_ref[pl.ds(start, 16), :]
        for i in range(hidden // TILE):
            part = pl.ds(i * TILE, TILE)
            weight_part = weight_ref[:, part] if hidden_dim == 1 else weight_ref[part, :]
            total = contract(placed_ref[...], weight_part, 1, 1 - hidden_dim)
            keep_ref[:, part] = total[:half]
            send_ref[:, part] = bf16(total[half:])

    return pl.pallas_call(
        body,
        in_specs=[SMEM, VMEM, VMEM],
        out_specs=[VMEM, VMEM, VMEM],
        out_shape=[
            pltpu.VMEM((half, hidden), jnp.float32),
            pltpu.VMEM((half, hidden), jnp.bfloat16),
            pltpu.VMEM((rows, k), jnp.bfloat16),
        ],
        compiler_params=params(16),
        cost_estimate=COST,
    )(place, tokens, weight)


def back_project(own, other, weight, place):
    p, q, _, t, hidden = own.shape
    half = p * q * t
    k = weight.shape[0]

    def body(place_ref, own_ref, other_ref, weight_ref, out_ref):
        grad = jnp.concatenate([own_ref[:, :, 1].reshape(half, hidden), other_ref[:, :, 1].reshape(half, hidden)])
        for i in range(k // 256):
            part = pl.ds(i * 256, 256)
            total = contract(grad, weight_ref[part, :], 1, 1)
            for b in range(2 * half // 16):
                start = pl.multiple_of(place_ref[b] * 16, 16)
                out_ref[pl.ds(start, 16), part] = total[16 * b : 16 * b + 16]

    return pl.pallas_call(
        body,
        in_specs=[SMEM, VMEM, VMEM, VMEM],
        out_specs=VMEM,
        out_shape=pltpu.VMEM((2 * half, k), jnp.float32),
        compiler_params=params(16),
        cost_estimate=COST,
    )(place, own, other, weight)


def weight_grad(parts, tokens, which):
    hidden = parts[0].shape[-1]
    rows, k = tokens[0].shape
    chunks = len(tokens)
    steps = hidden // TILE

    def body(*refs):
        part_refs, token_refs, out_ref = refs[: 2 * chunks], refs[2 * chunks : 3 * chunks], refs[3 * chunks]
        made, sems = refs[3 * chunks + 1 :][:2]
        both = jnp.concatenate([ref[...] for ref in token_refs])
        if which == 1:
            turned = refs[-1]
            turned[...] = both.T

        copies = []
        for i in range(steps):
            part = pl.ds(i * TILE, TILE)
            value = jnp.concatenate([ref[:, :, which, :, part].reshape(rows // 2, TILE) for ref in part_refs])
            if which == 0:
                made[i] = bf16(contract(value, both, 0, 0))
                target = out_ref.at[part, :]
            else:
                made[i] = bf16(contract(turned[...], value, 1, 0))
                target = out_ref.at[:, part]
            copies.append(pltpu.make_async_copy(made.at[i], target, sems.at[i]))
            copies[-1].start()
        for copy in copies:
            copy.wait()

    return pl.pallas_call(
        body,
        in_specs=[VMEM] * (3 * chunks),
        out_specs=pl.BlockSpec(memory_space=pl.ANY),
        out_shape=jax.ShapeDtypeStruct((hidden, k) if which == 0 else (k, hidden), jnp.bfloat16),
        scratch_shapes=[
            pltpu.VMEM((steps, TILE, k) if which == 0 else (steps, k, TILE), jnp.bfloat16),
            pltpu.SemaphoreType.DMA((steps,)),
        ]
        + ([] if which == 0 else [pltpu.VMEM((k, chunks * rows), jnp.bfloat16)]),
        compiler_params=params(16),
        cost_estimate=COST,
    )(*parts, *tokens)


def gather_y(a):
    return jnp.stack([a] + [from_row(a, dy, 0, 0) for dy in (1, 2, 3)])


def gather_x(a):
    return jnp.stack([a, from_row(a, 0, 1, 0)])


def gather_z(a):
    return jnp.stack([a] + [from_col(a, 0, dz) for dz in (1, 2, 3)])


def sum_y(part):
    got = [from_row(bf16(part(dy)), -dy, 0, 0) for dy in (1, 3, 2)]
    return part(0) + f32(got[0]) + f32(got[1]) + f32(got[2])


def sum_x(part):
    return part(0) + f32(from_row(bf16(part(1)), 0, 1, 0))


def sum_z(part):
    got = [from_col(bf16(part[dz]), 0, -dz) for dz in (1, 3, 2)]
    return part[0] + f32(got[0]) + f32(got[1]) + f32(got[2])


def tied(a, *others):
    return lax.optimization_barrier((a, *others))[0]


def on_device(inputs, cotangent, weight_in, weight_out):
    n, k = inputs.shape
    row = lax.axis_index("row")
    y, x, c = row // 4, (row // 2) % 2, row % 2

    def place_of(x_outer):
        b = jnp.arange(16, dtype=jnp.int32)
        dc = b // 8
        dx, dy = ((b // 4) % 2, b % 4) if x_outer else (b % 2, (b // 2) % 4)
        return (((y + dy) % 4) * 2 + (c + dc) % 2) * 2 + (x + dx) % 2

    def pairs_of(tokens, place, weights):
        pairs, placed = [], []
        for m in range(2):
            keep, send, rel = project(tokens[:, m].reshape(4 * n, k), weights[m], place, 1 - m)
            pairs.append(keep + f32(from_row(send, 0, 0, 1)))
            placed.append(rel)
        return jnp.stack(pairs), placed

    def made_of(sums):
        pre, act_grad = sums
        return jnp.stack([bf16(gelu_value(pre)), bf16(act_grad * gelu_slope(pre))])

    own = jnp.stack([inputs, cotangent])
    near = from_col(own, 1, 0)
    weights = loaded(tied(weight_in, near), weight_out)
    tokens_a = jnp.stack([tied(own, weights[0])] + [from_col(own, 0, dz) for dz in (1, 2, 3)])
    tokens_a, tokens_b = lax.optimization_barrier((tokens_a, gather_z(near)))
    place_a, place_b = place_of(True), place_of(False)
    pair_a, placed_a = pairs_of(tokens_a, place_a, weights)
    pair_b, placed_b = pairs_of(tokens_b, place_b, weights)
    pair_a, pair_b = pair_a.reshape(2, 2, 4, 16, -1), pair_b.reshape(2, 4, 2, 16, -1)

    one_a, one_b = sum_y(lambda dy: pair_a[:, :, dy]), sum_x(lambda dx: pair_b[:, :, dx])
    one_a, one_b = lax.optimization_barrier((one_a, one_b))
    sums_a, sums_b = sum_x(lambda dx: one_a[:, dx]), sum_y(lambda dy: one_b[:, dy])
    made_a, made_b = made_of(sums_a), made_of(sums_b)
    made_a, made_b = lax.optimization_barrier((made_a, made_b))
    part_a, part_b = lax.optimization_barrier((gather_y(made_a), gather_x(made_b)))
    half_a, half_b = gather_x(part_a), gather_y(part_b)
    other_b = from_row(half_b, 0, 0, 1)
    back_b = back_project(half_b, other_b, weights[0], place_b).reshape(4, n, k)
    other_a = from_row(half_a, 0, 0, 1)
    back_a = back_project(half_a, other_a, weights[0], place_a).reshape(4, n, k)
    total = sum_z(back_a)
    for dz in (0, 1, 3, 2):
        total = total + f32(from_col(bf16(back_b[dz]), 1, -dz))
    parts = [half_a, other_a, half_b, other_b]
    weight_out_grad = weight_grad(parts, [placed_a[1], placed_b[1]], 0)
    weight_in_grad = weight_grad(parts, [placed_a[0], placed_b[0]], 1)
    return (weight_in_grad, weight_out_grad, bf16(total))


def solution(mesh):
    return jax.shard_map(
        on_device,
        mesh=mesh,
        in_specs=(P("col", "row"), P("col", "row"), P("row", "col"), P("col", "row")),
        out_specs=(P("row", "col"), P("col", "row"), P("col", "row")),
        check_vma=False,
    )
```

time: 419 us -> 139 us (0.33)
  waiting for transfers between devices: 297 us -> 57.4 us
  blocking collectives: 62.1 us -> 0 us
  starting transfers between devices: 0.16 us -> 52.7 us
  matrix products: 33.5 us -> 0 us
  Pallas kernels: 0 us -> 22.8 us
  between operations: 13.8 us -> 1.03 us
  local copies, waits for them, and re-layouts: 7.45 us -> 0.31 us
    psum x1 -> x0, waiting for transfers between devices: 133 us -> none  [on_device(): lax.psum(jnp.dot(inputs_all, weight_in, preferred_element_type=jnp.float3...]
    reduce_scatter x2 -> x0, waiting for transfers between devices: 113 us -> none  [the longest x1 92.5 us: on_device(): lax.psum_scatter(lax.dot_general(cotangent_all, weight_out, (((1,), (1,))...]
    all_gather x2 -> x0, blocking collectives: 62.1 us -> none  [the longest x1 31.2 us: on_device(): lax.all_gather(inputs, 'col', axis=0, tiled=True)]
    ppermute x0 -> x36, waiting for transfers between devices: none -> 57.4 us  [the longest x22 50.7 us: from_row(): lax.ppermute(a, 'row', [(at_row(y + dy, x + dx, c + dc), at_row(y, x, c))...]
    ppermute x0 -> x36, starting transfers between devices: none -> 52.7 us  [the longest x22 28.2 us: from_row(): lax.ppermute(a, 'row', [(at_row(y + dy, x + dx, c + dc), at_row(y, x, c))...]
    all_gather x1 -> x0, waiting for transfers between devices: 50.7 us -> none  [on_device(): grad_all = lax.all_gather(pre_grad, 'row', axis=0, tiled=True)]
    dot_general x5 -> x0, matrix products: 33.5 us -> none  [the longest x1 8.47 us: on_device(): lax.dot_general(act_all, cotangent_all, (((0,), (0,)), ((), ())), preferr...]
    pallas_call x0 -> x9, Pallas kernels: none -> 22.8 us  [the longest x4 7.85 us: project(): pl.pallas_call(body, in_specs=[SMEM, VMEM, VMEM], out_specs=[VMEM, VMEM,...]
  transfers between devices with their start and end apart: 4 -> 36, of which waited for: 4 -> 14; matrix products, arithmetic and copies ran while one was open for 6% -> 2% of each run, Pallas kernels for 0% -> 15%
where the time goes in v2:
time: 139 us
  waiting for transfers between devices  57.4 us (41%)
  starting transfers between devices  52.7 us (38%)
  Pallas kernels  22.8 us (16%)
  other arithmetic  4.6 us (3%)
    ppermute x22, waiting for transfers between devices, from_row(): lax.ppermute(a, 'row', [(at_row(y + dy, x + dx, c + dc), at_row(y, x, c))...  50.7 us
    ppermute x22, starting transfers between devices, from_row(): lax.ppermute(a, 'row', [(at_row(y + dy, x + dx, c + dc), at_row(y, x, c))...  28.2 us
    ppermute x14, starting transfers between devices, from_col(): lax.ppermute(a, 'col', [(at_col(x + dx, z + dz), at_col(x, z)) for x, z i...  24.5 us
    pallas_call x4, Pallas kernels, project(): pl.pallas_call(body, in_specs=[SMEM, VMEM, VMEM], out_specs=[VMEM, VMEM,...  7.85 us
    pallas_call x2, Pallas kernels, weight_grad(): pl.pallas_call(body, in_specs=[VMEM] * (3 * chunks), out_specs=pl.BlockSp...  7.25 us
    ppermute x14, waiting for transfers between devices, from_col(): lax.ppermute(a, 'col', [(at_col(x + dx, z + dz), at_col(x, z)) for x, z i...  6.73 us
    pallas_call x2, Pallas kernels, back_project(): pl.pallas_call(body, in_specs=[SMEM, VMEM, VMEM, VMEM], out_specs=VMEM, o...  3.94 us
    pallas_call x1, Pallas kernels, loaded(): pl.pallas_call(body, in_specs=[pl.BlockSpec(memory_space=pl.ANY)] * 2, ou...  3.8 us
  transfers between devices with their start and end apart: 36, of which 14 were waited for; matrix products, arithmetic and copies ran while one was open for 2% of the time, Pallas kernels for 15%

profile of v2, /device:TPU:0, one launch (start us, length us, event | category | flops | bytes accessed | tf_op | source)
XLA Modules:
  0.0 138.8 jit_solution(10002282343341961653)
XLA Ops:
  0.6 1.0 pad_maximum_fusion.8
  1.6 1.7 %collective-permute-start = (bf16[2,64,768]{2,1,0:T(8,128)(2,1)S(1)}, bf16[2,64,768]{2,1,0:T(8,128)(2,1)S(1)}, u32[]{:S(2)}, u32[]{:S(2)}) collective-permute-start(bf16[2,64,768]{2,1,0:T(8,128)(2,1)S(1)} %pad_maximum_fusion.8), channel_id=1, source_target_pairs={{4,0},{5,1},{6,2},{7,3},{0,4},{1,5},{2,6},{3,7},{12,8},{13,9},{14,... | collective-permute-start | bytes 589832 | tf_op jit(solution)/shard_map/ppermute | solution.py:30
  3.2 1.9 %collective-permute-start.3 = (bf16[2,64,768]{2,1,0:T(8,128)(2,1)S(1)}, bf16[2,64,768]{2,1,0:T(8,128)(2,1)S(1)}, u32[]{:S(2)}, u32[]{:S(2)}) collective-permute-start(bf16[2,64,768]{2,1,0:T(8,128)(2,1)S(1)} %pad_maximum_fusion.8), channel_id=1, source_target_pairs={{3,0},{0,1},{1,2},{2,3},{7,4},{4,5},{5,6},{6,7},{11,8},{8,9},{9,10... | collective-permute-start | bytes 589832 | tf_op jit(solution)/shard_map/ppermute | solution.py:30
  5.2 3.6 %collective-permute-start.2 = (bf16[2,64,768]{2,1,0:T(8,128)(2,1)S(1)}, bf16[2,64,768]{2,1,0:T(8,128)(2,1)S(1)}, u32[]{:S(2)}, u32[]{:S(2)}) collective-permute-start(bf16[2,64,768]{2,1,0:T(8,128)(2,1)S(1)} %pad_maximum_fusion.8), channel_id=1, source_target_pairs={{2,0},{3,1},{0,2},{1,3},{6,4},{7,5},{4,6},{5,7},{10,8},{11,9},{8,1... | collective-permute-start | bytes 589832 | tf_op jit(solution)/shard_map/ppermute | solution.py:30
  8.7 1.0 collective-permute-start.1
  9.8 1.0 collective-permute-start.6
  10.8 3.1 %collective-permute-start.5 = (bf16[2,64,768]{2,1,0:T(8,128)(2,1)S(1)}, bf16[2,64,768]{2,1,0:T(8,128)(2,1)S(1)}, u32[]{:S(2)}, u32[]{:S(2)}) collective-permute-start(bf16[2,64,768]{2,1,0:T(8,128)(2,1)S(1)} %collective-permute-done), channel_id=1, source_target_pairs={{2,0},{3,1},{0,2},{1,3},{6,4},{7,5},{4,6},{5,7},{10,8},{11,9},{8,1... | collective-permute-start | bytes 589832 | tf_op jit(solution)/shard_map/ppermute | solution.py:30
  13.9 1.2 collective-permute-start.4
  15.1 3.8 %shard_map.67 = (bf16[768,3072]{1,0:T(8,128)(2,1)S(1)}, bf16[3072,768]{1,0:T(8,128)(2,1)S(1)}) custom-call(bf16[768,3072]{1,0:T(8,128)(2,1)} %first_ref, bf16[3072,768]{1,0:T(8,128)(2,1)} %second_ref.1), custom_call_target="tpu_custom_call" | custom-call | flops 1 | bytes 1 | tf_op jit(solution)/shard_map/pallas_call | solution.py:78
  19.1 1.6 %collective-permute-done.6 = bf16[2,64,768]{2,1,0:T(8,128)(2,1)S(1)} collective-permute-done((bf16[2,64,768]{2,1,0:T(8,128)(2,1)S(1)}, bf16[2,64,768]{2,1,0:T(8,128)(2,1)S(1)}, u32[]{:S(2)}, u32[]{:S(2)}) %collective-permute-start.6) | collective-permute-done | bytes 196640 | tf_op jit(solution)/shard_map/ppermute | solution.py:30
  20.7 5.1 %collective-permute-done.5 = bf16[2,64,768]{2,1,0:T(8,128)(2,1)S(1)} collective-permute-done((bf16[2,64,768]{2,1,0:T(8,128)(2,1)S(1)}, bf16[2,64,768]{2,1,0:T(8,128)(2,1)S(1)}, u32[]{:S(2)}, u32[]{:S(2)}) %collective-permute-start.5) | collective-permute-done | bytes 196640 | tf_op jit(solution)/shard_map/ppermute | solution.py:30
  26.0 2.0 %shard_map.69 = (f32[128,3072]{1,0:T(8,128)S(1)}, bf16[128,3072]{1,0:T(8,128)(2,1)S(1)}, bf16[256,768]{1,0:T(8,128)(2,1)S(1)}) custom-call(s32[16]{0:T(128)S(1)} %get-tuple-element.72.place_ref, bf16[256,768]{1,0:T(8,128)(2,1)S(1)} %bitcast.69, bf16[3072,768]{1,0:T(8,128)(2,1)S(1)} %get-tuple-element.33.weight_ref), custom_call_target="tpu_custom_call" | custom-call | flops 1 | bytes 1 | tf_op jit(solution)/shard_map/pallas_call | solution.py:105
  28.1 2.0 %shard_map.68 = (f32[128,3072]{1,0:T(8,128)S(1)}, bf16[128,3072]{1,0:T(8,128)(2,1)S(1)}, bf16[256,768]{1,0:T(8,128)(2,1)S(1)}) custom-call(s32[16]{0:T(128)S(1)} %get-tuple-element.72.place_ref, bf16[256,768]{1,0:T(8,128)(2,1)S(1)} %bitcast.68, bf16[768,3072]{1,0:T(8,128)(2,1)S(1)} %get-tuple-element.28.weight_ref), custom_call_target="tpu_custom_call" | custom-call | flops 1 | bytes 1 | tf_op jit(solution)/shard_map/pallas_call | solution.py:105
  30.6 2.0 %shard_map.71 = (f32[128,3072]{1,0:T(8,128)S(1)}, bf16[128,3072]{1,0:T(8,128)(2,1)S(1)}, bf16[256,768]{1,0:T(8,128)(2,1)S(1)}) custom-call(s32[16]{0:T(128)S(1)} %get-tuple-element.73.place_ref, bf16[256,768]{1,0:T(8,128)(2,1)S(1)} %bitcast.67, bf16[3072,768]{1,0:T(8,128)(2,1)S(1)} %get-tuple-element.33.weight_ref), custom_call_target="tpu_custom_call" | custom-call | flops 1 | bytes 1 | tf_op jit(solution)/shard_map/pallas_call | solution.py:105
  32.7 2.0 %shard_map.70 = (f32[128,3072]{1,0:T(8,128)S(1)}, bf16[128,3072]{1,0:T(8,128)(2,1)S(1)}, bf16[256,768]{1,0:T(8,128)(2,1)S(1)}) custom-call(s32[16]{0:T(128)S(1)} %get-tuple-element.73.place_ref, bf16[256,768]{1,0:T(8,128)(2,1)S(1)} %bitcast.66, bf16[768,3072]{1,0:T(8,128)(2,1)S(1)} %get-tuple-element.28.weight_ref), custom_call_target="tpu_custom_call" | custom-call | flops 1 | bytes 1 | tf_op jit(solution)/shard_map/pallas_call | solution.py:105
  35.7 1.7 %collective-permute-start.9 = (bf16[2,2,16,3072]{3,2,0,1:T(8,128)(2,1)S(1)}, bf16[2,2,16,3072]{3,2,0,1:T(8,128)(2,1)S(1)}, u32[]{:S(2)}, u32[]{:S(2)}) collective-permute-start(bf16[2,2,16,3072]{3,2,0,1:T(8,128)(2,1)S(1)} %get-tuple-element.51), channel_id=1, source_target_pairs={{96,0},{104,8},{112,16},{120,24},{0,32},{8,40},{16,48},{24,56},{32... | collective-permute-start | bytes 1179656 | tf_op jit(solution)/shard_map/ppermute | solution.py:26
  37.4 2.9 %collective-permute-start.11 = (bf16[2,2,16,3072]{3,2,0,1:T(8,128)(2,1)S(1)}, bf16[2,2,16,3072]{3,2,0,1:T(8,128)(2,1)S(1)}, u32[]{:S(2)}, u32[]{:S(2)}) collective-permute-start(bf16[2,2,16,3072]{3,2,0,1:T(8,128)(2,1)S(1)} %get-tuple-element.52), channel_id=1, source_target_pairs={{64,0},{72,8},{80,16},{88,24},{96,32},{104,40},{112,48},{120,56},{... | collective-permute-start | bytes 1179656 | tf_op jit(solution)/shard_map/ppermute | solution.py:26
  40.3 1.3 collective-permute-start.10
  42.5 2.8 %collective-permute-start.14 = (bf16[2,4,16,3072]{3,2,0,1:T(8,128)(2,1)S(1)}, bf16[2,4,16,3072]{3,2,0,1:T(8,128)(2,1)S(1)}, u32[]{:S(2)}, u32[]{:S(2)}) collective-permute-start(bf16[2,4,16,3072]{3,2,0,1:T(8,128)(2,1)S(1)} %fusion.1), channel_id=1, source_target_pairs={{16,0},{24,8},{0,16},{8,24},{48,32},{56,40},{32,48},{40,56},{80,64... | collective-permute-start | bytes 2359304 | tf_op jit(solution)/shard_map/ppermute | solution.py:26
  45.3 2.8 %collective-permute-done.9 = bf16[2,2,16,3072]{3,2,0,1:T(8,128)(2,1)S(1)} collective-permute-done((bf16[2,2,16,3072]{3,2,0,1:T(8,128)(2,1)S(1)}, bf16[2,2,16,3072]{3,2,0,1:T(8,128)(2,1)S(1)}, u32[]{:S(2)}, u32[]{:S(2)}) %collective-permute-start.9) | collective-permute-done | bytes 393248 | tf_op jit(solution)/shard_map/ppermute | solution.py:26
  48.1 9.6 %collective-permute-done.11 = bf16[2,2,16,3072]{3,2,0,1:T(8,128)(2,1)S(1)} collective-permute-done((bf16[2,2,16,3072]{3,2,0,1:T(8,128)(2,1)S(1)}, bf16[2,2,16,3072]{3,2,0,1:T(8,128)(2,1)S(1)}, u32[]{:S(2)}, u32[]{:S(2)}) %collective-permute-start.11) | collective-permute-done | bytes 393248 | tf_op jit(solution)/shard_map/ppermute | solution.py:26
  57.9 4.8 %collective-permute-done.14 = bf16[2,4,16,3072]{3,2,0,1:T(8,128)(2,1)S(1)} collective-permute-done((bf16[2,4,16,3072]{3,2,0,1:T(8,128)(2,1)S(1)}, bf16[2,4,16,3072]{3,2,0,1:T(8,128)(2,1)S(1)}, u32[]{:S(2)}, u32[]{:S(2)}) %collective-permute-start.14) | collective-permute-done | bytes 786464 | tf_op jit(solution)/shard_map/ppermute | solution.py:26
  62.9 2.8 %collective-permute-start.15 = (bf16[2,16,3072]{2,1,0:T(8,128)(2,1)S(1)}, bf16[2,16,3072]{2,1,0:T(8,128)(2,1)S(1)}, u32[]{:S(2)}, u32[]{:S(2)}) collective-permute-start(bf16[2,16,3072]{2,1,0:T(8,128)(2,1)S(1)} %fusion.21), channel_id=1, source_target_pairs={{16,0},{24,8},{0,16},{8,24},{48,32},{56,40},{32,48},{40,56},{80,64... | collective-permute-start | bytes 589832 | tf_op jit(solution)/shard_map/ppermute | solution.py:26
  65.9 0.7 collective-permute-start.16
  66.6 1.1 collective-permute-start.18
  67.7 1.7 %collective-permute-start.17 = (bf16[2,16,3072]{2,1,0:T(8,128)(2,1)S(1)}, bf16[2,16,3072]{2,1,0:T(8,128)(2,1)S(1)}, u32[]{:S(2)}, u32[]{:S(2)}) collective-permute-start(bf16[2,16,3072]{2,1,0:T(8,128)(2,1)S(1)} %get-tuple-element.56), channel_id=1, source_target_pairs={{32,0},{40,8},{48,16},{56,24},{64,32},{72,40},{80,48},{88,56},{96,... | collective-permute-start | bytes 589832 | tf_op jit(solution)/shard_map/ppermute | solution.py:26
  69.4 0.8 collective-permute-done.15
  70.4 5.8 %collective-permute-done.16 = bf16[2,16,3072]{2,1,0:T(8,128)(2,1)S(1)} collective-permute-done((bf16[2,16,3072]{2,1,0:T(8,128)(2,1)S(1)}, bf16[2,16,3072]{2,1,0:T(8,128)(2,1)S(1)}, u32[]{:S(2)}, u32[]{:S(2)}) %collective-permute-start.16) | collective-permute-done | bytes 196640 | tf_op jit(solution)/shard_map/ppermute | solution.py:26
  77.1 0.9 collective-permute-start.22
  78.4 3.6 %collective-permute-start.20 = (bf16[2,16,3072]{2,1,0:T(8,128)(2,1)S(1)}, bf16[2,16,3072]{2,1,0:T(8,128)(2,1)S(1)}, u32[]{:S(2)}, u32[]{:S(2)}) collective-permute-start(bf16[2,16,3072]{2,1,0:T(8,128)(2,1)S(1)} %pad_maximum_fusion.9), channel_id=1, source_target_pairs={{64,0},{72,8},{80,16},{88,24},{96,32},{104,40},{112,48},{120,56},{... | collective-permute-start | bytes 589832 | tf_op jit(solution)/shard_map/ppermute | solution.py:26
  82.0 2.4 %collective-permute-done.22 = bf16[2,16,3072]{2,1,0:T(8,128)(2,1)S(1)} collective-permute-done((bf16[2,16,3072]{2,1,0:T(8,128)(2,1)S(1)}, bf16[2,16,3072]{2,1,0:T(8,128)(2,1)S(1)}, u32[]{:S(2)}, u32[]{:S(2)}) %collective-permute-start.22) | collective-permute-done | bytes 196640 | tf_op jit(solution)/shard_map/ppermute | solution.py:26
  84.4 2.4 %collective-permute-done.21 = bf16[2,16,3072]{2,1,0:T(8,128)(2,1)S(1)} collective-permute-done((bf16[2,16,3072]{2,1,0:T(8,128)(2,1)S(1)}, bf16[2,16,3072]{2,1,0:T(8,128)(2,1)S(1)}, u32[]{:S(2)}, u32[]{:S(2)}) %collective-permute-start.21) | collective-permute-done | bytes 196640 | tf_op jit(solution)/shard_map/ppermute | solution.py:26
  86.8 2.7 %collective-permute-done.20 = bf16[2,16,3072]{2,1,0:T(8,128)(2,1)S(1)} collective-permute-done((bf16[2,16,3072]{2,1,0:T(8,128)(2,1)S(1)}, bf16[2,16,3072]{2,1,0:T(8,128)(2,1)S(1)}, u32[]{:S(2)}, u32[]{:S(2)}) %collective-permute-start.20) | collective-permute-done | bytes 196640 | tf_op jit(solution)/shard_map/ppermute | solution.py:26
  89.7 2.8 %collective-permute-start.23 = (bf16[4,2,16,3072]{3,2,1,0:T(8,128)(2,1)S(1)}, bf16[4,2,16,3072]{3,2,1,0:T(8,128)(2,1)S(1)}, u32[]{:S(2)}, u32[]{:S(2)}) collective-permute-start(bf16[4,2,16,3072]{3,2,1,0:T(8,128)(2,1)S(1)} %pad_maximum_fusion.6), channel_id=1, source_target_pairs={{16,0},{24,8},{0,16},{8,24},{48,32},{56,40},{32,48},{40,56},{80,64... | collective-permute-start | bytes 2359304 | tf_op jit(solution)/shard_map/ppermute | solution.py:26
  92.5 3.5 %collective-permute-start.26 = (bf16[2,2,16,3072]{3,2,1,0:T(8,128)(2,1)S(1)}, bf16[2,2,16,3072]{3,2,1,0:T(8,128)(2,1)S(1)}, u32[]{:S(2)}, u32[]{:S(2)}) collective-permute-start(bf16[2,2,16,3072]{3,2,1,0:T(8,128)(2,1)S(1)} %pad_maximum_fusion.7), channel_id=1, source_target_pairs={{64,0},{72,8},{80,16},{88,24},{96,32},{104,40},{112,48},{120,56},{... | collective-permute-start | bytes 1179656 | tf_op jit(solution)/shard_map/ppermute | solution.py:26
  96.0 7.7 %collective-permute-done.27 = bf16[2,2,16,3072]{3,2,1,0:T(8,128)(2,1)S(1)} collective-permute-done((bf16[2,2,16,3072]{3,2,1,0:T(8,128)(2,1)S(1)}, bf16[2,2,16,3072]{3,2,1,0:T(8,128)(2,1)S(1)}, u32[]{:S(2)}, u32[]{:S(2)}) %collective-permute-start.27) | collective-permute-done | bytes 393248 | tf_op jit(solution)/shard_map/ppermute | solution.py:26
  103.7 8.3 %collective-permute-done.26 = bf16[2,2,16,3072]{3,2,1,0:T(8,128)(2,1)S(1)} collective-permute-done((bf16[2,2,16,3072]{3,2,1,0:T(8,128)(2,1)S(1)}, bf16[2,2,16,3072]{3,2,1,0:T(8,128)(2,1)S(1)}, u32[]{:S(2)}, u32[]{:S(2)}) %collective-permute-start.26) | collective-permute-done | bytes 393248 | tf_op jit(solution)/shard_map/ppermute | solution.py:26
  113.0 2.7 %collective-permute-done.28.refs_3_.other_ref = bf16[4,2,2,16,3072]{4,3,2,1,0:T(8,128)(2,1)S(1)} collective-permute-done((bf16[4,2,2,16,3072]{4,3,2,1,0:T(8,128)(2,1)S(1)}, bf16[4,2,2,16,3072]{4,3,2,1,0:T(8,128)(2,1)S(1)}, u32[]{:S(2)}, u32[]{:S(2)}) %collective-permute-start.28) | collective-permute-done | bytes 1572896 | tf_op jit(solution)/shard_map/ppermute | solution.py:26
  115.7 2.0 %shard_map.75 = f32[256,768]{1,0:T(8,128)S(1)} custom-call(s32[16]{0:T(128)S(1)} %get-tuple-element.73.place_ref, bf16[4,2,2,16,3072]{4,3,2,1,0:T(8,128)(2,1)S(1)} %pad_maximum_fusion.3.refs_2_.own_ref, bf16[4,2,2,16,3072]{4,3,2,1,0:T(8,128)(2,1)S(1)} %collective-permute-done.28.refs_3_.other_ref, bf16[768,3072]{1,0:T(8,128)(2,1)S(1)} %get-tuple-element.28.weight_ref), custom_call_target="tpu_custom_call" | custom-call | flops 1 | bytes 1 | tf_op jit(solution)/shard_map/pallas_call | solution.py:133
  118.0 3.5 %collective-permute-start.35 = (bf16[64,768]{1,0:T(8,128)(2,1)S(1)}, bf16[64,768]{1,0:T(8,128)(2,1)S(1)}, u32[]{:S(2)}, u32[]{:S(2)}) collective-permute-start(bf16[64,768]{1,0:T(8,128)(2,1)S(1)} %get-tuple-element.65), channel_id=1, source_target_pairs={{6,0},{7,1},{4,2},{5,3},{2,4},{3,5},{0,6},{1,7},{14,8},{15,9},{12,... | collective-permute-start | bytes 294920 | tf_op jit(solution)/shard_map/ppermute | solution.py:30
  121.5 1.2 collective-permute-start.34
  122.7 1.7 %collective-permute-start.33 = (bf16[64,768]{1,0:T(8,128)(2,1)S(1)}, bf16[64,768]{1,0:T(8,128)(2,1)S(1)}, u32[]{:S(2)}, u32[]{:S(2)}) collective-permute-start(bf16[64,768]{1,0:T(8,128)(2,1)S(1)} %get-tuple-element.67), channel_id=1, source_target_pairs={{7,0},{4,1},{5,2},{6,3},{3,4},{0,5},{1,6},{2,7},{15,8},{12,9},{13,... | collective-permute-start | bytes 294920 | tf_op jit(solution)/shard_map/ppermute | solution.py:30
  124.4 2.0 %shard_map.74 = f32[256,768]{1,0:T(8,128)S(1)} custom-call(s32[16]{0:T(128)S(1)} %get-tuple-element.72.place_ref, bf16[2,4,2,16,3072]{4,3,2,1,0:T(8,128)(2,1)S(1)} %pad_maximum_fusion.2.refs_0_.own_ref, bf16[2,4,2,16,3072]{4,3,2,1,0:T(8,128)(2,1)S(1)} %collective-permute-done.24.refs_1_.other_ref, bf16[768,3072]{1,0:T(8,128)(2,1)S(1)} %get-tuple-element.28.weight_ref), custom_call_target="tpu_custom_call" | custom-call | flops 1 | bytes 1 | tf_op jit(solution)/shard_map/pallas_call | solution.py:133
  126.5 0.7 collective-permute-start.29
  127.2 3.6 %collective-permute-start.31 = (bf16[64,768]{1,0:T(8,128)(2,1)S(1)}, bf16[64,768]{1,0:T(8,128)(2,1)S(1)}, u32[]{:S(2)}, u32[]{:S(2)}) collective-permute-start(bf16[64,768]{1,0:T(8,128)(2,1)S(1)} %get-tuple-element.62), channel_id=1, source_target_pairs={{2,0},{3,1},{0,2},{1,3},{6,4},{7,5},{4,6},{5,7},{10,8},{11,9},{8,1... | collective-permute-start | bytes 294920 | tf_op jit(solution)/shard_map/ppermute | solution.py:30
  130.8 3.7 %shard_map.73 = bf16[3072,768]{1,0:T(8,128)(2,1)} custom-call(bf16[2,4,2,16,3072]{4,3,2,1,0:T(8,128)(2,1)S(1)} %pad_maximum_fusion.2.refs_0_.own_ref, bf16[2,4,2,16,3072]{4,3,2,1,0:T(8,128)(2,1)S(1)} %collective-permute-done.24.refs_1_.other_ref, bf16[4,2,2,16,3072]{4,3,2,1,0:T(8,128)(2,1)S(1)} %pad_maximum_fusion.3.refs_2_.own_ref, ...), custom_call_target="tpu_custom_call" | custom-call | flops 1 | bytes 1 | tf_op jit(solution)/shard_map/pallas_call | solution.py:172
  134.5 3.6 %shard_map.72 = bf16[768,3072]{1,0:T(8,128)(2,1)} custom-call(bf16[2,4,2,16,3072]{4,3,2,1,0:T(8,128)(2,1)S(1)} %pad_maximum_fusion.2.refs_0_.own_ref, bf16[2,4,2,16,3072]{4,3,2,1,0:T(8,128)(2,1)S(1)} %collective-permute-done.24.refs_1_.other_ref, bf16[4,2,2,16,3072]{4,3,2,1,0:T(8,128)(2,1)S(1)} %pad_maximum_fusion.3.refs_2_.own_ref, ...), custom_call_target="tpu_custom_call" | custom-call | flops 1 | bytes 1 | tf_op jit(solution)/shard_map/pallas_call | solution.py:172
  138.1 0.7 fusion.28
  (65 shorter events, 6.6 us)
Async XLA Ops:
  1.6 8.2 %collective-permute-start = (bf16[2,64,768]{2,1,0:T(8,128)(2,1)S(1)}, bf16[2,64,768]{2,1,0:T(8,128)(2,1)S(1)}, u32[]{:S(2)}, u32[]{:S(2)}) collective-permute-start(bf16[2,64,768]{2,1,0:T(8,128)(2,1)S(1)} %pad_maximum_fusion.8), channel_id=1, source_target_pairs={{4,0},{5,1},{6,2},{7,3},{0,4},{1,5},{2,6},{3,7},{12,8},{13,9},{14,... | collective-permute-start | bytes 589832 | tf_op jit(solution)/shard_map/ppermute | solution.py:30
  3.2 10.7 %collective-permute-start.3 = (bf16[2,64,768]{2,1,0:T(8,128)(2,1)S(1)}, bf16[2,64,768]{2,1,0:T(8,128)(2,1)S(1)}, u32[]{:S(2)}, u32[]{:S(2)}) collective-permute-start(bf16[2,64,768]{2,1,0:T(8,128)(2,1)S(1)} %pad_maximum_fusion.8), channel_id=1, source_target_pairs={{3,0},{0,1},{1,2},{2,3},{7,4},{4,5},{5,6},{6,7},{11,8},{8,9},{9,10... | collective-permute-start | bytes 589832 | tf_op jit(solution)/shard_map/ppermute | solution.py:30
  5.2 13.8 %collective-permute-start.2 = (bf16[2,64,768]{2,1,0:T(8,128)(2,1)S(1)}, bf16[2,64,768]{2,1,0:T(8,128)(2,1)S(1)}, u32[]{:S(2)}, u32[]{:S(2)}) collective-permute-start(bf16[2,64,768]{2,1,0:T(8,128)(2,1)S(1)} %pad_maximum_fusion.8), channel_id=1, source_target_pairs={{2,0},{3,1},{0,2},{1,3},{6,4},{7,5},{4,6},{5,7},{10,8},{11,9},{8,1... | collective-permute-start | bytes 589832 | tf_op jit(solution)/shard_map/ppermute | solution.py:30
  8.7 10.2 %collective-permute-start.1 = (bf16[2,64,768]{2,1,0:T(8,128)(2,1)S(1)}, bf16[2,64,768]{2,1,0:T(8,128)(2,1)S(1)}, u32[]{:S(2)}, u32[]{:S(2)}) collective-permute-start(bf16[2,64,768]{2,1,0:T(8,128)(2,1)S(1)} %pad_maximum_fusion.8), channel_id=1, source_target_pairs={{1,0},{2,1},{3,2},{0,3},{5,4},{6,5},{7,6},{4,7},{9,8},{10,9},{11,1... | collective-permute-start | bytes 589832 | tf_op jit(solution)/shard_map/ppermute | solution.py:30
  9.8 10.9 %collective-permute-start.6 = (bf16[2,64,768]{2,1,0:T(8,128)(2,1)S(1)}, bf16[2,64,768]{2,1,0:T(8,128)(2,1)S(1)}, u32[]{:S(2)}, u32[]{:S(2)}) collective-permute-start(bf16[2,64,768]{2,1,0:T(8,128)(2,1)S(1)} %collective-permute-done), channel_id=1, source_target_pairs={{3,0},{0,1},{1,2},{2,3},{7,4},{4,5},{5,6},{6,7},{11,8},{8,9},{9,10... | collective-permute-start | bytes 589832 | tf_op jit(solution)/shard_map/ppermute | solution.py:30
  10.8 15.0 %collective-permute-start.5 = (bf16[2,64,768]{2,1,0:T(8,128)(2,1)S(1)}, bf16[2,64,768]{2,1,0:T(8,128)(2,1)S(1)}, u32[]{:S(2)}, u32[]{:S(2)}) collective-permute-start(bf16[2,64,768]{2,1,0:T(8,128)(2,1)S(1)} %collective-permute-done), channel_id=1, source_target_pairs={{2,0},{3,1},{0,2},{1,3},{6,4},{7,5},{4,6},{5,7},{10,8},{11,9},{8,1... | collective-permute-start | bytes 589832 | tf_op jit(solution)/shard_map/ppermute | solution.py:30
  13.9 11.9 %collective-permute-start.4 = (bf16[2,64,768]{2,1,0:T(8,128)(2,1)S(1)}, bf16[2,64,768]{2,1,0:T(8,128)(2,1)S(1)}, u32[]{:S(2)}, u32[]{:S(2)}) collective-permute-start(bf16[2,64,768]{2,1,0:T(8,128)(2,1)S(1)} %collective-permute-done), channel_id=1, source_target_pairs={{1,0},{2,1},{3,2},{0,3},{5,4},{6,5},{7,6},{4,7},{9,8},{10,9},{11,1... | collective-permute-start | bytes 589832 | tf_op jit(solution)/shard_map/ppermute | solution.py:30
  28.0 7.2 %collective-permute-start.8 = (bf16[128,3072]{1,0:T(8,128)(2,1)S(1)}, bf16[128,3072]{1,0:T(8,128)(2,1)S(1)}, u32[]{:S(2)}, u32[]{:S(2)}) collective-permute-start(bf16[128,3072]{1,0:T(8,128)(2,1)S(1)} %get-tuple-element.35), channel_id=1, source_target_pairs={{8,0},{0,8},{24,16},{16,24},{40,32},{32,40},{56,48},{48,56},{72,64... | collective-permute-start | bytes 2359304 | tf_op jit(solution)/shard_map/ppermute | solution.py:26
  30.0 5.4 %collective-permute-start.7 = (bf16[128,3072]{1,0:T(8,128)(2,1)S(1)}, bf16[128,3072]{1,0:T(8,128)(2,1)S(1)}, u32[]{:S(2)}, u32[]{:S(2)}) collective-permute-start(bf16[128,3072]{1,0:T(8,128)(2,1)S(1)} %get-tuple-element.32), channel_id=1, source_target_pairs={{8,0},{0,8},{24,16},{16,24},{40,32},{32,40},{56,48},{48,56},{72,64... | collective-permute-start | bytes 2359304 | tf_op jit(solution)/shard_map/ppermute | solution.py:26
  32.6 9.1 %collective-permute-start.13 = (bf16[128,3072]{1,0:T(8,128)(2,1)S(1)}, bf16[128,3072]{1,0:T(8,128)(2,1)S(1)}, u32[]{:S(2)}, u32[]{:S(2)}) collective-permute-start(bf16[128,3072]{1,0:T(8,128)(2,1)S(1)} %get-tuple-element.40), channel_id=1, source_target_pairs={{8,0},{0,8},{24,16},{16,24},{40,32},{32,40},{56,48},{48,56},{72,64... | collective-permute-start | bytes 2359304 | tf_op jit(solution)/shard_map/ppermute | solution.py:26
  34.6 7.2 %collective-permute-start.12 = (bf16[128,3072]{1,0:T(8,128)(2,1)S(1)}, bf16[128,3072]{1,0:T(8,128)(2,1)S(1)}, u32[]{:S(2)}, u32[]{:S(2)}) collective-permute-start(bf16[128,3072]{1,0:T(8,128)(2,1)S(1)} %get-tuple-element.38), channel_id=1, source_target_pairs={{8,0},{0,8},{24,16},{16,24},{40,32},{32,40},{56,48},{48,56},{72,64... | collective-permute-start | bytes 2359304 | tf_op jit(solution)/shard_map/ppermute | solution.py:26
  35.7 12.4 %collective-permute-start.9 = (bf16[2,2,16,3072]{3,2,0,1:T(8,128)(2,1)S(1)}, bf16[2,2,16,3072]{3,2,0,1:T(8,128)(2,1)S(1)}, u32[]{:S(2)}, u32[]{:S(2)}) collective-permute-start(bf16[2,2,16,3072]{3,2,0,1:T(8,128)(2,1)S(1)} %get-tuple-element.51), channel_id=1, source_target_pairs={{96,0},{104,8},{112,16},{120,24},{0,32},{8,40},{16,48},{24,56},{32... | collective-permute-start | bytes 1179656 | tf_op jit(solution)/shard_map/ppermute | solution.py:26
  37.4 20.3 %collective-permute-start.11 = (bf16[2,2,16,3072]{3,2,0,1:T(8,128)(2,1)S(1)}, bf16[2,2,16,3072]{3,2,0,1:T(8,128)(2,1)S(1)}, u32[]{:S(2)}, u32[]{:S(2)}) collective-permute-start(bf16[2,2,16,3072]{3,2,0,1:T(8,128)(2,1)S(1)} %get-tuple-element.52), channel_id=1, source_target_pairs={{64,0},{72,8},{80,16},{88,24},{96,32},{104,40},{112,48},{120,56},{... | collective-permute-start | bytes 1179656 | tf_op jit(solution)/shard_map/ppermute | solution.py:26
  40.3 17.4 %collective-permute-start.10 = (bf16[2,2,16,3072]{3,2,0,1:T(8,128)(2,1)S(1)}, bf16[2,2,16,3072]{3,2,0,1:T(8,128)(2,1)S(1)}, u32[]{:S(2)}, u32[]{:S(2)}) collective-permute-start(bf16[2,2,16,3072]{3,2,0,1:T(8,128)(2,1)S(1)} %get-tuple-element.53), channel_id=1, source_target_pairs={{32,0},{40,8},{48,16},{56,24},{64,32},{72,40},{80,48},{88,56},{96,... | collective-permute-start | bytes 1179656 | tf_op jit(solution)/shard_map/ppermute | solution.py:26
  42.5 20.2 %collective-permute-start.14 = (bf16[2,4,16,3072]{3,2,0,1:T(8,128)(2,1)S(1)}, bf16[2,4,16,3072]{3,2,0,1:T(8,128)(2,1)S(1)}, u32[]{:S(2)}, u32[]{:S(2)}) collective-permute-start(bf16[2,4,16,3072]{3,2,0,1:T(8,128)(2,1)S(1)} %fusion.1), channel_id=1, source_target_pairs={{16,0},{24,8},{0,16},{8,24},{48,32},{56,40},{32,48},{40,56},{80,64... | collective-permute-start | bytes 2359304 | tf_op jit(solution)/shard_map/ppermute | solution.py:26
  62.9 7.3 %collective-permute-start.15 = (bf16[2,16,3072]{2,1,0:T(8,128)(2,1)S(1)}, bf16[2,16,3072]{2,1,0:T(8,128)(2,1)S(1)}, u32[]{:S(2)}, u32[]{:S(2)}) collective-permute-start(bf16[2,16,3072]{2,1,0:T(8,128)(2,1)S(1)} %fusion.21), channel_id=1, source_target_pairs={{16,0},{24,8},{0,16},{8,24},{48,32},{56,40},{32,48},{40,56},{80,64... | collective-permute-start | bytes 589832 | tf_op jit(solution)/shard_map/ppermute | solution.py:26
  65.9 10.3 %collective-permute-start.16 = (bf16[2,16,3072]{2,1,0:T(8,128)(2,1)S(1)}, bf16[2,16,3072]{2,1,0:T(8,128)(2,1)S(1)}, u32[]{:S(2)}, u32[]{:S(2)}) collective-permute-start(bf16[2,16,3072]{2,1,0:T(8,128)(2,1)S(1)} %get-tuple-element.54), channel_id=1, source_target_pairs={{96,0},{104,8},{112,16},{120,24},{0,32},{8,40},{16,48},{24,56},{32... | collective-permute-start | bytes 589832 | tf_op jit(solution)/shard_map/ppermute | solution.py:26
  66.6 9.5 %collective-permute-start.18 = (bf16[2,16,3072]{2,1,0:T(8,128)(2,1)S(1)}, bf16[2,16,3072]{2,1,0:T(8,128)(2,1)S(1)}, u32[]{:S(2)}, u32[]{:S(2)}) collective-permute-start(bf16[2,16,3072]{2,1,0:T(8,128)(2,1)S(1)} %get-tuple-element.55), channel_id=1, source_target_pairs={{64,0},{72,8},{80,16},{88,24},{96,32},{104,40},{112,48},{120,56},{... | collective-permute-start | bytes 589832 | tf_op jit(solution)/shard_map/ppermute | solution.py:26
  67.7 9.1 %collective-permute-start.17 = (bf16[2,16,3072]{2,1,0:T(8,128)(2,1)S(1)}, bf16[2,16,3072]{2,1,0:T(8,128)(2,1)S(1)}, u32[]{:S(2)}, u32[]{:S(2)}) collective-permute-start(bf16[2,16,3072]{2,1,0:T(8,128)(2,1)S(1)} %get-tuple-element.56), channel_id=1, source_target_pairs={{32,0},{40,8},{48,16},{56,24},{64,32},{72,40},{80,48},{88,56},{96,... | collective-permute-start | bytes 589832 | tf_op jit(solution)/shard_map/ppermute | solution.py:26
  77.1 7.3 %collective-permute-start.22 = (bf16[2,16,3072]{2,1,0:T(8,128)(2,1)S(1)}, bf16[2,16,3072]{2,1,0:T(8,128)(2,1)S(1)}, u32[]{:S(2)}, u32[]{:S(2)}) collective-permute-start(bf16[2,16,3072]{2,1,0:T(8,128)(2,1)S(1)} %pad_maximum_fusion.10), channel_id=1, source_target_pairs={{16,0},{24,8},{0,16},{8,24},{48,32},{56,40},{32,48},{40,56},{80,64... | collective-permute-start | bytes 589832 | tf_op jit(solution)/shard_map/ppermute | solution.py:26
  78.0 8.8 %collective-permute-start.21 = (bf16[2,16,3072]{2,1,0:T(8,128)(2,1)S(1)}, bf16[2,16,3072]{2,1,0:T(8,128)(2,1)S(1)}, u32[]{:S(2)}, u32[]{:S(2)}) collective-permute-start(bf16[2,16,3072]{2,1,0:T(8,128)(2,1)S(1)} %pad_maximum_fusion.9), channel_id=1, source_target_pairs={{96,0},{104,8},{112,16},{120,24},{0,32},{8,40},{16,48},{24,56},{32... | collective-permute-start | bytes 589832 | tf_op jit(solution)/shard_map/ppermute | solution.py:26
  78.4 11.2 %collective-permute-start.20 = (bf16[2,16,3072]{2,1,0:T(8,128)(2,1)S(1)}, bf16[2,16,3072]{2,1,0:T(8,128)(2,1)S(1)}, u32[]{:S(2)}, u32[]{:S(2)}) collective-permute-start(bf16[2,16,3072]{2,1,0:T(8,128)(2,1)S(1)} %pad_maximum_fusion.9), channel_id=1, source_target_pairs={{64,0},{72,8},{80,16},{88,24},{96,32},{104,40},{112,48},{120,56},{... | collective-permute-start | bytes 589832 | tf_op jit(solution)/shard_map/ppermute | solution.py:26
  82.0 7.6 %collective-permute-start.19 = (bf16[2,16,3072]{2,1,0:T(8,128)(2,1)S(1)}, bf16[2,16,3072]{2,1,0:T(8,128)(2,1)S(1)}, u32[]{:S(2)}, u32[]{:S(2)}) collective-permute-start(bf16[2,16,3072]{2,1,0:T(8,128)(2,1)S(1)} %pad_maximum_fusion.9), channel_id=1, source_target_pairs={{32,0},{40,8},{48,16},{56,24},{64,32},{72,40},{80,48},{88,56},{96,... | collective-permute-start | bytes 589832 | tf_op jit(solution)/shard_map/ppermute | solution.py:26
  89.7 22.6 %collective-permute-start.23 = (bf16[4,2,16,3072]{3,2,1,0:T(8,128)(2,1)S(1)}, bf16[4,2,16,3072]{3,2,1,0:T(8,128)(2,1)S(1)}, u32[]{:S(2)}, u32[]{:S(2)}) collective-permute-start(bf16[4,2,16,3072]{3,2,1,0:T(8,128)(2,1)S(1)} %pad_maximum_fusion.6), channel_id=1, source_target_pairs={{16,0},{24,8},{0,16},{8,24},{48,32},{56,40},{32,48},{40,56},{80,64... | collective-permute-start | bytes 2359304 | tf_op jit(solution)/shard_map/ppermute | solution.py:26
  92.5 11.2 %collective-permute-start.27 = (bf16[2,2,16,3072]{3,2,1,0:T(8,128)(2,1)S(1)}, bf16[2,2,16,3072]{3,2,1,0:T(8,128)(2,1)S(1)}, u32[]{:S(2)}, u32[]{:S(2)}) collective-permute-start(bf16[2,2,16,3072]{3,2,1,0:T(8,128)(2,1)S(1)} %pad_maximum_fusion.7), channel_id=1, source_target_pairs={{96,0},{104,8},{112,16},{120,24},{0,32},{8,40},{16,48},{24,56},{32... | collective-permute-start | bytes 1179656 | tf_op jit(solution)/shard_map/ppermute | solution.py:26
  92.5 19.5 %collective-permute-start.26 = (bf16[2,2,16,3072]{3,2,1,0:T(8,128)(2,1)S(1)}, bf16[2,2,16,3072]{3,2,1,0:T(8,128)(2,1)S(1)}, u32[]{:S(2)}, u32[]{:S(2)}) collective-permute-start(bf16[2,2,16,3072]{3,2,1,0:T(8,128)(2,1)S(1)} %pad_maximum_fusion.7), channel_id=1, source_target_pairs={{64,0},{72,8},{80,16},{88,24},{96,32},{104,40},{112,48},{120,56},{... | collective-permute-start | bytes 1179656 | tf_op jit(solution)/shard_map/ppermute | solution.py:26
  96.0 15.9 %collective-permute-start.25 = (bf16[2,2,16,3072]{3,2,1,0:T(8,128)(2,1)S(1)}, bf16[2,2,16,3072]{3,2,1,0:T(8,128)(2,1)S(1)}, u32[]{:S(2)}, u32[]{:S(2)}) collective-permute-start(bf16[2,2,16,3072]{3,2,1,0:T(8,128)(2,1)S(1)} %pad_maximum_fusion.7), channel_id=1, source_target_pairs={{32,0},{40,8},{48,16},{56,24},{64,32},{72,40},{80,48},{88,56},{96,... | collective-permute-start | bytes 1179656 | tf_op jit(solution)/shard_map/ppermute | solution.py:26
  112.2 3.5 %collective-permute-start.28 = (bf16[4,2,2,16,3072]{4,3,2,1,0:T(8,128)(2,1)S(1)}, bf16[4,2,2,16,3072]{4,3,2,1,0:T(8,128)(2,1)S(1)}, u32[]{:S(2)}, u32[]{:S(2)}) collective-permute-start(bf16[4,2,2,16,3072]{4,3,2,1,0:T(8,128)(2,1)S(1)} %pad_maximum_fusion.3.refs_2_.own_ref), channel_id=1, source_target_pairs={{8,0},{0,8},{24,16},{16,24},{40,32},{32,40},{56,48},{48,56},{72,64... | collective-permute-start | bytes 4718600 | tf_op jit(solution)/shard_map/ppermute | solution.py:26
  112.4 12.0 %collective-permute-start.24 = (bf16[2,4,2,16,3072]{4,3,2,1,0:T(8,128)(2,1)S(1)}, bf16[2,4,2,16,3072]{4,3,2,1,0:T(8,128)(2,1)S(1)}, u32[]{:S(2)}, u32[]{:S(2)}) collective-permute-start(bf16[2,4,2,16,3072]{4,3,2,1,0:T(8,128)(2,1)S(1)} %pad_maximum_fusion.2.refs_0_.own_ref), channel_id=1, source_target_pairs={{8,0},{0,8},{24,16},{16,24},{40,32},{32,40},{56,48},{48,56},{72,64... | collective-permute-start | bytes 4718600 | tf_op jit(solution)/shard_map/ppermute | solution.py:26
  117.7 9.5 %collective-permute-start.32 = (bf16[64,768]{1,0:T(8,128)(2,1)S(1)}, bf16[64,768]{1,0:T(8,128)(2,1)S(1)}, u32[]{:S(2)}, u32[]{:S(2)}) collective-permute-start(bf16[64,768]{1,0:T(8,128)(2,1)S(1)} %get-tuple-element.64), channel_id=1, source_target_pairs={{4,0},{5,1},{6,2},{7,3},{0,4},{1,5},{2,6},{3,7},{12,8},{13,9},{14,... | collective-permute-start | bytes 294920 | tf_op jit(solution)/shard_map/ppermute | solution.py:30
  118.0 12.8 %collective-permute-start.35 = (bf16[64,768]{1,0:T(8,128)(2,1)S(1)}, bf16[64,768]{1,0:T(8,128)(2,1)S(1)}, u32[]{:S(2)}, u32[]{:S(2)}) collective-permute-start(bf16[64,768]{1,0:T(8,128)(2,1)S(1)} %get-tuple-element.65), channel_id=1, source_target_pairs={{6,0},{7,1},{4,2},{5,3},{2,4},{3,5},{0,6},{1,7},{14,8},{15,9},{12,... | collective-permute-start | bytes 294920 | tf_op jit(solution)/shard_map/ppermute | solution.py:30
  121.5 16.6 %collective-permute-start.34 = (bf16[64,768]{1,0:T(8,128)(2,1)S(1)}, bf16[64,768]{1,0:T(8,128)(2,1)S(1)}, u32[]{:S(2)}, u32[]{:S(2)}) collective-permute-start(bf16[64,768]{1,0:T(8,128)(2,1)S(1)} %get-tuple-element.66), channel_id=1, source_target_pairs={{5,0},{6,1},{7,2},{4,3},{1,4},{2,5},{3,6},{0,7},{13,8},{14,9},{15,... | collective-permute-start | bytes 294920 | tf_op jit(solution)/shard_map/ppermute | solution.py:30
  122.7 15.4 %collective-permute-start.33 = (bf16[64,768]{1,0:T(8,128)(2,1)S(1)}, bf16[64,768]{1,0:T(8,128)(2,1)S(1)}, u32[]{:S(2)}, u32[]{:S(2)}) collective-permute-start(bf16[64,768]{1,0:T(8,128)(2,1)S(1)} %get-tuple-element.67), channel_id=1, source_target_pairs={{7,0},{4,1},{5,2},{6,3},{3,4},{0,5},{1,6},{2,7},{15,8},{12,9},{13,... | collective-permute-start | bytes 294920 | tf_op jit(solution)/shard_map/ppermute | solution.py:30
  126.5 11.6 %collective-permute-start.29 = (bf16[64,768]{1,0:T(8,128)(2,1)S(1)}, bf16[64,768]{1,0:T(8,128)(2,1)S(1)}, u32[]{:S(2)}, u32[]{:S(2)}) collective-permute-start(bf16[64,768]{1,0:T(8,128)(2,1)S(1)} %get-tuple-element.61), channel_id=1, source_target_pairs={{3,0},{0,1},{1,2},{2,3},{7,4},{4,5},{5,6},{6,7},{11,8},{8,9},{9,10... | collective-permute-start | bytes 294920 | tf_op jit(solution)/shard_map/ppermute | solution.py:30
  127.2 10.9 %collective-permute-start.31 = (bf16[64,768]{1,0:T(8,128)(2,1)S(1)}, bf16[64,768]{1,0:T(8,128)(2,1)S(1)}, u32[]{:S(2)}, u32[]{:S(2)}) collective-permute-start(bf16[64,768]{1,0:T(8,128)(2,1)S(1)} %get-tuple-element.62), channel_id=1, source_target_pairs={{2,0},{3,1},{0,2},{1,3},{6,4},{7,5},{4,6},{5,7},{10,8},{11,9},{8,1... | collective-permute-start | bytes 294920 | tf_op jit(solution)/shard_map/ppermute | solution.py:30
  130.8 7.3 %collective-permute-start.30 = (bf16[64,768]{1,0:T(8,128)(2,1)S(1)}, bf16[64,768]{1,0:T(8,128)(2,1)S(1)}, u32[]{:S(2)}, u32[]{:S(2)}) collective-permute-start(bf16[64,768]{1,0:T(8,128)(2,1)S(1)} %get-tuple-element.63), channel_id=1, source_target_pairs={{1,0},{2,1},{3,2},{0,3},{5,4},{6,5},{7,6},{4,7},{9,8},{10,9},{11,1... | collective-permute-start | bytes 294920 | tf_op jit(solution)/shard_map/ppermute | solution.py:30

commit v3 on v2

--- a/solution.py
+++ b/solution.py
@@ -86,34 +86,37 @@
     )(pltpu.with_memory_space_constraint(first, pltpu.HBM), pltpu.with_memory_space_constraint(second, pltpu.HBM))
 
 
-def project(tokens, weight, place, hidden_dim):
-    rows, k = tokens.shape
-    hidden = weight.shape[hidden_dim]
-    half = rows // 2
-
-    def body(place_ref, tokens_ref, weight_ref, keep_ref, send_ref, placed_ref):
-        for b in range(rows // 16):
-            start = pl.multiple_of(place_ref[b] * 16, 16)
-            placed_ref[pl.ds(16 * b, 16), :] = tokens_ref[pl.ds(start, 16), :]
-        for i in range(hidden // TILE):
-            part = pl.ds(i * TILE, TILE)
-            weight_part = weight_ref[:, part] if hidden_dim == 1 else weight_ref[part, :]
-            total = contract(placed_ref[...], weight_part, 1, 1 - hidden_dim)
-            keep_ref[:, part] = total[:half]
-            send_ref[:, part] = bf16(total[half:])
-
-    return pl.pallas_call(
-        body,
-        in_specs=[SMEM, VMEM, VMEM],
-        out_specs=[VMEM, VMEM, VMEM],
+def project(tokens, weights, place):
+    z, _, n, k = tokens.shape
+    rows = z * n
+    half, hidden = rows // 2, weights[0].shape[1]
+
+    def body(place_ref, tokens_ref, in_ref, out_ref, keep_ref, send_ref, *placed_refs):
+        for m, (weight_ref, placed_ref) in enumerate(zip((in_ref, out_ref), placed_refs)):
+            for b in range(rows // 16):
+                at = place_ref[b]
+                start = pl.multiple_of(lax.rem(at, n // 16) * 16, 16)
+                placed_ref[pl.ds(16 * b, 16), :] = tokens_ref[lax.div(at, n // 16), m, pl.ds(start, 16), :]
+            for i in range(hidden // TILE):
+                part = pl.ds(i * TILE, TILE)
+                weight_part = weight_ref[part, :] if m else weight_ref[:, part]
+                total = contract(placed_ref[...], weight_part, 1, m)
+                keep_ref[m, :, part] = total[:half]
+                send_ref[m, :, part] = bf16(total[half:])
+
+    return pl.pallas_call(
+        body,
+        in_specs=[SMEM, VMEM, VMEM, VMEM],
+        out_specs=[VMEM] * 4,
         out_shape=[
-            pltpu.VMEM((half, hidden), jnp.float32),
-            pltpu.VMEM((half, hidden), jnp.bfloat16),
+            pltpu.VMEM((2, half, hidden), jnp.float32),
+            pltpu.VMEM((2, half, hidden), jnp.bfloat16),
+            pltpu.VMEM((rows, k), jnp.bfloat16),
             pltpu.VMEM((rows, k), jnp.bfloat16),
         ],
         compiler_params=params(16),
         cost_estimate=COST,
-    )(place, tokens, weight)
+    )(place, tokens, *weights)
 
 
 def back_project(own, other, weight, place):
@@ -225,14 +228,6 @@
         dx, dy = ((b // 4) % 2, b % 4) if x_outer else (b % 2, (b // 2) % 4)
         return (((y + dy) % 4) * 2 + (c + dc) % 2) * 2 + (x + dx) % 2
 
-    def pairs_of(tokens, place, weights):
-        pairs, placed = [], []
-        for m in range(2):
-            keep, send, rel = project(tokens[:, m].reshape(4 * n, k), weights[m], place, 1 - m)
-            pairs.append(keep + f32(from_row(send, 0, 0, 1)))
-            placed.append(rel)
-        return jnp.stack(pairs), placed
-
     def made_of(sums):
         pre, act_grad = sums
         return jnp.stack([bf16(gelu_value(pre)), bf16(act_grad * gelu_slope(pre))])
@@ -241,18 +236,23 @@
     near = from_col(own, 1, 0)
     weights = loaded(tied(weight_in, near), weight_out)
     tokens_a = jnp.stack([tied(own, weights[0])] + [from_col(own, 0, dz) for dz in (1, 2, 3)])
-    tokens_a, tokens_b = lax.optimization_barrier((tokens_a, gather_z(near)))
     place_a, place_b = place_of(True), place_of(False)
-    pair_a, placed_a = pairs_of(tokens_a, place_a, weights)
-    pair_b, placed_b = pairs_of(tokens_b, place_b, weights)
+    keep_a, send_a, *placed_a = project(tokens_a, weights, place_a)
+    send_a, tokens_b = lax.optimization_barrier((send_a, gather_z(near)))
+    pair_a = keep_a + f32(from_row(send_a, 0, 0, 1))
+    keep_b, send_b, *placed_b = project(tokens_b, weights, place_b)
+    pair_b = keep_b + f32(from_row(send_b, 0, 0, 1))
     pair_a, pair_b = pair_a.reshape(2, 2, 4, 16, -1), pair_b.reshape(2, 4, 2, 16, -1)
 
     one_a, one_b = sum_y(lambda dy: pair_a[:, :, dy]), sum_x(lambda dx: pair_b[:, :, dx])
     one_a, one_b = lax.optimization_barrier((one_a, one_b))
-    sums_a, sums_b = sum_x(lambda dx: one_a[:, dx]), sum_y(lambda dy: one_b[:, dy])
+    sums_b = sum_y(lambda dy: one_b[:, dy])
+    sums_a = one_a[:, 0] + f32(tied(from_row(bf16(one_a[:, 1]), 0, 1, 0), sums_b))
     made_a, made_b = made_of(sums_a), made_of(sums_b)
     made_a, made_b = lax.optimization_barrier((made_a, made_b))
-    part_a, part_b = lax.optimization_barrier((gather_y(made_a), gather_x(made_b)))
+    part_a = gather_y(made_a)
+    part_b = jnp.stack([made_b, tied(from_row(made_b, 0, 1, 0), part_a)])
+    part_a, part_b = lax.optimization_barrier((part_a, part_b))
     half_a, half_b = gather_x(part_a), gather_y(part_b)
     other_b = from_row(half_b, 0, 0, 1)
     back_b = back_project(half_b, other_b, weights[0], place_b).reshape(4, n, k)

time: 139 us -> 129 us (0.928)
  waiting for transfers between devices: 57.4 us -> 47.4 us
  starting transfers between devices: 52.7 us -> 54.8 us
  Pallas kernels: 22.8 us -> 21.3 us
    ppermute x22 -> x20, waiting for transfers between devices: 50.7 us -> 43.8 us  [from_row(): lax.ppermute(a, 'row', [(at_row(y + dy, x + dx, c + dc), at_row(y, x, c))...]
    ppermute x14, waiting for transfers between devices: 6.73 us -> 3.56 us  [from_col(): lax.ppermute(a, 'col', [(at_col(x + dx, z + dz), at_col(x, z)) for x, z i...]
    ppermute x22 -> x20, starting transfers between devices: 28.2 us -> 30.8 us  [from_row(): lax.ppermute(a, 'row', [(at_row(y + dy, x + dx, c + dc), at_row(y, x, c))...]
    pallas_call x4 -> x2, Pallas kernels: 7.85 us -> 6.33 us  [project(): pl.pallas_call(body, in_specs=[SMEM, VMEM, VMEM, VMEM], out_specs=[VMEM]...]
  transfers between devices with their start and end apart: 36 -> 34, of which waited for: 14 -> 13; matrix products, arithmetic and copies ran while one was open for 2% -> 2% of each run, Pallas kernels for 15% -> 17%
where the time goes in v3:
time: 129 us
  starting transfers between devices  54.8 us (42%)
  waiting for transfers between devices  47.4 us (37%)
  Pallas kernels  21.3 us (17%)
  other arithmetic  4.51 us (3%)
    ppermute x20, waiting for transfers between devices, from_row(): lax.ppermute(a, 'row', [(at_row(y + dy, x + dx, c + dc), at_row(y, x, c))...  43.8 us
    ppermute x20, starting transfers between devices, from_row(): lax.ppermute(a, 'row', [(at_row(y + dy, x + dx, c + dc), at_row(y, x, c))...  30.8 us
    ppermute x14, starting transfers between devices, from_col(): lax.ppermute(a, 'col', [(at_col(x + dx, z + dz), at_col(x, z)) for x, z i...  24 us
    pallas_call x2, Pallas kernels, weight_grad(): pl.pallas_call(body, in_specs=[VMEM] * (3 * chunks), out_specs=pl.BlockSp...  7.27 us
    pallas_call x2, Pallas kernels, project(): pl.pallas_call(body, in_specs=[SMEM, VMEM, VMEM, VMEM], out_specs=[VMEM]...  6.33 us
    pallas_call x2, Pallas kernels, back_project(): pl.pallas_call(body, in_specs=[SMEM, VMEM, VMEM, VMEM], out_specs=VMEM, o...  3.94 us
    pallas_call x1, Pallas kernels, loaded(): pl.pallas_call(body, in_specs=[pl.BlockSpec(memory_space=pl.ANY)] * 2, ou...  3.79 us
    ppermute x14, waiting for transfers between devices, from_col(): lax.ppermute(a, 'col', [(at_col(x + dx, z + dz), at_col(x, z)) for x, z i...  3.56 us
  transfers between devices with their start and end apart: 34, of which 13 were waited for; matrix products, arithmetic and copies ran while one was open for 2% of the time, Pallas kernels for 17%

profile of v3, /device:TPU:0, one launch (start us, length us, event | category | flops | bytes accessed | tf_op | source)
XLA Modules:
  0.0 129.3 jit_solution(3028016194569703789)
XLA Ops:
  0.6 1.0 pad_maximum_fusion.6
  1.6 1.7 %collective-permute-start = (bf16[2,64,768]{2,1,0:T(8,128)(2,1)S(1)}, bf16[2,64,768]{2,1,0:T(8,128)(2,1)S(1)}, u32[]{:S(2)}, u32[]{:S(2)}) collective-permute-start(bf16[2,64,768]{2,1,0:T(8,128)(2,1)S(1)} %pad_maximum_fusion.6), channel_id=1, source_target_pairs={{4,0},{5,1},{6,2},{7,3},{0,4},{1,5},{2,6},{3,7},{12,8},{13,9},{14,... | collective-permute-start | bytes 589832 | tf_op jit(solution)/shard_map/ppermute | solution.py:30
  3.2 1.9 %collective-permute-start.3 = (bf16[2,64,768]{2,1,0:T(8,128)(2,1)S(1)}, bf16[2,64,768]{2,1,0:T(8,128)(2,1)S(1)}, u32[]{:S(2)}, u32[]{:S(2)}) collective-permute-start(bf16[2,64,768]{2,1,0:T(8,128)(2,1)S(1)} %pad_maximum_fusion.6), channel_id=1, source_target_pairs={{3,0},{0,1},{1,2},{2,3},{7,4},{4,5},{5,6},{6,7},{11,8},{8,9},{9,10... | collective-permute-start | bytes 589832 | tf_op jit(solution)/shard_map/ppermute | solution.py:30
  5.2 3.6 %collective-permute-start.2 = (bf16[2,64,768]{2,1,0:T(8,128)(2,1)S(1)}, bf16[2,64,768]{2,1,0:T(8,128)(2,1)S(1)}, u32[]{:S(2)}, u32[]{:S(2)}) collective-permute-start(bf16[2,64,768]{2,1,0:T(8,128)(2,1)S(1)} %pad_maximum_fusion.6), channel_id=1, source_target_pairs={{2,0},{3,1},{0,2},{1,3},{6,4},{7,5},{4,6},{5,7},{10,8},{11,9},{8,1... | collective-permute-start | bytes 589832 | tf_op jit(solution)/shard_map/ppermute | solution.py:30
  8.7 1.0 collective-permute-start.1
  9.8 1.0 collective-permute-start.6
  10.8 3.1 %collective-permute-start.5 = (bf16[2,64,768]{2,1,0:T(8,128)(2,1)S(1)}, bf16[2,64,768]{2,1,0:T(8,128)(2,1)S(1)}, u32[]{:S(2)}, u32[]{:S(2)}) collective-permute-start(bf16[2,64,768]{2,1,0:T(8,128)(2,1)S(1)} %collective-permute-done), channel_id=1, source_target_pairs={{2,0},{3,1},{0,2},{1,3},{6,4},{7,5},{4,6},{5,7},{10,8},{11,9},{8,1... | collective-permute-start | bytes 589832 | tf_op jit(solution)/shard_map/ppermute | solution.py:30
  13.9 1.2 collective-permute-start.4
  15.1 3.8 %shard_map.67 = (bf16[768,3072]{1,0:T(8,128)(2,1)S(1)}, bf16[3072,768]{1,0:T(8,128)(2,1)S(1)}) custom-call(bf16[768,3072]{1,0:T(8,128)(2,1)} %first_ref, bf16[3072,768]{1,0:T(8,128)(2,1)} %second_ref.1), custom_call_target="tpu_custom_call" | custom-call | flops 1 | bytes 1 | tf_op jit(solution)/shard_map/pallas_call | solution.py:78
  19.1 3.2 %shard_map.68 = (f32[2,128,3072]{2,1,0:T(8,128)S(1)}, bf16[2,128,3072]{2,1,0:T(8,128)(2,1)S(1)}, bf16[256,768]{1,0:T(8,128)(2,1)S(1)}, bf16[256,768]{1,0:T(8,128)(2,1)S(1)}) custom-call(s32[16]{0:T(128)S(1)} %fusion.29.place_ref, bf16[4,2,64,768]{3,2,1,0:T(8,128)(2,1)S(1)} %pad_maximum_fusion.2.tokens_ref, ...), custom_call_target="tpu_custom_call" | custom-call | flops 1 | bytes 1 | tf_op jit(solution)/shard_map/pallas_call | solution.py:107
  22.2 3.5 %collective-permute-done.5 = bf16[2,64,768]{2,1,0:T(8,128)(2,1)S(1)} collective-permute-done((bf16[2,64,768]{2,1,0:T(8,128)(2,1)S(1)}, bf16[2,64,768]{2,1,0:T(8,128)(2,1)S(1)}, u32[]{:S(2)}, u32[]{:S(2)}) %collective-permute-start.5) | collective-permute-done | bytes 196640 | tf_op jit(solution)/shard_map/ppermute | solution.py:30
  26.0 3.2 %shard_map.69 = (f32[2,128,3072]{2,1,0:T(8,128)S(1)}, bf16[2,128,3072]{2,1,0:T(8,128)(2,1)S(1)}, bf16[256,768]{1,0:T(8,128)(2,1)S(1)}, bf16[256,768]{1,0:T(8,128)(2,1)S(1)}) custom-call(s32[16]{0:T(128)S(1)} %fusion.31.place_ref, bf16[4,2,64,768]{3,2,1,0:T(8,128)(2,1)S(1)} %pad_maximum_fusion.3.tokens_ref, ...), custom_call_target="tpu_custom_call" | custom-call | flops 1 | bytes 1 | tf_op jit(solution)/shard_map/pallas_call | solution.py:107
  29.2 0.6 collective-permute-start.11
  30.4 3.3 %collective-permute-start.10 = (bf16[2,2,16,3072]{3,2,0,1:T(8,128)(2,1)S(1)}, bf16[2,2,16,3072]{3,2,0,1:T(8,128)(2,1)S(1)}, u32[]{:S(2)}, u32[]{:S(2)}) collective-permute-start(bf16[2,2,16,3072]{3,2,0,1:T(8,128)(2,1)S(1)} %get-tuple-element.48), channel_id=1, source_target_pairs={{64,0},{72,8},{80,16},{88,24},{96,32},{104,40},{112,48},{120,56},{... | collective-permute-start | bytes 1179656 | tf_op jit(solution)/shard_map/ppermute | solution.py:26
  33.7 1.1 collective-permute-start.9
  34.8 1.0 collective-permute-start.8
  36.4 2.8 %collective-permute-start.12 = (bf16[2,4,16,3072]{3,2,0,1:T(8,128)(2,1)S(1)}, bf16[2,4,16,3072]{3,2,0,1:T(8,128)(2,1)S(1)}, u32[]{:S(2)}, u32[]{:S(2)}) collective-permute-start(bf16[2,4,16,3072]{3,2,0,1:T(8,128)(2,1)S(1)} %fusion.1), channel_id=1, source_target_pairs={{16,0},{24,8},{0,16},{8,24},{48,32},{56,40},{32,48},{40,56},{80,64... | collective-permute-start | bytes 2359304 | tf_op jit(solution)/shard_map/ppermute | solution.py:26
  39.2 4.8 %collective-permute-done.10 = bf16[2,2,16,3072]{3,2,0,1:T(8,128)(2,1)S(1)} collective-permute-done((bf16[2,2,16,3072]{3,2,0,1:T(8,128)(2,1)S(1)}, bf16[2,2,16,3072]{3,2,0,1:T(8,128)(2,1)S(1)}, u32[]{:S(2)}, u32[]{:S(2)}) %collective-permute-start.10) | collective-permute-done | bytes 393248 | tf_op jit(solution)/shard_map/ppermute | solution.py:26
  44.0 7.8 %collective-permute-done.9 = bf16[2,2,16,3072]{3,2,0,1:T(8,128)(2,1)S(1)} collective-permute-done((bf16[2,2,16,3072]{3,2,0,1:T(8,128)(2,1)S(1)}, bf16[2,2,16,3072]{3,2,0,1:T(8,128)(2,1)S(1)}, u32[]{:S(2)}, u32[]{:S(2)}) %collective-permute-start.9) | collective-permute-done | bytes 393248 | tf_op jit(solution)/shard_map/ppermute | solution.py:26
  52.0 4.6 %collective-permute-done.12 = bf16[2,4,16,3072]{3,2,0,1:T(8,128)(2,1)S(1)} collective-permute-done((bf16[2,4,16,3072]{3,2,0,1:T(8,128)(2,1)S(1)}, bf16[2,4,16,3072]{3,2,0,1:T(8,128)(2,1)S(1)}, u32[]{:S(2)}, u32[]{:S(2)}) %collective-permute-start.12) | collective-permute-done | bytes 786464 | tf_op jit(solution)/shard_map/ppermute | solution.py:26
  57.0 1.5 %collective-permute-start.16 = (bf16[2,16,3072]{2,1,0:T(8,128)(2,1)S(1)}, bf16[2,16,3072]{2,1,0:T(8,128)(2,1)S(1)}, u32[]{:S(2)}, u32[]{:S(2)}) collective-permute-start(bf16[2,16,3072]{2,1,0:T(8,128)(2,1)S(1)} %get-tuple-element.51), channel_id=1, source_target_pairs={{64,0},{72,8},{80,16},{88,24},{96,32},{104,40},{112,48},{120,56},{... | collective-permute-start | bytes 589832 | tf_op jit(solution)/shard_map/ppermute | solution.py:26
  58.5 1.9 %collective-permute-start.15 = (bf16[2,16,3072]{2,1,0:T(8,128)(2,1)S(1)}, bf16[2,16,3072]{2,1,0:T(8,128)(2,1)S(1)}, u32[]{:S(2)}, u32[]{:S(2)}) collective-permute-start(bf16[2,16,3072]{2,1,0:T(8,128)(2,1)S(1)} %get-tuple-element.52), channel_id=1, source_target_pairs={{32,0},{40,8},{48,16},{56,24},{64,32},{72,40},{80,48},{88,56},{96,... | collective-permute-start | bytes 589832 | tf_op jit(solution)/shard_map/ppermute | solution.py:26
  60.5 2.8 %collective-permute-start.13 = (bf16[2,16,3072]{2,1,0:T(8,128)(2,1)S(1)}, bf16[2,16,3072]{2,1,0:T(8,128)(2,1)S(1)}, u32[]{:S(2)}, u32[]{:S(2)}) collective-permute-start(bf16[2,16,3072]{2,1,0:T(8,128)(2,1)S(1)} %fusion.21), channel_id=1, source_target_pairs={{16,0},{24,8},{0,16},{8,24},{48,32},{56,40},{32,48},{40,56},{80,64... | collective-permute-start | bytes 589832 | tf_op jit(solution)/shard_map/ppermute | solution.py:26
  63.3 2.5 %collective-permute-done.16 = bf16[2,16,3072]{2,1,0:T(8,128)(2,1)S(1)} collective-permute-done((bf16[2,16,3072]{2,1,0:T(8,128)(2,1)S(1)}, bf16[2,16,3072]{2,1,0:T(8,128)(2,1)S(1)}, u32[]{:S(2)}, u32[]{:S(2)}) %collective-permute-start.16) | collective-permute-done | bytes 196640 | tf_op jit(solution)/shard_map/ppermute | solution.py:26
  65.8 1.6 %collective-permute-done.15 = bf16[2,16,3072]{2,1,0:T(8,128)(2,1)S(1)} collective-permute-done((bf16[2,16,3072]{2,1,0:T(8,128)(2,1)S(1)}, bf16[2,16,3072]{2,1,0:T(8,128)(2,1)S(1)}, u32[]{:S(2)}, u32[]{:S(2)}) %collective-permute-start.15) | collective-permute-done | bytes 196640 | tf_op jit(solution)/shard_map/ppermute | solution.py:26
  67.4 0.8 collective-permute-done.14
  68.7 1.2 collective-permute-start.19
  70.0 2.9 %collective-permute-start.18 = (bf16[2,16,3072]{2,1,0:T(8,128)(2,1)S(1)}, bf16[2,16,3072]{2,1,0:T(8,128)(2,1)S(1)}, u32[]{:S(2)}, u32[]{:S(2)}) collective-permute-start(bf16[2,16,3072]{2,1,0:T(8,128)(2,1)S(1)} %get-tuple-element.38), channel_id=1, source_target_pairs={{64,0},{72,8},{80,16},{88,24},{96,32},{104,40},{112,48},{120,56},{... | collective-permute-start | bytes 589832 | tf_op jit(solution)/shard_map/ppermute | solution.py:26
  73.4 2.7 %collective-permute-start.20 = (bf16[2,16,3072]{2,1,0:T(8,128)(2,1)S(1)}, bf16[2,16,3072]{2,1,0:T(8,128)(2,1)S(1)}, u32[]{:S(2)}, u32[]{:S(2)}) collective-permute-start(bf16[2,16,3072]{2,1,0:T(8,128)(2,1)S(1)} %get-tuple-element.39), channel_id=1, source_target_pairs={{16,0},{24,8},{0,16},{8,24},{48,32},{56,40},{32,48},{40,56},{80,64... | collective-permute-start | bytes 589832 | tf_op jit(solution)/shard_map/ppermute | solution.py:26
  76.1 1.8 %collective-permute-done.19 = bf16[2,16,3072]{2,1,0:T(8,128)(2,1)S(1)} collective-permute-done((bf16[2,16,3072]{2,1,0:T(8,128)(2,1)S(1)}, bf16[2,16,3072]{2,1,0:T(8,128)(2,1)S(1)}, u32[]{:S(2)}, u32[]{:S(2)}) %collective-permute-start.19) | collective-permute-done | bytes 196640 | tf_op jit(solution)/shard_map/ppermute | solution.py:26
  78.0 2.4 %collective-permute-done.18 = bf16[2,16,3072]{2,1,0:T(8,128)(2,1)S(1)} collective-permute-done((bf16[2,16,3072]{2,1,0:T(8,128)(2,1)S(1)}, bf16[2,16,3072]{2,1,0:T(8,128)(2,1)S(1)}, u32[]{:S(2)}, u32[]{:S(2)}) %collective-permute-start.18) | collective-permute-done | bytes 196640 | tf_op jit(solution)/shard_map/ppermute | solution.py:26
  80.6 2.8 %collective-permute-start.21 = (bf16[4,2,16,3072]{3,2,1,0:T(8,128)(2,1)S(1)}, bf16[4,2,16,3072]{3,2,1,0:T(8,128)(2,1)S(1)}, u32[]{:S(2)}, u32[]{:S(2)}) collective-permute-start(bf16[4,2,16,3072]{3,2,1,0:T(8,128)(2,1)S(1)} %pad_maximum_fusion.4), channel_id=1, source_target_pairs={{16,0},{24,8},{0,16},{8,24},{48,32},{56,40},{32,48},{40,56},{80,64... | collective-permute-start | bytes 2359304 | tf_op jit(solution)/shard_map/ppermute | solution.py:26
  83.4 1.5 %collective-permute-start.25 = (bf16[2,2,16,3072]{3,2,1,0:T(8,128)(2,1)S(1)}, bf16[2,2,16,3072]{3,2,1,0:T(8,128)(2,1)S(1)}, u32[]{:S(2)}, u32[]{:S(2)}) collective-permute-start(bf16[2,2,16,3072]{3,2,1,0:T(8,128)(2,1)S(1)} %pad_maximum_fusion.5), channel_id=1, source_target_pairs={{96,0},{104,8},{112,16},{120,24},{0,32},{8,40},{16,48},{24,56},{32... | collective-permute-start | bytes 1179656 | tf_op jit(solution)/shard_map/ppermute | solution.py:26
  84.9 2.2 %collective-permute-start.24 = (bf16[2,2,16,3072]{3,2,1,0:T(8,128)(2,1)S(1)}, bf16[2,2,16,3072]{3,2,1,0:T(8,128)(2,1)S(1)}, u32[]{:S(2)}, u32[]{:S(2)}) collective-permute-start(bf16[2,2,16,3072]{3,2,1,0:T(8,128)(2,1)S(1)} %pad_maximum_fusion.5), channel_id=1, source_target_pairs={{64,0},{72,8},{80,16},{88,24},{96,32},{104,40},{112,48},{120,56},{... | collective-permute-start | bytes 1179656 | tf_op jit(solution)/shard_map/ppermute | solution.py:26
  87.1 1.1 collective-permute-start.23
  88.2 6.5 %collective-permute-done.25 = bf16[2,2,16,3072]{3,2,1,0:T(8,128)(2,1)S(1)} collective-permute-done((bf16[2,2,16,3072]{3,2,1,0:T(8,128)(2,1)S(1)}, bf16[2,2,16,3072]{3,2,1,0:T(8,128)(2,1)S(1)}, u32[]{:S(2)}, u32[]{:S(2)}) %collective-permute-start.25) | collective-permute-done | bytes 393248 | tf_op jit(solution)/shard_map/ppermute | solution.py:26
  94.8 8.1 %collective-permute-done.24 = bf16[2,2,16,3072]{3,2,1,0:T(8,128)(2,1)S(1)} collective-permute-done((bf16[2,2,16,3072]{3,2,1,0:T(8,128)(2,1)S(1)}, bf16[2,2,16,3072]{3,2,1,0:T(8,128)(2,1)S(1)}, u32[]{:S(2)}, u32[]{:S(2)}) %collective-permute-start.24) | collective-permute-done | bytes 393248 | tf_op jit(solution)/shard_map/ppermute | solution.py:26
  104.0 2.7 %collective-permute-done.26.refs_3_.other_ref = bf16[4,2,2,16,3072]{4,3,2,1,0:T(8,128)(2,1)S(1)} collective-permute-done((bf16[4,2,2,16,3072]{4,3,2,1,0:T(8,128)(2,1)S(1)}, bf16[4,2,2,16,3072]{4,3,2,1,0:T(8,128)(2,1)S(1)}, u32[]{:S(2)}, u32[]{:S(2)}) %collective-permute-start.26) | collective-permute-done | bytes 1572896 | tf_op jit(solution)/shard_map/ppermute | solution.py:26
  106.6 2.0 %shard_map.73 = f32[256,768]{1,0:T(8,128)S(1)} custom-call(s32[16]{0:T(128)S(1)} %fusion.31.place_ref, bf16[4,2,2,16,3072]{4,3,2,1,0:T(8,128)(2,1)S(1)} %pad_maximum_fusion.1.refs_2_.own_ref, bf16[4,2,2,16,3072]{4,3,2,1,0:T(8,128)(2,1)S(1)} %collective-permute-done.26.refs_3_.other_ref, bf16[768,3072]{1,0:T(8,128)(2,1)S(1)} %get-tuple-element.26.in_ref.weight_ref), custom_call_target="tpu_custom_call" | custom-call | flops 1 | bytes 1 | tf_op jit(solution)/shard_map/pallas_call | solution.py:136
  108.7 1.9 %collective-permute-start.33 = (bf16[64,768]{1,0:T(8,128)(2,1)S(1)}, bf16[64,768]{1,0:T(8,128)(2,1)S(1)}, u32[]{:S(2)}, u32[]{:S(2)}) collective-permute-start(bf16[64,768]{1,0:T(8,128)(2,1)S(1)} %get-tuple-element.57), channel_id=1, source_target_pairs={{6,0},{7,1},{4,2},{5,3},{2,4},{3,5},{0,6},{1,7},{14,8},{15,9},{12,... | collective-permute-start | bytes 294920 | tf_op jit(solution)/shard_map/ppermute | solution.py:30
  110.6 2.8 %collective-permute-start.32 = (bf16[64,768]{1,0:T(8,128)(2,1)S(1)}, bf16[64,768]{1,0:T(8,128)(2,1)S(1)}, u32[]{:S(2)}, u32[]{:S(2)}) collective-permute-start(bf16[64,768]{1,0:T(8,128)(2,1)S(1)} %get-tuple-element.58), channel_id=1, source_target_pairs={{5,0},{6,1},{7,2},{4,3},{1,4},{2,5},{3,6},{0,7},{13,8},{14,9},{15,... | collective-permute-start | bytes 294920 | tf_op jit(solution)/shard_map/ppermute | solution.py:30
  113.5 1.8 %collective-permute-start.30 = (bf16[64,768]{1,0:T(8,128)(2,1)S(1)}, bf16[64,768]{1,0:T(8,128)(2,1)S(1)}, u32[]{:S(2)}, u32[]{:S(2)}) collective-permute-start(bf16[64,768]{1,0:T(8,128)(2,1)S(1)} %get-tuple-element.56), channel_id=1, source_target_pairs={{4,0},{5,1},{6,2},{7,3},{0,4},{1,5},{2,6},{3,7},{12,8},{13,9},{14,... | collective-permute-start | bytes 294920 | tf_op jit(solution)/shard_map/ppermute | solution.py:30
  115.4 2.0 %shard_map.72 = f32[256,768]{1,0:T(8,128)S(1)} custom-call(s32[16]{0:T(128)S(1)} %fusion.29.place_ref, bf16[2,4,2,16,3072]{4,3,2,1,0:T(8,128)(2,1)S(1)} %pad_maximum_fusion.refs_0_.own_ref, bf16[2,4,2,16,3072]{4,3,2,1,0:T(8,128)(2,1)S(1)} %collective-permute-done.22.refs_1_.other_ref, bf16[768,3072]{1,0:T(8,128)(2,1)S(1)} %get-tuple-element.26.in_ref.weight_ref), custom_call_target="tpu_custom_call" | custom-call | flops 1 | bytes 1 | tf_op jit(solution)/shard_map/pallas_call | solution.py:136
  117.4 1.4 %collective-permute-start.29 = (bf16[64,768]{1,0:T(8,128)(2,1)S(1)}, bf16[64,768]{1,0:T(8,128)(2,1)S(1)}, u32[]{:S(2)}, u32[]{:S(2)}) collective-permute-start(bf16[64,768]{1,0:T(8,128)(2,1)S(1)} %get-tuple-element.54), channel_id=1, source_target_pairs={{2,0},{3,1},{0,2},{1,3},{6,4},{7,5},{4,6},{5,7},{10,8},{11,9},{8,1... | collective-permute-start | bytes 294920 | tf_op jit(solution)/shard_map/ppermute | solution.py:30
  118.8 2.0 %collective-permute-start.28 = (bf16[64,768]{1,0:T(8,128)(2,1)S(1)}, bf16[64,768]{1,0:T(8,128)(2,1)S(1)}, u32[]{:S(2)}, u32[]{:S(2)}) collective-permute-start(bf16[64,768]{1,0:T(8,128)(2,1)S(1)} %get-tuple-element.55), channel_id=1, source_target_pairs={{1,0},{2,1},{3,2},{0,3},{5,4},{6,5},{7,6},{4,7},{9,8},{10,9},{11,1... | collective-permute-start | bytes 294920 | tf_op jit(solution)/shard_map/ppermute | solution.py:30
  121.2 3.6 %shard_map.70 = bf16[768,3072]{1,0:T(8,128)(2,1)} custom-call(bf16[2,4,2,16,3072]{4,3,2,1,0:T(8,128)(2,1)S(1)} %pad_maximum_fusion.refs_0_.own_ref, bf16[2,4,2,16,3072]{4,3,2,1,0:T(8,128)(2,1)S(1)} %collective-permute-done.22.refs_1_.other_ref, bf16[4,2,2,16,3072]{4,3,2,1,0:T(8,128)(2,1)S(1)} %pad_maximum_fusion.1.refs_2_.own_ref, ...), custom_call_target="tpu_custom_call" | custom-call | flops 1 | bytes 1 | tf_op jit(solution)/shard_map/pallas_call | solution.py:175
  124.8 3.7 %shard_map.71 = bf16[3072,768]{1,0:T(8,128)(2,1)} custom-call(bf16[2,4,2,16,3072]{4,3,2,1,0:T(8,128)(2,1)S(1)} %pad_maximum_fusion.refs_0_.own_ref, bf16[2,4,2,16,3072]{4,3,2,1,0:T(8,128)(2,1)S(1)} %collective-permute-done.22.refs_1_.other_ref, bf16[4,2,2,16,3072]{4,3,2,1,0:T(8,128)(2,1)S(1)} %pad_maximum_fusion.1.refs_2_.own_ref, ...), custom_call_target="tpu_custom_call" | custom-call | flops 1 | bytes 1 | tf_op jit(solution)/shard_map/pallas_call | solution.py:175
  128.6 0.7 fusion.28
  (55 shorter events, 5.1 us)
Async XLA Ops:
  1.6 8.2 %collective-permute-start = (bf16[2,64,768]{2,1,0:T(8,128)(2,1)S(1)}, bf16[2,64,768]{2,1,0:T(8,128)(2,1)S(1)}, u32[]{:S(2)}, u32[]{:S(2)}) collective-permute-start(bf16[2,64,768]{2,1,0:T(8,128)(2,1)S(1)} %pad_maximum_fusion.6), channel_id=1, source_target_pairs={{4,0},{5,1},{6,2},{7,3},{0,4},{1,5},{2,6},{3,7},{12,8},{13,9},{14,... | collective-permute-start | bytes 589832 | tf_op jit(solution)/shard_map/ppermute | solution.py:30
  3.2 10.7 %collective-permute-start.3 = (bf16[2,64,768]{2,1,0:T(8,128)(2,1)S(1)}, bf16[2,64,768]{2,1,0:T(8,128)(2,1)S(1)}, u32[]{:S(2)}, u32[]{:S(2)}) collective-permute-start(bf16[2,64,768]{2,1,0:T(8,128)(2,1)S(1)} %pad_maximum_fusion.6), channel_id=1, source_target_pairs={{3,0},{0,1},{1,2},{2,3},{7,4},{4,5},{5,6},{6,7},{11,8},{8,9},{9,10... | collective-permute-start | bytes 589832 | tf_op jit(solution)/shard_map/ppermute | solution.py:30
  5.2 13.8 %collective-permute-start.2 = (bf16[2,64,768]{2,1,0:T(8,128)(2,1)S(1)}, bf16[2,64,768]{2,1,0:T(8,128)(2,1)S(1)}, u32[]{:S(2)}, u32[]{:S(2)}) collective-permute-start(bf16[2,64,768]{2,1,0:T(8,128)(2,1)S(1)} %pad_maximum_fusion.6), channel_id=1, source_target_pairs={{2,0},{3,1},{0,2},{1,3},{6,4},{7,5},{4,6},{5,7},{10,8},{11,9},{8,1... | collective-permute-start | bytes 589832 | tf_op jit(solution)/shard_map/ppermute | solution.py:30
  8.7 10.2 %collective-permute-start.1 = (bf16[2,64,768]{2,1,0:T(8,128)(2,1)S(1)}, bf16[2,64,768]{2,1,0:T(8,128)(2,1)S(1)}, u32[]{:S(2)}, u32[]{:S(2)}) collective-permute-start(bf16[2,64,768]{2,1,0:T(8,128)(2,1)S(1)} %pad_maximum_fusion.6), channel_id=1, source_target_pairs={{1,0},{2,1},{3,2},{0,3},{5,4},{6,5},{7,6},{4,7},{9,8},{10,9},{11,1... | collective-permute-start | bytes 589832 | tf_op jit(solution)/shard_map/ppermute | solution.py:30
  9.8 12.5 %collective-permute-start.6 = (bf16[2,64,768]{2,1,0:T(8,128)(2,1)S(1)}, bf16[2,64,768]{2,1,0:T(8,128)(2,1)S(1)}, u32[]{:S(2)}, u32[]{:S(2)}) collective-permute-start(bf16[2,64,768]{2,1,0:T(8,128)(2,1)S(1)} %collective-permute-done), channel_id=1, source_target_pairs={{3,0},{0,1},{1,2},{2,3},{7,4},{4,5},{5,6},{6,7},{11,8},{8,9},{9,10... | collective-permute-start | bytes 589832 | tf_op jit(solution)/shard_map/ppermute | solution.py:30
  10.8 15.0 %collective-permute-start.5 = (bf16[2,64,768]{2,1,0:T(8,128)(2,1)S(1)}, bf16[2,64,768]{2,1,0:T(8,128)(2,1)S(1)}, u32[]{:S(2)}, u32[]{:S(2)}) collective-permute-start(bf16[2,64,768]{2,1,0:T(8,128)(2,1)S(1)} %collective-permute-done), channel_id=1, source_target_pairs={{2,0},{3,1},{0,2},{1,3},{6,4},{7,5},{4,6},{5,7},{10,8},{11,9},{8,1... | collective-permute-start | bytes 589832 | tf_op jit(solution)/shard_map/ppermute | solution.py:30
  13.9 11.9 %collective-permute-start.4 = (bf16[2,64,768]{2,1,0:T(8,128)(2,1)S(1)}, bf16[2,64,768]{2,1,0:T(8,128)(2,1)S(1)}, u32[]{:S(2)}, u32[]{:S(2)}) collective-permute-start(bf16[2,64,768]{2,1,0:T(8,128)(2,1)S(1)} %collective-permute-done), channel_id=1, source_target_pairs={{1,0},{2,1},{3,2},{0,3},{5,4},{6,5},{7,6},{4,7},{9,8},{10,9},{11,1... | collective-permute-start | bytes 589832 | tf_op jit(solution)/shard_map/ppermute | solution.py:30
  25.9 3.9 %collective-permute-start.7 = (bf16[2,128,3072]{2,1,0:T(8,128)(2,1)S(1)}, bf16[2,128,3072]{2,1,0:T(8,128)(2,1)S(1)}, u32[]{:S(2)}, u32[]{:S(2)}) collective-permute-start(bf16[2,128,3072]{2,1,0:T(8,128)(2,1)S(1)} %get-tuple-element.31), channel_id=1, source_target_pairs={{8,0},{0,8},{24,16},{16,24},{40,32},{32,40},{56,48},{48,56},{72,64... | collective-permute-start | bytes 4718600 | tf_op jit(solution)/shard_map/ppermute | solution.py:26
  29.2 6.6 %collective-permute-start.11 = (bf16[2,128,3072]{2,1,0:T(8,128)(2,1)S(1)}, bf16[2,128,3072]{2,1,0:T(8,128)(2,1)S(1)}, u32[]{:S(2)}, u32[]{:S(2)}) collective-permute-start(bf16[2,128,3072]{2,1,0:T(8,128)(2,1)S(1)} %get-tuple-element.34), channel_id=1, source_target_pairs={{8,0},{0,8},{24,16},{16,24},{40,32},{32,40},{56,48},{48,56},{72,64... | collective-permute-start | bytes 4718600 | tf_op jit(solution)/shard_map/ppermute | solution.py:26
  30.4 13.6 %collective-permute-start.10 = (bf16[2,2,16,3072]{3,2,0,1:T(8,128)(2,1)S(1)}, bf16[2,2,16,3072]{3,2,0,1:T(8,128)(2,1)S(1)}, u32[]{:S(2)}, u32[]{:S(2)}) collective-permute-start(bf16[2,2,16,3072]{3,2,0,1:T(8,128)(2,1)S(1)} %get-tuple-element.48), channel_id=1, source_target_pairs={{64,0},{72,8},{80,16},{88,24},{96,32},{104,40},{112,48},{120,56},{... | collective-permute-start | bytes 1179656 | tf_op jit(solution)/shard_map/ppermute | solution.py:26
  33.7 18.2 %collective-permute-start.9 = (bf16[2,2,16,3072]{3,2,0,1:T(8,128)(2,1)S(1)}, bf16[2,2,16,3072]{3,2,0,1:T(8,128)(2,1)S(1)}, u32[]{:S(2)}, u32[]{:S(2)}) collective-permute-start(bf16[2,2,16,3072]{3,2,0,1:T(8,128)(2,1)S(1)} %get-tuple-element.49), channel_id=1, source_target_pairs={{32,0},{40,8},{48,16},{56,24},{64,32},{72,40},{80,48},{88,56},{96,... | collective-permute-start | bytes 1179656 | tf_op jit(solution)/shard_map/ppermute | solution.py:26
  34.8 17.1 %collective-permute-start.8 = (bf16[2,2,16,3072]{3,2,0,1:T(8,128)(2,1)S(1)}, bf16[2,2,16,3072]{3,2,0,1:T(8,128)(2,1)S(1)}, u32[]{:S(2)}, u32[]{:S(2)}) collective-permute-start(bf16[2,2,16,3072]{3,2,0,1:T(8,128)(2,1)S(1)} %get-tuple-element.47), channel_id=1, source_target_pairs={{96,0},{104,8},{112,16},{120,24},{0,32},{8,40},{16,48},{24,56},{32... | collective-permute-start | bytes 1179656 | tf_op jit(solution)/shard_map/ppermute | solution.py:26
  36.4 20.2 %collective-permute-start.12 = (bf16[2,4,16,3072]{3,2,0,1:T(8,128)(2,1)S(1)}, bf16[2,4,16,3072]{3,2,0,1:T(8,128)(2,1)S(1)}, u32[]{:S(2)}, u32[]{:S(2)}) collective-permute-start(bf16[2,4,16,3072]{3,2,0,1:T(8,128)(2,1)S(1)} %fusion.1), channel_id=1, source_target_pairs={{16,0},{24,8},{0,16},{8,24},{48,32},{56,40},{32,48},{40,56},{80,64... | collective-permute-start | bytes 2359304 | tf_op jit(solution)/shard_map/ppermute | solution.py:26
  57.0 8.9 %collective-permute-start.16 = (bf16[2,16,3072]{2,1,0:T(8,128)(2,1)S(1)}, bf16[2,16,3072]{2,1,0:T(8,128)(2,1)S(1)}, u32[]{:S(2)}, u32[]{:S(2)}) collective-permute-start(bf16[2,16,3072]{2,1,0:T(8,128)(2,1)S(1)} %get-tuple-element.51), channel_id=1, source_target_pairs={{64,0},{72,8},{80,16},{88,24},{96,32},{104,40},{112,48},{120,56},{... | collective-permute-start | bytes 589832 | tf_op jit(solution)/shard_map/ppermute | solution.py:26
  58.5 9.0 %collective-permute-start.15 = (bf16[2,16,3072]{2,1,0:T(8,128)(2,1)S(1)}, bf16[2,16,3072]{2,1,0:T(8,128)(2,1)S(1)}, u32[]{:S(2)}, u32[]{:S(2)}) collective-permute-start(bf16[2,16,3072]{2,1,0:T(8,128)(2,1)S(1)} %get-tuple-element.52), channel_id=1, source_target_pairs={{32,0},{40,8},{48,16},{56,24},{64,32},{72,40},{80,48},{88,56},{96,... | collective-permute-start | bytes 589832 | tf_op jit(solution)/shard_map/ppermute | solution.py:26
  60.4 7.8 %collective-permute-start.14 = (bf16[2,16,3072]{2,1,0:T(8,128)(2,1)S(1)}, bf16[2,16,3072]{2,1,0:T(8,128)(2,1)S(1)}, u32[]{:S(2)}, u32[]{:S(2)}) collective-permute-start(bf16[2,16,3072]{2,1,0:T(8,128)(2,1)S(1)} %get-tuple-element.50), channel_id=1, source_target_pairs={{96,0},{104,8},{112,16},{120,24},{0,32},{8,40},{16,48},{24,56},{32... | collective-permute-start | bytes 589832 | tf_op jit(solution)/shard_map/ppermute | solution.py:26
  60.5 8.0 %collective-permute-start.13 = (bf16[2,16,3072]{2,1,0:T(8,128)(2,1)S(1)}, bf16[2,16,3072]{2,1,0:T(8,128)(2,1)S(1)}, u32[]{:S(2)}, u32[]{:S(2)}) collective-permute-start(bf16[2,16,3072]{2,1,0:T(8,128)(2,1)S(1)} %fusion.21), channel_id=1, source_target_pairs={{16,0},{24,8},{0,16},{8,24},{48,32},{56,40},{32,48},{40,56},{80,64... | collective-permute-start | bytes 589832 | tf_op jit(solution)/shard_map/ppermute | solution.py:26
  68.7 9.2 %collective-permute-start.19 = (bf16[2,16,3072]{2,1,0:T(8,128)(2,1)S(1)}, bf16[2,16,3072]{2,1,0:T(8,128)(2,1)S(1)}, u32[]{:S(2)}, u32[]{:S(2)}) collective-permute-start(bf16[2,16,3072]{2,1,0:T(8,128)(2,1)S(1)} %get-tuple-element.38), channel_id=1, source_target_pairs={{96,0},{104,8},{112,16},{120,24},{0,32},{8,40},{16,48},{24,56},{32... | collective-permute-start | bytes 589832 | tf_op jit(solution)/shard_map/ppermute | solution.py:26
  70.0 10.4 %collective-permute-start.18 = (bf16[2,16,3072]{2,1,0:T(8,128)(2,1)S(1)}, bf16[2,16,3072]{2,1,0:T(8,128)(2,1)S(1)}, u32[]{:S(2)}, u32[]{:S(2)}) collective-permute-start(bf16[2,16,3072]{2,1,0:T(8,128)(2,1)S(1)} %get-tuple-element.38), channel_id=1, source_target_pairs={{64,0},{72,8},{80,16},{88,24},{96,32},{104,40},{112,48},{120,56},{... | collective-permute-start | bytes 589832 | tf_op jit(solution)/shard_map/ppermute | solution.py:26
  72.9 7.5 %collective-permute-start.17 = (bf16[2,16,3072]{2,1,0:T(8,128)(2,1)S(1)}, bf16[2,16,3072]{2,1,0:T(8,128)(2,1)S(1)}, u32[]{:S(2)}, u32[]{:S(2)}) collective-permute-start(bf16[2,16,3072]{2,1,0:T(8,128)(2,1)S(1)} %get-tuple-element.38), channel_id=1, source_target_pairs={{32,0},{40,8},{48,16},{56,24},{64,32},{72,40},{80,48},{88,56},{96,... | collective-permute-start | bytes 589832 | tf_op jit(solution)/shard_map/ppermute | solution.py:26
  73.4 7.2 %collective-permute-start.20 = (bf16[2,16,3072]{2,1,0:T(8,128)(2,1)S(1)}, bf16[2,16,3072]{2,1,0:T(8,128)(2,1)S(1)}, u32[]{:S(2)}, u32[]{:S(2)}) collective-permute-start(bf16[2,16,3072]{2,1,0:T(8,128)(2,1)S(1)} %get-tuple-element.39), channel_id=1, source_target_pairs={{16,0},{24,8},{0,16},{8,24},{48,32},{56,40},{32,48},{40,56},{80,64... | collective-permute-start | bytes 589832 | tf_op jit(solution)/shard_map/ppermute | solution.py:26
  80.6 22.6 %collective-permute-start.21 = (bf16[4,2,16,3072]{3,2,1,0:T(8,128)(2,1)S(1)}, bf16[4,2,16,3072]{3,2,1,0:T(8,128)(2,1)S(1)}, u32[]{:S(2)}, u32[]{:S(2)}) collective-permute-start(bf16[4,2,16,3072]{3,2,1,0:T(8,128)(2,1)S(1)} %pad_maximum_fusion.4), channel_id=1, source_target_pairs={{16,0},{24,8},{0,16},{8,24},{48,32},{56,40},{32,48},{40,56},{80,64... | collective-permute-start | bytes 2359304 | tf_op jit(solution)/shard_map/ppermute | solution.py:26
  83.4 11.4 %collective-permute-start.25 = (bf16[2,2,16,3072]{3,2,1,0:T(8,128)(2,1)S(1)}, bf16[2,2,16,3072]{3,2,1,0:T(8,128)(2,1)S(1)}, u32[]{:S(2)}, u32[]{:S(2)}) collective-permute-start(bf16[2,2,16,3072]{3,2,1,0:T(8,128)(2,1)S(1)} %pad_maximum_fusion.5), channel_id=1, source_target_pairs={{96,0},{104,8},{112,16},{120,24},{0,32},{8,40},{16,48},{24,56},{32... | collective-permute-start | bytes 1179656 | tf_op jit(solution)/shard_map/ppermute | solution.py:26
  84.9 18.0 %collective-permute-start.24 = (bf16[2,2,16,3072]{3,2,1,0:T(8,128)(2,1)S(1)}, bf16[2,2,16,3072]{3,2,1,0:T(8,128)(2,1)S(1)}, u32[]{:S(2)}, u32[]{:S(2)}) collective-permute-start(bf16[2,2,16,3072]{3,2,1,0:T(8,128)(2,1)S(1)} %pad_maximum_fusion.5), channel_id=1, source_target_pairs={{64,0},{72,8},{80,16},{88,24},{96,32},{104,40},{112,48},{120,56},{... | collective-permute-start | bytes 1179656 | tf_op jit(solution)/shard_map/ppermute | solution.py:26
  87.1 15.8 %collective-permute-start.23 = (bf16[2,2,16,3072]{3,2,1,0:T(8,128)(2,1)S(1)}, bf16[2,2,16,3072]{3,2,1,0:T(8,128)(2,1)S(1)}, u32[]{:S(2)}, u32[]{:S(2)}) collective-permute-start(bf16[2,2,16,3072]{3,2,1,0:T(8,128)(2,1)S(1)} %pad_maximum_fusion.5), channel_id=1, source_target_pairs={{32,0},{40,8},{48,16},{56,24},{64,32},{72,40},{80,48},{88,56},{96,... | collective-permute-start | bytes 1179656 | tf_op jit(solution)/shard_map/ppermute | solution.py:26
  103.1 3.5 %collective-permute-start.26 = (bf16[4,2,2,16,3072]{4,3,2,1,0:T(8,128)(2,1)S(1)}, bf16[4,2,2,16,3072]{4,3,2,1,0:T(8,128)(2,1)S(1)}, u32[]{:S(2)}, u32[]{:S(2)}) collective-permute-start(bf16[4,2,2,16,3072]{4,3,2,1,0:T(8,128)(2,1)S(1)} %pad_maximum_fusion.1.refs_2_.own_ref), channel_id=1, source_target_pairs={{8,0},{0,8},{24,16},{16,24},{40,32},{32,40},{56,48},{48,56},{72,64... | collective-permute-start | bytes 4718600 | tf_op jit(solution)/shard_map/ppermute | solution.py:26
  103.4 12.0 %collective-permute-start.22 = (bf16[2,4,2,16,3072]{4,3,2,1,0:T(8,128)(2,1)S(1)}, bf16[2,4,2,16,3072]{4,3,2,1,0:T(8,128)(2,1)S(1)}, u32[]{:S(2)}, u32[]{:S(2)}) collective-permute-start(bf16[2,4,2,16,3072]{4,3,2,1,0:T(8,128)(2,1)S(1)} %pad_maximum_fusion.refs_0_.own_ref), channel_id=1, source_target_pairs={{8,0},{0,8},{24,16},{16,24},{40,32},{32,40},{56,48},{48,56},{72,64... | collective-permute-start | bytes 4718600 | tf_op jit(solution)/shard_map/ppermute | solution.py:26
  108.7 10.1 %collective-permute-start.33 = (bf16[64,768]{1,0:T(8,128)(2,1)S(1)}, bf16[64,768]{1,0:T(8,128)(2,1)S(1)}, u32[]{:S(2)}, u32[]{:S(2)}) collective-permute-start(bf16[64,768]{1,0:T(8,128)(2,1)S(1)} %get-tuple-element.57), channel_id=1, source_target_pairs={{6,0},{7,1},{4,2},{5,3},{2,4},{3,5},{0,6},{1,7},{14,8},{15,9},{12,... | collective-permute-start | bytes 294920 | tf_op jit(solution)/shard_map/ppermute | solution.py:30
  110.6 10.2 %collective-permute-start.32 = (bf16[64,768]{1,0:T(8,128)(2,1)S(1)}, bf16[64,768]{1,0:T(8,128)(2,1)S(1)}, u32[]{:S(2)}, u32[]{:S(2)}) collective-permute-start(bf16[64,768]{1,0:T(8,128)(2,1)S(1)} %get-tuple-element.58), channel_id=1, source_target_pairs={{5,0},{6,1},{7,2},{4,3},{1,4},{2,5},{3,6},{0,7},{13,8},{14,9},{15,... | collective-permute-start | bytes 294920 | tf_op jit(solution)/shard_map/ppermute | solution.py:30
  113.4 15.1 %collective-permute-start.31 = (bf16[64,768]{1,0:T(8,128)(2,1)S(1)}, bf16[64,768]{1,0:T(8,128)(2,1)S(1)}, u32[]{:S(2)}, u32[]{:S(2)}) collective-permute-start(bf16[64,768]{1,0:T(8,128)(2,1)S(1)} %get-tuple-element.59), channel_id=1, source_target_pairs={{7,0},{4,1},{5,2},{6,3},{3,4},{0,5},{1,6},{2,7},{15,8},{12,9},{13,... | collective-permute-start | bytes 294920 | tf_op jit(solution)/shard_map/ppermute | solution.py:30
  113.5 15.0 %collective-permute-start.30 = (bf16[64,768]{1,0:T(8,128)(2,1)S(1)}, bf16[64,768]{1,0:T(8,128)(2,1)S(1)}, u32[]{:S(2)}, u32[]{:S(2)}) collective-permute-start(bf16[64,768]{1,0:T(8,128)(2,1)S(1)} %get-tuple-element.56), channel_id=1, source_target_pairs={{4,0},{5,1},{6,2},{7,3},{0,4},{1,5},{2,6},{3,7},{12,8},{13,9},{14,... | collective-permute-start | bytes 294920 | tf_op jit(solution)/shard_map/ppermute | solution.py:30
  117.4 11.1 %collective-permute-start.29 = (bf16[64,768]{1,0:T(8,128)(2,1)S(1)}, bf16[64,768]{1,0:T(8,128)(2,1)S(1)}, u32[]{:S(2)}, u32[]{:S(2)}) collective-permute-start(bf16[64,768]{1,0:T(8,128)(2,1)S(1)} %get-tuple-element.54), channel_id=1, source_target_pairs={{2,0},{3,1},{0,2},{1,3},{6,4},{7,5},{4,6},{5,7},{10,8},{11,9},{8,1... | collective-permute-start | bytes 294920 | tf_op jit(solution)/shard_map/ppermute | solution.py:30
  118.8 9.7 %collective-permute-start.28 = (bf16[64,768]{1,0:T(8,128)(2,1)S(1)}, bf16[64,768]{1,0:T(8,128)(2,1)S(1)}, u32[]{:S(2)}, u32[]{:S(2)}) collective-permute-start(bf16[64,768]{1,0:T(8,128)(2,1)S(1)} %get-tuple-element.55), channel_id=1, source_target_pairs={{1,0},{2,1},{3,2},{0,3},{5,4},{6,5},{7,6},{4,7},{9,8},{10,9},{11,1... | collective-permute-start | bytes 294920 | tf_op jit(solution)/shard_map/ppermute | solution.py:30
  120.9 7.7 %collective-permute-start.27 = (bf16[64,768]{1,0:T(8,128)(2,1)S(1)}, bf16[64,768]{1,0:T(8,128)(2,1)S(1)}, u32[]{:S(2)}, u32[]{:S(2)}) collective-permute-start(bf16[64,768]{1,0:T(8,128)(2,1)S(1)} %get-tuple-element.53), channel_id=1, source_target_pairs={{3,0},{0,1},{1,2},{2,3},{7,4},{4,5},{5,6},{6,7},{11,8},{8,9},{9,10... | collective-permute-start | bytes 294920 | tf_op jit(solution)/shard_map/ppermute | solution.py:30

commit v4 on v3

--- a/solution.py
+++ b/solution.py
@@ -120,12 +120,12 @@
 
 
 def back_project(own, other, weight, place):
-    p, q, _, t, hidden = own.shape
+    p, q, t, hidden = own.shape
     half = p * q * t
     k = weight.shape[0]
 
     def body(place_ref, own_ref, other_ref, weight_ref, out_ref):
-        grad = jnp.concatenate([own_ref[:, :, 1].reshape(half, hidden), other_ref[:, :, 1].reshape(half, hidden)])
+        grad = jnp.concatenate([ref[...].reshape(half, hidden) for ref in (own_ref, other_ref)])
         for i in range(k // 256):
             part = pl.ds(i * 256, 256)
             total = contract(grad, weight_ref[part, :], 1, 1)
@@ -160,7 +160,7 @@
         copies = []
         for i in range(steps):
             part = pl.ds(i * TILE, TILE)
-            value = jnp.concatenate([ref[:, :, which, :, part].reshape(rows // 2, TILE) for ref in part_refs])
+            value = jnp.concatenate([ref[:, :, :, part].reshape(rows // 2, TILE) for ref in part_refs])
             if which == 0:
                 made[i] = bf16(contract(value, both, 0, 0))
                 target = out_ref.at[part, :]
@@ -253,17 +253,21 @@
     part_a = gather_y(made_a)
     part_b = jnp.stack([made_b, tied(from_row(made_b, 0, 1, 0), part_a)])
     part_a, part_b = lax.optimization_barrier((part_a, part_b))
-    half_a, half_b = gather_x(part_a), gather_y(part_b)
-    other_b = from_row(half_b, 0, 0, 1)
-    back_b = back_project(half_b, other_b, weights[0], place_b).reshape(4, n, k)
-    other_a = from_row(half_a, 0, 0, 1)
-    back_a = back_project(half_a, other_a, weights[0], place_a).reshape(4, n, k)
+    both_a = [part_a, from_row(part_a, 0, 1, 0)]
+    both_b = [part_b] + [from_row(part_b, dy, 0, 0) for dy in (1, 2, 3)]
+    (act_a, grad_a), (act_b, grad_b) = (
+        [jnp.stack([block[:, m] for block in both]) for m in range(2)] for both in (both_a, both_b)
+    )
+    grad_other_b = from_row(grad_b, 0, 0, 1)
+    back_b = back_project(grad_b, grad_other_b, weights[0], place_b).reshape(4, n, k)
+    grad_other_a = from_row(grad_a, 0, 0, 1)
+    back_a = back_project(grad_a, grad_other_a, weights[0], place_a).reshape(4, n, k)
+    act_other_a, act_other_b = from_row(act_a, 0, 0, 1), from_row(act_b, 0, 0, 1)
     total = sum_z(back_a)
     for dz in (0, 1, 3, 2):
         total = total + f32(from_col(bf16(back_b[dz]), 1, -dz))
-    parts = [half_a, other_a, half_b, other_b]
-    weight_out_grad = weight_grad(parts, [placed_a[1], placed_b[1]], 0)
-    weight_in_grad = weight_grad(parts, [placed_a[0], placed_b[0]], 1)
+    weight_out_grad = weight_grad([act_a, act_other_a, act_b, act_other_b], [placed_a[1], placed_b[1]], 0)
+    weight_in_grad = weight_grad([grad_a, grad_other_a, grad_b, grad_other_b], [placed_a[0], placed_b[0]], 1)
     return (weight_in_grad, weight_out_grad, bf16(total))
 
 

time: 129 us -> 129 us (level)
  waiting for transfers between devices: 47.4 us -> 45.2 us
    ppermute x20 -> x22, waiting for transfers between devices: 43.8 us -> 41.6 us  [from_row(): lax.ppermute(a, 'row', [(at_row(y + dy, x + dx, c + dc), at_row(y, x, c))...]
    ppermute x20 -> x22, starting transfers between devices: 30.8 us -> 31.5 us  [from_row(): lax.ppermute(a, 'row', [(at_row(y + dy, x + dx, c + dc), at_row(y, x, c))...]
  transfers between devices with their start and end apart: 34 -> 36, of which waited for: 13 -> 13; matrix products, arithmetic and copies ran while one was open for 2% -> 2% of each run, Pallas kernels for 17% -> 17%
where the time goes in v4:
time: 129 us; the launch traced here: 128 us
  starting transfers between devices  55.7 us (43%)
  waiting for transfers between devices  45.2 us (35%)
  Pallas kernels  21.3 us (17%)
  other arithmetic  4.49 us (3%)
    ppermute x22, waiting for transfers between devices, from_row(): lax.ppermute(a, 'row', [(at_row(y + dy, x + dx, c + dc), at_row(y, x, c))...  41.6 us
    ppermute x22, starting transfers between devices, from_row(): lax.ppermute(a, 'row', [(at_row(y + dy, x + dx, c + dc), at_row(y, x, c))...  31.5 us
    ppermute x14, starting transfers between devices, from_col(): lax.ppermute(a, 'col', [(at_col(x + dx, z + dz), at_col(x, z)) for x, z i...  24.2 us
    pallas_call x2, Pallas kernels, weight_grad(): pl.pallas_call(body, in_specs=[VMEM] * (3 * chunks), out_specs=pl.BlockSp...  7.25 us
    pallas_call x2, Pallas kernels, project(): pl.pallas_call(body, in_specs=[SMEM, VMEM, VMEM, VMEM], out_specs=[VMEM]...  6.33 us
    pallas_call x2, Pallas kernels, back_project(): pl.pallas_call(body, in_specs=[SMEM, VMEM, VMEM, VMEM], out_specs=VMEM, o...  3.95 us
    pallas_call x1, Pallas kernels, loaded(): pl.pallas_call(body, in_specs=[pl.BlockSpec(memory_space=pl.ANY)] * 2, ou...  3.79 us
    ppermute x14, waiting for transfers between devices, from_col(): lax.ppermute(a, 'col', [(at_col(x + dx, z + dz), at_col(x, z)) for x, z i...  3.56 us
  transfers between devices with their start and end apart: 36, of which 13 were waited for; matrix products, arithmetic and copies ran while one was open for 2% of the time, Pallas kernels for 17%

profile of v4, /device:TPU:0, one launch (start us, length us, event | category | flops | bytes accessed | tf_op | source)
XLA Modules:
  0.0 128.4 jit_solution(11535468396983764570)
XLA Ops:
  0.6 1.0 pad_maximum_fusion.8
  1.6 1.7 %collective-permute-start = (bf16[2,64,768]{2,1,0:T(8,128)(2,1)S(1)}, bf16[2,64,768]{2,1,0:T(8,128)(2,1)S(1)}, u32[]{:S(2)}, u32[]{:S(2)}) collective-permute-start(bf16[2,64,768]{2,1,0:T(8,128)(2,1)S(1)} %pad_maximum_fusion.8), channel_id=1, source_target_pairs={{4,0},{5,1},{6,2},{7,3},{0,4},{1,5},{2,6},{3,7},{12,8},{13,9},{14,... | collective-permute-start | bytes 589832 | tf_op jit(solution)/shard_map/ppermute | solution.py:30
  3.2 1.9 %collective-permute-start.3 = (bf16[2,64,768]{2,1,0:T(8,128)(2,1)S(1)}, bf16[2,64,768]{2,1,0:T(8,128)(2,1)S(1)}, u32[]{:S(2)}, u32[]{:S(2)}) collective-permute-start(bf16[2,64,768]{2,1,0:T(8,128)(2,1)S(1)} %pad_maximum_fusion.8), channel_id=1, source_target_pairs={{3,0},{0,1},{1,2},{2,3},{7,4},{4,5},{5,6},{6,7},{11,8},{8,9},{9,10... | collective-permute-start | bytes 589832 | tf_op jit(solution)/shard_map/ppermute | solution.py:30
  5.2 3.6 %collective-permute-start.2 = (bf16[2,64,768]{2,1,0:T(8,128)(2,1)S(1)}, bf16[2,64,768]{2,1,0:T(8,128)(2,1)S(1)}, u32[]{:S(2)}, u32[]{:S(2)}) collective-permute-start(bf16[2,64,768]{2,1,0:T(8,128)(2,1)S(1)} %pad_maximum_fusion.8), channel_id=1, source_target_pairs={{2,0},{3,1},{0,2},{1,3},{6,4},{7,5},{4,6},{5,7},{10,8},{11,9},{8,1... | collective-permute-start | bytes 589832 | tf_op jit(solution)/shard_map/ppermute | solution.py:30
  8.7 1.0 collective-permute-start.1
  9.8 1.0 collective-permute-start.6
  10.8 3.1 %collective-permute-start.5 = (bf16[2,64,768]{2,1,0:T(8,128)(2,1)S(1)}, bf16[2,64,768]{2,1,0:T(8,128)(2,1)S(1)}, u32[]{:S(2)}, u32[]{:S(2)}) collective-permute-start(bf16[2,64,768]{2,1,0:T(8,128)(2,1)S(1)} %collective-permute-done), channel_id=1, source_target_pairs={{2,0},{3,1},{0,2},{1,3},{6,4},{7,5},{4,6},{5,7},{10,8},{11,9},{8,1... | collective-permute-start | bytes 589832 | tf_op jit(solution)/shard_map/ppermute | solution.py:30
  13.9 1.2 collective-permute-start.4
  15.1 3.8 %shard_map.67 = (bf16[768,3072]{1,0:T(8,128)(2,1)S(1)}, bf16[3072,768]{1,0:T(8,128)(2,1)S(1)}) custom-call(bf16[768,3072]{1,0:T(8,128)(2,1)} %first_ref, bf16[3072,768]{1,0:T(8,128)(2,1)} %second_ref.1), custom_call_target="tpu_custom_call" | custom-call | flops 1 | bytes 1 | tf_op jit(solution)/shard_map/pallas_call | solution.py:78
  19.1 3.2 %shard_map.68 = (f32[2,128,3072]{2,1,0:T(8,128)S(1)}, bf16[2,128,3072]{2,1,0:T(8,128)(2,1)S(1)}, bf16[256,768]{1,0:T(8,128)(2,1)S(1)}, bf16[256,768]{1,0:T(8,128)(2,1)S(1)}) custom-call(s32[16]{0:T(128)S(1)} %fusion.29.place_ref, bf16[4,2,64,768]{3,2,1,0:T(8,128)(2,1)S(1)} %pad_maximum_fusion.tokens_ref, ...), custom_call_target="tpu_custom_call" | custom-call | flops 1 | bytes 1 | tf_op jit(solution)/shard_map/pallas_call | solution.py:107
  22.2 3.5 %collective-permute-done.5 = bf16[2,64,768]{2,1,0:T(8,128)(2,1)S(1)} collective-permute-done((bf16[2,64,768]{2,1,0:T(8,128)(2,1)S(1)}, bf16[2,64,768]{2,1,0:T(8,128)(2,1)S(1)}, u32[]{:S(2)}, u32[]{:S(2)}) %collective-permute-start.5) | collective-permute-done | bytes 196640 | tf_op jit(solution)/shard_map/ppermute | solution.py:30
  26.0 3.2 %shard_map.69 = (f32[2,128,3072]{2,1,0:T(8,128)S(1)}, bf16[2,128,3072]{2,1,0:T(8,128)(2,1)S(1)}, bf16[256,768]{1,0:T(8,128)(2,1)S(1)}, bf16[256,768]{1,0:T(8,128)(2,1)S(1)}) custom-call(s32[16]{0:T(128)S(1)} %fusion.31.place_ref, bf16[4,2,64,768]{3,2,1,0:T(8,128)(2,1)S(1)} %pad_maximum_fusion.1.tokens_ref, ...), custom_call_target="tpu_custom_call" | custom-call | flops 1 | bytes 1 | tf_op jit(solution)/shard_map/pallas_call | solution.py:107
  29.2 0.6 collective-permute-start.11
  30.4 3.3 %collective-permute-start.10 = (bf16[2,2,16,3072]{3,2,0,1:T(8,128)(2,1)S(1)}, bf16[2,2,16,3072]{3,2,0,1:T(8,128)(2,1)S(1)}, u32[]{:S(2)}, u32[]{:S(2)}) collective-permute-start(bf16[2,2,16,3072]{3,2,0,1:T(8,128)(2,1)S(1)} %get-tuple-element.48), channel_id=1, source_target_pairs={{64,0},{72,8},{80,16},{88,24},{96,32},{104,40},{112,48},{120,56},{... | collective-permute-start | bytes 1179656 | tf_op jit(solution)/shard_map/ppermute | solution.py:26
  33.7 1.1 collective-permute-start.9
  34.8 1.0 collective-permute-start.8
  36.4 2.8 %collective-permute-start.12 = (bf16[2,4,16,3072]{3,2,0,1:T(8,128)(2,1)S(1)}, bf16[2,4,16,3072]{3,2,0,1:T(8,128)(2,1)S(1)}, u32[]{:S(2)}, u32[]{:S(2)}) collective-permute-start(bf16[2,4,16,3072]{3,2,0,1:T(8,128)(2,1)S(1)} %fusion.1), channel_id=1, source_target_pairs={{16,0},{24,8},{0,16},{8,24},{48,32},{56,40},{32,48},{40,56},{80,64... | collective-permute-start | bytes 2359304 | tf_op jit(solution)/shard_map/ppermute | solution.py:26
  39.2 4.9 %collective-permute-done.10 = bf16[2,2,16,3072]{3,2,0,1:T(8,128)(2,1)S(1)} collective-permute-done((bf16[2,2,16,3072]{3,2,0,1:T(8,128)(2,1)S(1)}, bf16[2,2,16,3072]{3,2,0,1:T(8,128)(2,1)S(1)}, u32[]{:S(2)}, u32[]{:S(2)}) %collective-permute-start.10) | collective-permute-done | bytes 393248 | tf_op jit(solution)/shard_map/ppermute | solution.py:26
  44.0 7.8 %collective-permute-done.9 = bf16[2,2,16,3072]{3,2,0,1:T(8,128)(2,1)S(1)} collective-permute-done((bf16[2,2,16,3072]{3,2,0,1:T(8,128)(2,1)S(1)}, bf16[2,2,16,3072]{3,2,0,1:T(8,128)(2,1)S(1)}, u32[]{:S(2)}, u32[]{:S(2)}) %collective-permute-start.9) | collective-permute-done | bytes 393248 | tf_op jit(solution)/shard_map/ppermute | solution.py:26
  52.0 4.5 %collective-permute-done.12 = bf16[2,4,16,3072]{3,2,0,1:T(8,128)(2,1)S(1)} collective-permute-done((bf16[2,4,16,3072]{3,2,0,1:T(8,128)(2,1)S(1)}, bf16[2,4,16,3072]{3,2,0,1:T(8,128)(2,1)S(1)}, u32[]{:S(2)}, u32[]{:S(2)}) %collective-permute-start.12) | collective-permute-done | bytes 786464 | tf_op jit(solution)/shard_map/ppermute | solution.py:26
  56.9 1.5 %collective-permute-start.16 = (bf16[2,16,3072]{2,1,0:T(8,128)(2,1)S(1)}, bf16[2,16,3072]{2,1,0:T(8,128)(2,1)S(1)}, u32[]{:S(2)}, u32[]{:S(2)}) collective-permute-start(bf16[2,16,3072]{2,1,0:T(8,128)(2,1)S(1)} %get-tuple-element.53), channel_id=1, source_target_pairs={{64,0},{72,8},{80,16},{88,24},{96,32},{104,40},{112,48},{120,56},{... | collective-permute-start | bytes 589832 | tf_op jit(solution)/shard_map/ppermute | solution.py:26
  58.4 1.9 %collective-permute-start.15 = (bf16[2,16,3072]{2,1,0:T(8,128)(2,1)S(1)}, bf16[2,16,3072]{2,1,0:T(8,128)(2,1)S(1)}, u32[]{:S(2)}, u32[]{:S(2)}) collective-permute-start(bf16[2,16,3072]{2,1,0:T(8,128)(2,1)S(1)} %get-tuple-element.54), channel_id=1, source_target_pairs={{32,0},{40,8},{48,16},{56,24},{64,32},{72,40},{80,48},{88,56},{96,... | collective-permute-start | bytes 589832 | tf_op jit(solution)/shard_map/ppermute | solution.py:26
  60.5 2.8 %collective-permute-start.13 = (bf16[2,16,3072]{2,1,0:T(8,128)(2,1)S(1)}, bf16[2,16,3072]{2,1,0:T(8,128)(2,1)S(1)}, u32[]{:S(2)}, u32[]{:S(2)}) collective-permute-start(bf16[2,16,3072]{2,1,0:T(8,128)(2,1)S(1)} %fusion.21), channel_id=1, source_target_pairs={{16,0},{24,8},{0,16},{8,24},{48,32},{56,40},{32,48},{40,56},{80,64... | collective-permute-start | bytes 589832 | tf_op jit(solution)/shard_map/ppermute | solution.py:26
  63.3 2.5 %collective-permute-done.16 = bf16[2,16,3072]{2,1,0:T(8,128)(2,1)S(1)} collective-permute-done((bf16[2,16,3072]{2,1,0:T(8,128)(2,1)S(1)}, bf16[2,16,3072]{2,1,0:T(8,128)(2,1)S(1)}, u32[]{:S(2)}, u32[]{:S(2)}) %collective-permute-start.16) | collective-permute-done | bytes 196640 | tf_op jit(solution)/shard_map/ppermute | solution.py:26
  65.8 1.6 %collective-permute-done.15 = bf16[2,16,3072]{2,1,0:T(8,128)(2,1)S(1)} collective-permute-done((bf16[2,16,3072]{2,1,0:T(8,128)(2,1)S(1)}, bf16[2,16,3072]{2,1,0:T(8,128)(2,1)S(1)}, u32[]{:S(2)}, u32[]{:S(2)}) %collective-permute-start.15) | collective-permute-done | bytes 196640 | tf_op jit(solution)/shard_map/ppermute | solution.py:26
  67.4 0.8 collective-permute-done.14
  68.7 1.2 collective-permute-start.19
  69.9 2.9 %collective-permute-start.18 = (bf16[2,16,3072]{2,1,0:T(8,128)(2,1)S(1)}, bf16[2,16,3072]{2,1,0:T(8,128)(2,1)S(1)}, u32[]{:S(2)}, u32[]{:S(2)}) collective-permute-start(bf16[2,16,3072]{2,1,0:T(8,128)(2,1)S(1)} %get-tuple-element.38), channel_id=1, source_target_pairs={{64,0},{72,8},{80,16},{88,24},{96,32},{104,40},{112,48},{120,56},{... | collective-permute-start | bytes 589832 | tf_op jit(solution)/shard_map/ppermute | solution.py:26
  73.4 2.7 %collective-permute-start.20 = (bf16[2,16,3072]{2,1,0:T(8,128)(2,1)S(1)}, bf16[2,16,3072]{2,1,0:T(8,128)(2,1)S(1)}, u32[]{:S(2)}, u32[]{:S(2)}) collective-permute-start(bf16[2,16,3072]{2,1,0:T(8,128)(2,1)S(1)} %get-tuple-element.39), channel_id=1, source_target_pairs={{16,0},{24,8},{0,16},{8,24},{48,32},{56,40},{32,48},{40,56},{80,64... | collective-permute-start | bytes 589832 | tf_op jit(solution)/shard_map/ppermute | solution.py:26
  76.1 1.8 %collective-permute-done.19 = bf16[2,16,3072]{2,1,0:T(8,128)(2,1)S(1)} collective-permute-done((bf16[2,16,3072]{2,1,0:T(8,128)(2,1)S(1)}, bf16[2,16,3072]{2,1,0:T(8,128)(2,1)S(1)}, u32[]{:S(2)}, u32[]{:S(2)}) %collective-permute-start.19) | collective-permute-done | bytes 196640 | tf_op jit(solution)/shard_map/ppermute | solution.py:26
  77.9 2.4 %collective-permute-done.18 = bf16[2,16,3072]{2,1,0:T(8,128)(2,1)S(1)} collective-permute-done((bf16[2,16,3072]{2,1,0:T(8,128)(2,1)S(1)}, bf16[2,16,3072]{2,1,0:T(8,128)(2,1)S(1)}, u32[]{:S(2)}, u32[]{:S(2)}) %collective-permute-start.18) | collective-permute-done | bytes 196640 | tf_op jit(solution)/shard_map/ppermute | solution.py:26
  80.7 1.6 %collective-permute-start.25 = (bf16[2,2,16,3072]{3,2,0,1:T(8,128)(2,1)S(1)}, bf16[2,2,16,3072]{3,2,0,1:T(8,128)(2,1)S(1)}, u32[]{:S(2)}, u32[]{:S(2)}) collective-permute-start(bf16[2,2,16,3072]{3,2,0,1:T(8,128)(2,1)S(1)} %pad_maximum_fusion.7), channel_id=1, source_target_pairs={{96,0},{104,8},{112,16},{120,24},{0,32},{8,40},{16,48},{24,56},{32... | collective-permute-start | bytes 1179656 | tf_op jit(solution)/shard_map/ppermute | solution.py:26
  82.2 2.2 %collective-permute-start.24 = (bf16[2,2,16,3072]{3,2,0,1:T(8,128)(2,1)S(1)}, bf16[2,2,16,3072]{3,2,0,1:T(8,128)(2,1)S(1)}, u32[]{:S(2)}, u32[]{:S(2)}) collective-permute-start(bf16[2,2,16,3072]{3,2,0,1:T(8,128)(2,1)S(1)} %pad_maximum_fusion.7), channel_id=1, source_target_pairs={{64,0},{72,8},{80,16},{88,24},{96,32},{104,40},{112,48},{120,56},{... | collective-permute-start | bytes 1179656 | tf_op jit(solution)/shard_map/ppermute | solution.py:26
  84.5 1.1 collective-permute-start.23
  85.6 2.8 %collective-permute-start.21 = (bf16[4,2,16,3072]{3,2,0,1:T(8,128)(2,1)S(1)}, bf16[4,2,16,3072]{3,2,0,1:T(8,128)(2,1)S(1)}, u32[]{:S(2)}, u32[]{:S(2)}) collective-permute-start(bf16[4,2,16,3072]{3,2,0,1:T(8,128)(2,1)S(1)} %copy.15), channel_id=1, source_target_pairs={{16,0},{24,8},{0,16},{8,24},{48,32},{56,40},{32,48},{40,56},{80,64... | collective-permute-start | bytes 2359304 | tf_op jit(solution)/shard_map/ppermute | solution.py:26
  88.4 3.7 %collective-permute-done.25 = bf16[2,2,16,3072]{3,2,0,1:T(8,128)(2,1)S(1)} collective-permute-done((bf16[2,2,16,3072]{3,2,0,1:T(8,128)(2,1)S(1)}, bf16[2,2,16,3072]{3,2,0,1:T(8,128)(2,1)S(1)}, u32[]{:S(2)}, u32[]{:S(2)}) %collective-permute-start.25) | collective-permute-done | bytes 393248 | tf_op jit(solution)/shard_map/ppermute | solution.py:26
  92.2 8.4 %collective-permute-done.24 = bf16[2,2,16,3072]{3,2,0,1:T(8,128)(2,1)S(1)} collective-permute-done((bf16[2,2,16,3072]{3,2,0,1:T(8,128)(2,1)S(1)}, bf16[2,2,16,3072]{3,2,0,1:T(8,128)(2,1)S(1)}, u32[]{:S(2)}, u32[]{:S(2)}) %collective-permute-start.24) | collective-permute-done | bytes 393248 | tf_op jit(solution)/shard_map/ppermute | solution.py:26
  101.5 3.1 %collective-permute-done.21 = bf16[4,2,16,3072]{3,2,0,1:T(8,128)(2,1)S(1)} collective-permute-done((bf16[4,2,16,3072]{3,2,0,1:T(8,128)(2,1)S(1)}, bf16[4,2,16,3072]{3,2,0,1:T(8,128)(2,1)S(1)}, u32[]{:S(2)}, u32[]{:S(2)}) %collective-permute-start.21) | collective-permute-done | bytes 786464 | tf_op jit(solution)/shard_map/ppermute | solution.py:26
  105.5 2.0 %shard_map.73 = f32[256,768]{1,0:T(8,128)S(1)} custom-call(s32[16]{0:T(128)S(1)} %fusion.31.place_ref, bf16[4,2,16,3072]{3,2,1,0:T(8,128)(2,1)S(1)} %pad_maximum_fusion.4.refs_2_.own_ref, bf16[4,2,16,3072]{3,2,1,0:T(8,128)(2,1)S(1)} %collective-permute-done.26.refs_3_.other_ref, bf16[768,3072]{1,0:T(8,128)(2,1)S(1)} %get-tuple-element.26.in_ref.weight_ref), custom_call_target="tpu_custom_call" | custom-call | flops 1 | bytes 1 | tf_op jit(solution)/shard_map/pallas_call | solution.py:136
  107.5 2.2 %collective-permute-start.35 = (bf16[64,768]{1,0:T(8,128)(2,1)S(1)}, bf16[64,768]{1,0:T(8,128)(2,1)S(1)}, u32[]{:S(2)}, u32[]{:S(2)}) collective-permute-start(bf16[64,768]{1,0:T(8,128)(2,1)S(1)} %get-tuple-element.59), channel_id=1, source_target_pairs={{6,0},{7,1},{4,2},{5,3},{2,4},{3,5},{0,6},{1,7},{14,8},{15,9},{12,... | collective-permute-start | bytes 294920 | tf_op jit(solution)/shard_map/ppermute | solution.py:30
  109.8 2.5 %collective-permute-start.34 = (bf16[64,768]{1,0:T(8,128)(2,1)S(1)}, bf16[64,768]{1,0:T(8,128)(2,1)S(1)}, u32[]{:S(2)}, u32[]{:S(2)}) collective-permute-start(bf16[64,768]{1,0:T(8,128)(2,1)S(1)} %get-tuple-element.60), channel_id=1, source_target_pairs={{5,0},{6,1},{7,2},{4,3},{1,4},{2,5},{3,6},{0,7},{13,8},{14,9},{15,... | collective-permute-start | bytes 294920 | tf_op jit(solution)/shard_map/ppermute | solution.py:30
  112.7 2.0 %shard_map.72 = f32[256,768]{1,0:T(8,128)S(1)} custom-call(s32[16]{0:T(128)S(1)} %fusion.29.place_ref, bf16[2,4,16,3072]{3,2,1,0:T(8,128)(2,1)S(1)} %pad_maximum_fusion.3.refs_0_.own_ref, bf16[2,4,16,3072]{3,2,1,0:T(8,128)(2,1)S(1)} %collective-permute-done.22.refs_1_.other_ref, bf16[768,3072]{1,0:T(8,128)(2,1)S(1)} %get-tuple-element.26.in_ref.weight_ref), custom_call_target="tpu_custom_call" | custom-call | flops 1 | bytes 1 | tf_op jit(solution)/shard_map/pallas_call | solution.py:136
  114.8 1.6 %collective-permute-start.32 = (bf16[64,768]{1,0:T(8,128)(2,1)S(1)}, bf16[64,768]{1,0:T(8,128)(2,1)S(1)}, u32[]{:S(2)}, u32[]{:S(2)}) collective-permute-start(bf16[64,768]{1,0:T(8,128)(2,1)S(1)} %get-tuple-element.58), channel_id=1, source_target_pairs={{4,0},{5,1},{6,2},{7,3},{0,4},{1,5},{2,6},{3,7},{12,8},{13,9},{14,... | collective-permute-start | bytes 294920 | tf_op jit(solution)/shard_map/ppermute | solution.py:30
  116.4 1.4 %collective-permute-start.31 = (bf16[64,768]{1,0:T(8,128)(2,1)S(1)}, bf16[64,768]{1,0:T(8,128)(2,1)S(1)}, u32[]{:S(2)}, u32[]{:S(2)}) collective-permute-start(bf16[64,768]{1,0:T(8,128)(2,1)S(1)} %get-tuple-element.56), channel_id=1, source_target_pairs={{2,0},{3,1},{0,2},{1,3},{6,4},{7,5},{4,6},{5,7},{10,8},{11,9},{8,1... | collective-permute-start | bytes 294920 | tf_op jit(solution)/shard_map/ppermute | solution.py:30
  117.8 2.4 %collective-permute-start.30 = (bf16[64,768]{1,0:T(8,128)(2,1)S(1)}, bf16[64,768]{1,0:T(8,128)(2,1)S(1)}, u32[]{:S(2)}, u32[]{:S(2)}) collective-permute-start(bf16[64,768]{1,0:T(8,128)(2,1)S(1)} %get-tuple-element.57), channel_id=1, source_target_pairs={{1,0},{2,1},{3,2},{0,3},{5,4},{6,5},{7,6},{4,7},{9,8},{10,9},{11,1... | collective-permute-start | bytes 294920 | tf_op jit(solution)/shard_map/ppermute | solution.py:30
  120.3 3.6 %shard_map.70 = bf16[768,3072]{1,0:T(8,128)(2,1)} custom-call(bf16[2,4,16,3072]{3,2,1,0:T(8,128)(2,1)S(1)} %pad_maximum_fusion.3.refs_0_.own_ref, bf16[2,4,16,3072]{3,2,1,0:T(8,128)(2,1)S(1)} %collective-permute-done.22.refs_1_.other_ref, bf16[4,2,16,3072]{3,2,1,0:T(8,128)(2,1)S(1)} %pad_maximum_fusion.4.refs_2_.own_ref, ...), custom_call_target="tpu_custom_call" | custom-call | flops 1 | bytes 1 | tf_op jit(solution)/shard_map/pallas_call | solution.py:175
  123.9 3.7 %shard_map.71 = bf16[3072,768]{1,0:T(8,128)(2,1)} custom-call(bf16[2,4,16,3072]{3,2,1,0:T(8,128)(2,1)S(1)} %pad_maximum_fusion.5.refs_0_, bf16[2,4,16,3072]{3,2,1,0:T(8,128)(2,1)S(1)} %collective-permute-done.27.refs_1_, bf16[4,2,16,3072]{3,2,1,0:T(8,128)(2,1)S(1)} %pad_maximum_fusion.6.refs_2_, ...), custom_call_target="tpu_custom_call" | custom-call | flops 1 | bytes 1 | tf_op jit(solution)/shard_map/pallas_call | solution.py:175
  127.6 0.7 fusion.28
  (69 shorter events, 6.2 us)
Async XLA Ops:
  1.6 8.2 %collective-permute-start = (bf16[2,64,768]{2,1,0:T(8,128)(2,1)S(1)}, bf16[2,64,768]{2,1,0:T(8,128)(2,1)S(1)}, u32[]{:S(2)}, u32[]{:S(2)}) collective-permute-start(bf16[2,64,768]{2,1,0:T(8,128)(2,1)S(1)} %pad_maximum_fusion.8), channel_id=1, source_target_pairs={{4,0},{5,1},{6,2},{7,3},{0,4},{1,5},{2,6},{3,7},{12,8},{13,9},{14,... | collective-permute-start | bytes 589832 | tf_op jit(solution)/shard_map/ppermute | solution.py:30
  3.2 10.7 %collective-permute-start.3 = (bf16[2,64,768]{2,1,0:T(8,128)(2,1)S(1)}, bf16[2,64,768]{2,1,0:T(8,128)(2,1)S(1)}, u32[]{:S(2)}, u32[]{:S(2)}) collective-permute-start(bf16[2,64,768]{2,1,0:T(8,128)(2,1)S(1)} %pad_maximum_fusion.8), channel_id=1, source_target_pairs={{3,0},{0,1},{1,2},{2,3},{7,4},{4,5},{5,6},{6,7},{11,8},{8,9},{9,10... | collective-permute-start | bytes 589832 | tf_op jit(solution)/shard_map/ppermute | solution.py:30
  5.2 13.8 %collective-permute-start.2 = (bf16[2,64,768]{2,1,0:T(8,128)(2,1)S(1)}, bf16[2,64,768]{2,1,0:T(8,128)(2,1)S(1)}, u32[]{:S(2)}, u32[]{:S(2)}) collective-permute-start(bf16[2,64,768]{2,1,0:T(8,128)(2,1)S(1)} %pad_maximum_fusion.8), channel_id=1, source_target_pairs={{2,0},{3,1},{0,2},{1,3},{6,4},{7,5},{4,6},{5,7},{10,8},{11,9},{8,1... | collective-permute-start | bytes 589832 | tf_op jit(solution)/shard_map/ppermute | solution.py:30
  8.7 10.2 %collective-permute-start.1 = (bf16[2,64,768]{2,1,0:T(8,128)(2,1)S(1)}, bf16[2,64,768]{2,1,0:T(8,128)(2,1)S(1)}, u32[]{:S(2)}, u32[]{:S(2)}) collective-permute-start(bf16[2,64,768]{2,1,0:T(8,128)(2,1)S(1)} %pad_maximum_fusion.8), channel_id=1, source_target_pairs={{1,0},{2,1},{3,2},{0,3},{5,4},{6,5},{7,6},{4,7},{9,8},{10,9},{11,1... | collective-permute-start | bytes 589832 | tf_op jit(solution)/shard_map/ppermute | solution.py:30
  9.8 12.5 %collective-permute-start.6 = (bf16[2,64,768]{2,1,0:T(8,128)(2,1)S(1)}, bf16[2,64,768]{2,1,0:T(8,128)(2,1)S(1)}, u32[]{:S(2)}, u32[]{:S(2)}) collective-permute-start(bf16[2,64,768]{2,1,0:T(8,128)(2,1)S(1)} %collective-permute-done), channel_id=1, source_target_pairs={{3,0},{0,1},{1,2},{2,3},{7,4},{4,5},{5,6},{6,7},{11,8},{8,9},{9,10... | collective-permute-start | bytes 589832 | tf_op jit(solution)/shard_map/ppermute | solution.py:30
  10.8 15.0 %collective-permute-start.5 = (bf16[2,64,768]{2,1,0:T(8,128)(2,1)S(1)}, bf16[2,64,768]{2,1,0:T(8,128)(2,1)S(1)}, u32[]{:S(2)}, u32[]{:S(2)}) collective-permute-start(bf16[2,64,768]{2,1,0:T(8,128)(2,1)S(1)} %collective-permute-done), channel_id=1, source_target_pairs={{2,0},{3,1},{0,2},{1,3},{6,4},{7,5},{4,6},{5,7},{10,8},{11,9},{8,1... | collective-permute-start | bytes 589832 | tf_op jit(solution)/shard_map/ppermute | solution.py:30
  13.9 11.9 %collective-permute-start.4 = (bf16[2,64,768]{2,1,0:T(8,128)(2,1)S(1)}, bf16[2,64,768]{2,1,0:T(8,128)(2,1)S(1)}, u32[]{:S(2)}, u32[]{:S(2)}) collective-permute-start(bf16[2,64,768]{2,1,0:T(8,128)(2,1)S(1)} %collective-permute-done), channel_id=1, source_target_pairs={{1,0},{2,1},{3,2},{0,3},{5,4},{6,5},{7,6},{4,7},{9,8},{10,9},{11,1... | collective-permute-start | bytes 589832 | tf_op jit(solution)/shard_map/ppermute | solution.py:30
  25.9 3.9 %collective-permute-start.7 = (bf16[2,128,3072]{2,1,0:T(8,128)(2,1)S(1)}, bf16[2,128,3072]{2,1,0:T(8,128)(2,1)S(1)}, u32[]{:S(2)}, u32[]{:S(2)}) collective-permute-start(bf16[2,128,3072]{2,1,0:T(8,128)(2,1)S(1)} %get-tuple-element.31), channel_id=1, source_target_pairs={{8,0},{0,8},{24,16},{16,24},{40,32},{32,40},{56,48},{48,56},{72,64... | collective-permute-start | bytes 4718600 | tf_op jit(solution)/shard_map/ppermute | solution.py:26
  29.2 6.6 %collective-permute-start.11 = (bf16[2,128,3072]{2,1,0:T(8,128)(2,1)S(1)}, bf16[2,128,3072]{2,1,0:T(8,128)(2,1)S(1)}, u32[]{:S(2)}, u32[]{:S(2)}) collective-permute-start(bf16[2,128,3072]{2,1,0:T(8,128)(2,1)S(1)} %get-tuple-element.34), channel_id=1, source_target_pairs={{8,0},{0,8},{24,16},{16,24},{40,32},{32,40},{56,48},{48,56},{72,64... | collective-permute-start | bytes 4718600 | tf_op jit(solution)/shard_map/ppermute | solution.py:26
  30.4 13.6 %collective-permute-start.10 = (bf16[2,2,16,3072]{3,2,0,1:T(8,128)(2,1)S(1)}, bf16[2,2,16,3072]{3,2,0,1:T(8,128)(2,1)S(1)}, u32[]{:S(2)}, u32[]{:S(2)}) collective-permute-start(bf16[2,2,16,3072]{3,2,0,1:T(8,128)(2,1)S(1)} %get-tuple-element.48), channel_id=1, source_target_pairs={{64,0},{72,8},{80,16},{88,24},{96,32},{104,40},{112,48},{120,56},{... | collective-permute-start | bytes 1179656 | tf_op jit(solution)/shard_map/ppermute | solution.py:26
  33.7 18.2 %collective-permute-start.9 = (bf16[2,2,16,3072]{3,2,0,1:T(8,128)(2,1)S(1)}, bf16[2,2,16,3072]{3,2,0,1:T(8,128)(2,1)S(1)}, u32[]{:S(2)}, u32[]{:S(2)}) collective-permute-start(bf16[2,2,16,3072]{3,2,0,1:T(8,128)(2,1)S(1)} %get-tuple-element.49), channel_id=1, source_target_pairs={{32,0},{40,8},{48,16},{56,24},{64,32},{72,40},{80,48},{88,56},{96,... | collective-permute-start | bytes 1179656 | tf_op jit(solution)/shard_map/ppermute | solution.py:26
  34.8 17.1 %collective-permute-start.8 = (bf16[2,2,16,3072]{3,2,0,1:T(8,128)(2,1)S(1)}, bf16[2,2,16,3072]{3,2,0,1:T(8,128)(2,1)S(1)}, u32[]{:S(2)}, u32[]{:S(2)}) collective-permute-start(bf16[2,2,16,3072]{3,2,0,1:T(8,128)(2,1)S(1)} %get-tuple-element.47), channel_id=1, source_target_pairs={{96,0},{104,8},{112,16},{120,24},{0,32},{8,40},{16,48},{24,56},{32... | collective-permute-start | bytes 1179656 | tf_op jit(solution)/shard_map/ppermute | solution.py:26
  36.4 20.2 %collective-permute-start.12 = (bf16[2,4,16,3072]{3,2,0,1:T(8,128)(2,1)S(1)}, bf16[2,4,16,3072]{3,2,0,1:T(8,128)(2,1)S(1)}, u32[]{:S(2)}, u32[]{:S(2)}) collective-permute-start(bf16[2,4,16,3072]{3,2,0,1:T(8,128)(2,1)S(1)} %fusion.1), channel_id=1, source_target_pairs={{16,0},{24,8},{0,16},{8,24},{48,32},{56,40},{32,48},{40,56},{80,64... | collective-permute-start | bytes 2359304 | tf_op jit(solution)/shard_map/ppermute | solution.py:26
  56.9 8.9 %collective-permute-start.16 = (bf16[2,16,3072]{2,1,0:T(8,128)(2,1)S(1)}, bf16[2,16,3072]{2,1,0:T(8,128)(2,1)S(1)}, u32[]{:S(2)}, u32[]{:S(2)}) collective-permute-start(bf16[2,16,3072]{2,1,0:T(8,128)(2,1)S(1)} %get-tuple-element.53), channel_id=1, source_target_pairs={{64,0},{72,8},{80,16},{88,24},{96,32},{104,40},{112,48},{120,56},{... | collective-permute-start | bytes 589832 | tf_op jit(solution)/shard_map/ppermute | solution.py:26
  58.4 9.0 %collective-permute-start.15 = (bf16[2,16,3072]{2,1,0:T(8,128)(2,1)S(1)}, bf16[2,16,3072]{2,1,0:T(8,128)(2,1)S(1)}, u32[]{:S(2)}, u32[]{:S(2)}) collective-permute-start(bf16[2,16,3072]{2,1,0:T(8,128)(2,1)S(1)} %get-tuple-element.54), channel_id=1, source_target_pairs={{32,0},{40,8},{48,16},{56,24},{64,32},{72,40},{80,48},{88,56},{96,... | collective-permute-start | bytes 589832 | tf_op jit(solution)/shard_map/ppermute | solution.py:26
  60.4 7.8 %collective-permute-start.14 = (bf16[2,16,3072]{2,1,0:T(8,128)(2,1)S(1)}, bf16[2,16,3072]{2,1,0:T(8,128)(2,1)S(1)}, u32[]{:S(2)}, u32[]{:S(2)}) collective-permute-start(bf16[2,16,3072]{2,1,0:T(8,128)(2,1)S(1)} %get-tuple-element.52), channel_id=1, source_target_pairs={{96,0},{104,8},{112,16},{120,24},{0,32},{8,40},{16,48},{24,56},{32... | collective-permute-start | bytes 589832 | tf_op jit(solution)/shard_map/ppermute | solution.py:26
  60.5 8.0 %collective-permute-start.13 = (bf16[2,16,3072]{2,1,0:T(8,128)(2,1)S(1)}, bf16[2,16,3072]{2,1,0:T(8,128)(2,1)S(1)}, u32[]{:S(2)}, u32[]{:S(2)}) collective-permute-start(bf16[2,16,3072]{2,1,0:T(8,128)(2,1)S(1)} %fusion.21), channel_id=1, source_target_pairs={{16,0},{24,8},{0,16},{8,24},{48,32},{56,40},{32,48},{40,56},{80,64... | collective-permute-start | bytes 589832 | tf_op jit(solution)/shard_map/ppermute | solution.py:26
  68.7 9.2 %collective-permute-start.19 = (bf16[2,16,3072]{2,1,0:T(8,128)(2,1)S(1)}, bf16[2,16,3072]{2,1,0:T(8,128)(2,1)S(1)}, u32[]{:S(2)}, u32[]{:S(2)}) collective-permute-start(bf16[2,16,3072]{2,1,0:T(8,128)(2,1)S(1)} %get-tuple-element.38), channel_id=1, source_target_pairs={{96,0},{104,8},{112,16},{120,24},{0,32},{8,40},{16,48},{24,56},{32... | collective-permute-start | bytes 589832 | tf_op jit(solution)/shard_map/ppermute | solution.py:26
  69.9 10.4 %collective-permute-start.18 = (bf16[2,16,3072]{2,1,0:T(8,128)(2,1)S(1)}, bf16[2,16,3072]{2,1,0:T(8,128)(2,1)S(1)}, u32[]{:S(2)}, u32[]{:S(2)}) collective-permute-start(bf16[2,16,3072]{2,1,0:T(8,128)(2,1)S(1)} %get-tuple-element.38), channel_id=1, source_target_pairs={{64,0},{72,8},{80,16},{88,24},{96,32},{104,40},{112,48},{120,56},{... | collective-permute-start | bytes 589832 | tf_op jit(solution)/shard_map/ppermute | solution.py:26
  72.8 7.5 %collective-permute-start.17 = (bf16[2,16,3072]{2,1,0:T(8,128)(2,1)S(1)}, bf16[2,16,3072]{2,1,0:T(8,128)(2,1)S(1)}, u32[]{:S(2)}, u32[]{:S(2)}) collective-permute-start(bf16[2,16,3072]{2,1,0:T(8,128)(2,1)S(1)} %get-tuple-element.38), channel_id=1, source_target_pairs={{32,0},{40,8},{48,16},{56,24},{64,32},{72,40},{80,48},{88,56},{96,... | collective-permute-start | bytes 589832 | tf_op jit(solution)/shard_map/ppermute | solution.py:26
  73.4 7.2 %collective-permute-start.20 = (bf16[2,16,3072]{2,1,0:T(8,128)(2,1)S(1)}, bf16[2,16,3072]{2,1,0:T(8,128)(2,1)S(1)}, u32[]{:S(2)}, u32[]{:S(2)}) collective-permute-start(bf16[2,16,3072]{2,1,0:T(8,128)(2,1)S(1)} %get-tuple-element.39), channel_id=1, source_target_pairs={{16,0},{24,8},{0,16},{8,24},{48,32},{56,40},{32,48},{40,56},{80,64... | collective-permute-start | bytes 589832 | tf_op jit(solution)/shard_map/ppermute | solution.py:26
  80.7 11.4 %collective-permute-start.25 = (bf16[2,2,16,3072]{3,2,0,1:T(8,128)(2,1)S(1)}, bf16[2,2,16,3072]{3,2,0,1:T(8,128)(2,1)S(1)}, u32[]{:S(2)}, u32[]{:S(2)}) collective-permute-start(bf16[2,2,16,3072]{3,2,0,1:T(8,128)(2,1)S(1)} %pad_maximum_fusion.7), channel_id=1, source_target_pairs={{96,0},{104,8},{112,16},{120,24},{0,32},{8,40},{16,48},{24,56},{32... | collective-permute-start | bytes 1179656 | tf_op jit(solution)/shard_map/ppermute | solution.py:26
  82.2 18.3 %collective-permute-start.24 = (bf16[2,2,16,3072]{3,2,0,1:T(8,128)(2,1)S(1)}, bf16[2,2,16,3072]{3,2,0,1:T(8,128)(2,1)S(1)}, u32[]{:S(2)}, u32[]{:S(2)}) collective-permute-start(bf16[2,2,16,3072]{3,2,0,1:T(8,128)(2,1)S(1)} %pad_maximum_fusion.7), channel_id=1, source_target_pairs={{64,0},{72,8},{80,16},{88,24},{96,32},{104,40},{112,48},{120,56},{... | collective-permute-start | bytes 1179656 | tf_op jit(solution)/shard_map/ppermute | solution.py:26
  84.5 16.1 %collective-permute-start.23 = (bf16[2,2,16,3072]{3,2,0,1:T(8,128)(2,1)S(1)}, bf16[2,2,16,3072]{3,2,0,1:T(8,128)(2,1)S(1)}, u32[]{:S(2)}, u32[]{:S(2)}) collective-permute-start(bf16[2,2,16,3072]{3,2,0,1:T(8,128)(2,1)S(1)} %pad_maximum_fusion.7), channel_id=1, source_target_pairs={{32,0},{40,8},{48,16},{56,24},{64,32},{72,40},{80,48},{88,56},{96,... | collective-permute-start | bytes 1179656 | tf_op jit(solution)/shard_map/ppermute | solution.py:26
  85.6 19.0 %collective-permute-start.21 = (bf16[4,2,16,3072]{3,2,0,1:T(8,128)(2,1)S(1)}, bf16[4,2,16,3072]{3,2,0,1:T(8,128)(2,1)S(1)}, u32[]{:S(2)}, u32[]{:S(2)}) collective-permute-start(bf16[4,2,16,3072]{3,2,0,1:T(8,128)(2,1)S(1)} %copy.15), channel_id=1, source_target_pairs={{16,0},{24,8},{0,16},{8,24},{48,32},{56,40},{32,48},{40,56},{80,64... | collective-permute-start | bytes 2359304 | tf_op jit(solution)/shard_map/ppermute | solution.py:26
  100.7 4.7 %collective-permute-start.26 = (bf16[4,2,16,3072]{3,2,1,0:T(8,128)(2,1)S(1)}, bf16[4,2,16,3072]{3,2,1,0:T(8,128)(2,1)S(1)}, u32[]{:S(2)}, u32[]{:S(2)}) collective-permute-start(bf16[4,2,16,3072]{3,2,1,0:T(8,128)(2,1)S(1)} %pad_maximum_fusion.4.refs_2_.own_ref), channel_id=1, source_target_pairs={{8,0},{0,8},{24,16},{16,24},{40,32},{32,40},{56,48},{48,56},{72,64... | collective-permute-start | bytes 2359304 | tf_op jit(solution)/shard_map/ppermute | solution.py:26
  100.9 13.9 %collective-permute-start.28 = (bf16[4,2,16,3072]{3,2,1,0:T(8,128)(2,1)S(1)}, bf16[4,2,16,3072]{3,2,1,0:T(8,128)(2,1)S(1)}, u32[]{:S(2)}, u32[]{:S(2)}) collective-permute-start(bf16[4,2,16,3072]{3,2,1,0:T(8,128)(2,1)S(1)} %pad_maximum_fusion.6.refs_2_), channel_id=1, source_target_pairs={{8,0},{0,8},{24,16},{16,24},{40,32},{32,40},{56,48},{48,56},{72,64... | collective-permute-start | bytes 2359304 | tf_op jit(solution)/shard_map/ppermute | solution.py:26
  104.7 7.6 %collective-permute-start.22 = (bf16[2,4,16,3072]{3,2,1,0:T(8,128)(2,1)S(1)}, bf16[2,4,16,3072]{3,2,1,0:T(8,128)(2,1)S(1)}, u32[]{:S(2)}, u32[]{:S(2)}) collective-permute-start(bf16[2,4,16,3072]{3,2,1,0:T(8,128)(2,1)S(1)} %pad_maximum_fusion.3.refs_0_.own_ref), channel_id=1, source_target_pairs={{8,0},{0,8},{24,16},{16,24},{40,32},{32,40},{56,48},{48,56},{72,64... | collective-permute-start | bytes 2359304 | tf_op jit(solution)/shard_map/ppermute | solution.py:26
  104.9 15.3 %collective-permute-start.27 = (bf16[2,4,16,3072]{3,2,1,0:T(8,128)(2,1)S(1)}, bf16[2,4,16,3072]{3,2,1,0:T(8,128)(2,1)S(1)}, u32[]{:S(2)}, u32[]{:S(2)}) collective-permute-start(bf16[2,4,16,3072]{3,2,1,0:T(8,128)(2,1)S(1)} %pad_maximum_fusion.5.refs_0_), channel_id=1, source_target_pairs={{8,0},{0,8},{24,16},{16,24},{40,32},{32,40},{56,48},{48,56},{72,64... | collective-permute-start | bytes 2359304 | tf_op jit(solution)/shard_map/ppermute | solution.py:26
  107.5 8.8 %collective-permute-start.35 = (bf16[64,768]{1,0:T(8,128)(2,1)S(1)}, bf16[64,768]{1,0:T(8,128)(2,1)S(1)}, u32[]{:S(2)}, u32[]{:S(2)}) collective-permute-start(bf16[64,768]{1,0:T(8,128)(2,1)S(1)} %get-tuple-element.59), channel_id=1, source_target_pairs={{6,0},{7,1},{4,2},{5,3},{2,4},{3,5},{0,6},{1,7},{14,8},{15,9},{12,... | collective-permute-start | bytes 294920 | tf_op jit(solution)/shard_map/ppermute | solution.py:30
  109.8 8.0 %collective-permute-start.34 = (bf16[64,768]{1,0:T(8,128)(2,1)S(1)}, bf16[64,768]{1,0:T(8,128)(2,1)S(1)}, u32[]{:S(2)}, u32[]{:S(2)}) collective-permute-start(bf16[64,768]{1,0:T(8,128)(2,1)S(1)} %get-tuple-element.60), channel_id=1, source_target_pairs={{5,0},{6,1},{7,2},{4,3},{1,4},{2,5},{3,6},{0,7},{13,8},{14,9},{15,... | collective-permute-start | bytes 294920 | tf_op jit(solution)/shard_map/ppermute | solution.py:30
  112.3 15.3 %collective-permute-start.33 = (bf16[64,768]{1,0:T(8,128)(2,1)S(1)}, bf16[64,768]{1,0:T(8,128)(2,1)S(1)}, u32[]{:S(2)}, u32[]{:S(2)}) collective-permute-start(bf16[64,768]{1,0:T(8,128)(2,1)S(1)} %get-tuple-element.61), channel_id=1, source_target_pairs={{7,0},{4,1},{5,2},{6,3},{3,4},{0,5},{1,6},{2,7},{15,8},{12,9},{13,... | collective-permute-start | bytes 294920 | tf_op jit(solution)/shard_map/ppermute | solution.py:30
  114.8 12.8 %collective-permute-start.32 = (bf16[64,768]{1,0:T(8,128)(2,1)S(1)}, bf16[64,768]{1,0:T(8,128)(2,1)S(1)}, u32[]{:S(2)}, u32[]{:S(2)}) collective-permute-start(bf16[64,768]{1,0:T(8,128)(2,1)S(1)} %get-tuple-element.58), channel_id=1, source_target_pairs={{4,0},{5,1},{6,2},{7,3},{0,4},{1,5},{2,6},{3,7},{12,8},{13,9},{14,... | collective-permute-start | bytes 294920 | tf_op jit(solution)/shard_map/ppermute | solution.py:30
  116.4 11.2 %collective-permute-start.31 = (bf16[64,768]{1,0:T(8,128)(2,1)S(1)}, bf16[64,768]{1,0:T(8,128)(2,1)S(1)}, u32[]{:S(2)}, u32[]{:S(2)}) collective-permute-start(bf16[64,768]{1,0:T(8,128)(2,1)S(1)} %get-tuple-element.56), channel_id=1, source_target_pairs={{2,0},{3,1},{0,2},{1,3},{6,4},{7,5},{4,6},{5,7},{10,8},{11,9},{8,1... | collective-permute-start | bytes 294920 | tf_op jit(solution)/shard_map/ppermute | solution.py:30
  117.8 9.8 %collective-permute-start.30 = (bf16[64,768]{1,0:T(8,128)(2,1)S(1)}, bf16[64,768]{1,0:T(8,128)(2,1)S(1)}, u32[]{:S(2)}, u32[]{:S(2)}) collective-permute-start(bf16[64,768]{1,0:T(8,128)(2,1)S(1)} %get-tuple-element.57), channel_id=1, source_target_pairs={{1,0},{2,1},{3,2},{0,3},{5,4},{6,5},{7,6},{4,7},{9,8},{10,9},{11,1... | collective-permute-start | bytes 294920 | tf_op jit(solution)/shard_map/ppermute | solution.py:30
  120.2 7.5 %collective-permute-start.29 = (bf16[64,768]{1,0:T(8,128)(2,1)S(1)}, bf16[64,768]{1,0:T(8,128)(2,1)S(1)}, u32[]{:S(2)}, u32[]{:S(2)}) collective-permute-start(bf16[64,768]{1,0:T(8,128)(2,1)S(1)} %get-tuple-element.55), channel_id=1, source_target_pairs={{3,0},{0,1},{1,2},{2,3},{7,4},{4,5},{5,6},{6,7},{11,8},{8,9},{9,10... | collective-permute-start | bytes 294920 | tf_op jit(solution)/shard_map/ppermute | solution.py:30

commit v5 on v4

--- a/solution.py
+++ b/solution.py
@@ -58,6 +58,7 @@
 VMEM = pl.BlockSpec(memory_space=pltpu.VMEM)
 SMEM = pl.BlockSpec(memory_space=pltpu.SMEM)
 TILE = 512
+GRAD_TILE = 256
 
 
 def params(mib):
@@ -147,7 +148,7 @@
     hidden = parts[0].shape[-1]
     rows, k = tokens[0].shape
     chunks = len(tokens)
-    steps = hidden // TILE
+    steps = hidden // GRAD_TILE
 
     def body(*refs):
         part_refs, token_refs, out_ref = refs[: 2 * chunks], refs[2 * chunks : 3 * chunks], refs[3 * chunks]
@@ -159,8 +160,8 @@
 
         copies = []
         for i in range(steps):
-            part = pl.ds(i * TILE, TILE)
-            value = jnp.concatenate([ref[:, :, :, part].reshape(rows // 2, TILE) for ref in part_refs])
+            part = pl.ds(i * GRAD_TILE, GRAD_TILE)
+            value = jnp.concatenate([ref[:, :, :, part].reshape(rows // 2, GRAD_TILE) for ref in part_refs])
             if which == 0:
                 made[i] = bf16(contract(value, both, 0, 0))
                 target = out_ref.at[part, :]
@@ -178,7 +179,7 @@
         out_specs=pl.BlockSpec(memory_space=pl.ANY),
         out_shape=jax.ShapeDtypeStruct((hidden, k) if which == 0 else (k, hidden), jnp.bfloat16),
         scratch_shapes=[
-            pltpu.VMEM((steps, TILE, k) if which == 0 else (steps, k, TILE), jnp.bfloat16),
+            pltpu.VMEM((steps, GRAD_TILE, k) if which == 0 else (steps, k, GRAD_TILE), jnp.bfloat16),
             pltpu.SemaphoreType.DMA((steps,)),
         ]
         + ([] if which == 0 else [pltpu.VMEM((k, chunks * rows), jnp.bfloat16)]),

time: 129 us -> 129 us (level)
  no operation moved by 1% of the time
where the time goes in v5:
time: 129 us
  starting transfers between devices  55.7 us (43%)
  waiting for transfers between devices  45.2 us (35%)
  Pallas kernels  21.5 us (17%)
  other arithmetic  4.49 us (3%)
    ppermute x22, waiting for transfers between devices, from_row(): lax.ppermute(a, 'row', [(at_row(y + dy, x + dx, c + dc), at_row(y, x, c))...  41.6 us
    ppermute x22, starting transfers between devices, from_row(): lax.ppermute(a, 'row', [(at_row(y + dy, x + dx, c + dc), at_row(y, x, c))...  31.5 us
    ppermute x14, starting transfers between devices, from_col(): lax.ppermute(a, 'col', [(at_col(x + dx, z + dz), at_col(x, z)) for x, z i...  24.2 us
    pallas_call x2, Pallas kernels, weight_grad(): pl.pallas_call(body, in_specs=[VMEM] * (3 * chunks), out_specs=pl.BlockSp...  7.42 us
    pallas_call x2, Pallas kernels, project(): pl.pallas_call(body, in_specs=[SMEM, VMEM, VMEM, VMEM], out_specs=[VMEM]...  6.33 us
    pallas_call x2, Pallas kernels, back_project(): pl.pallas_call(body, in_specs=[SMEM, VMEM, VMEM, VMEM], out_specs=VMEM, o...  3.95 us
    pallas_call x1, Pallas kernels, loaded(): pl.pallas_call(body, in_specs=[pl.BlockSpec(memory_space=pl.ANY)] * 2, ou...  3.79 us
    ppermute x14, waiting for transfers between devices, from_col(): lax.ppermute(a, 'col', [(at_col(x + dx, z + dz), at_col(x, z)) for x, z i...  3.56 us
  transfers between devices with their start and end apart: 36, of which 13 were waited for; matrix products, arithmetic and copies ran while one was open for 2% of the time, Pallas kernels for 17%

profile of v5, /device:TPU:0, one launch (start us, length us, event | category | flops | bytes accessed | tf_op | source)
XLA Modules:
  0.0 128.5 jit_solution(8858726564887727689)
XLA Ops:
  0.6 1.0 pad_maximum_fusion.8
  1.6 1.7 %collective-permute-start = (bf16[2,64,768]{2,1,0:T(8,128)(2,1)S(1)}, bf16[2,64,768]{2,1,0:T(8,128)(2,1)S(1)}, u32[]{:S(2)}, u32[]{:S(2)}) collective-permute-start(bf16[2,64,768]{2,1,0:T(8,128)(2,1)S(1)} %pad_maximum_fusion.8), channel_id=1, source_target_pairs={{4,0},{5,1},{6,2},{7,3},{0,4},{1,5},{2,6},{3,7},{12,8},{13,9},{14,... | collective-permute-start | bytes 589832 | tf_op jit(solution)/shard_map/ppermute | solution.py:30
  3.2 1.9 %collective-permute-start.3 = (bf16[2,64,768]{2,1,0:T(8,128)(2,1)S(1)}, bf16[2,64,768]{2,1,0:T(8,128)(2,1)S(1)}, u32[]{:S(2)}, u32[]{:S(2)}) collective-permute-start(bf16[2,64,768]{2,1,0:T(8,128)(2,1)S(1)} %pad_maximum_fusion.8), channel_id=1, source_target_pairs={{3,0},{0,1},{1,2},{2,3},{7,4},{4,5},{5,6},{6,7},{11,8},{8,9},{9,10... | collective-permute-start | bytes 589832 | tf_op jit(solution)/shard_map/ppermute | solution.py:30
  5.2 3.6 %collective-permute-start.2 = (bf16[2,64,768]{2,1,0:T(8,128)(2,1)S(1)}, bf16[2,64,768]{2,1,0:T(8,128)(2,1)S(1)}, u32[]{:S(2)}, u32[]{:S(2)}) collective-permute-start(bf16[2,64,768]{2,1,0:T(8,128)(2,1)S(1)} %pad_maximum_fusion.8), channel_id=1, source_target_pairs={{2,0},{3,1},{0,2},{1,3},{6,4},{7,5},{4,6},{5,7},{10,8},{11,9},{8,1... | collective-permute-start | bytes 589832 | tf_op jit(solution)/shard_map/ppermute | solution.py:30
  8.7 1.0 collective-permute-start.1
  9.8 1.0 collective-permute-start.6
  10.8 3.1 %collective-permute-start.5 = (bf16[2,64,768]{2,1,0:T(8,128)(2,1)S(1)}, bf16[2,64,768]{2,1,0:T(8,128)(2,1)S(1)}, u32[]{:S(2)}, u32[]{:S(2)}) collective-permute-start(bf16[2,64,768]{2,1,0:T(8,128)(2,1)S(1)} %collective-permute-done), channel_id=1, source_target_pairs={{2,0},{3,1},{0,2},{1,3},{6,4},{7,5},{4,6},{5,7},{10,8},{11,9},{8,1... | collective-permute-start | bytes 589832 | tf_op jit(solution)/shard_map/ppermute | solution.py:30
  13.9 1.2 collective-permute-start.4
  15.1 3.8 %shard_map.67 = (bf16[768,3072]{1,0:T(8,128)(2,1)S(1)}, bf16[3072,768]{1,0:T(8,128)(2,1)S(1)}) custom-call(bf16[768,3072]{1,0:T(8,128)(2,1)} %first_ref, bf16[3072,768]{1,0:T(8,128)(2,1)} %second_ref.1), custom_call_target="tpu_custom_call" | custom-call | flops 1 | bytes 1 | tf_op jit(solution)/shard_map/pallas_call | solution.py:79
  19.1 3.2 %shard_map.68 = (f32[2,128,3072]{2,1,0:T(8,128)S(1)}, bf16[2,128,3072]{2,1,0:T(8,128)(2,1)S(1)}, bf16[256,768]{1,0:T(8,128)(2,1)S(1)}, bf16[256,768]{1,0:T(8,128)(2,1)S(1)}) custom-call(s32[16]{0:T(128)S(1)} %fusion.29.place_ref, bf16[4,2,64,768]{3,2,1,0:T(8,128)(2,1)S(1)} %pad_maximum_fusion.tokens_ref, ...), custom_call_target="tpu_custom_call" | custom-call | flops 1 | bytes 1 | tf_op jit(solution)/shard_map/pallas_call | solution.py:108
  22.2 3.5 %collective-permute-done.5 = bf16[2,64,768]{2,1,0:T(8,128)(2,1)S(1)} collective-permute-done((bf16[2,64,768]{2,1,0:T(8,128)(2,1)S(1)}, bf16[2,64,768]{2,1,0:T(8,128)(2,1)S(1)}, u32[]{:S(2)}, u32[]{:S(2)}) %collective-permute-start.5) | collective-permute-done | bytes 196640 | tf_op jit(solution)/shard_map/ppermute | solution.py:30
  26.0 3.2 %shard_map.69 = (f32[2,128,3072]{2,1,0:T(8,128)S(1)}, bf16[2,128,3072]{2,1,0:T(8,128)(2,1)S(1)}, bf16[256,768]{1,0:T(8,128)(2,1)S(1)}, bf16[256,768]{1,0:T(8,128)(2,1)S(1)}) custom-call(s32[16]{0:T(128)S(1)} %fusion.31.place_ref, bf16[4,2,64,768]{3,2,1,0:T(8,128)(2,1)S(1)} %pad_maximum_fusion.1.tokens_ref, ...), custom_call_target="tpu_custom_call" | custom-call | flops 1 | bytes 1 | tf_op jit(solution)/shard_map/pallas_call | solution.py:108
  29.2 0.6 collective-permute-start.11
  30.4 3.3 %collective-permute-start.10 = (bf16[2,2,16,3072]{3,2,0,1:T(8,128)(2,1)S(1)}, bf16[2,2,16,3072]{3,2,0,1:T(8,128)(2,1)S(1)}, u32[]{:S(2)}, u32[]{:S(2)}) collective-permute-start(bf16[2,2,16,3072]{3,2,0,1:T(8,128)(2,1)S(1)} %get-tuple-element.48), channel_id=1, source_target_pairs={{64,0},{72,8},{80,16},{88,24},{96,32},{104,40},{112,48},{120,56},{... | collective-permute-start | bytes 1179656 | tf_op jit(solution)/shard_map/ppermute | solution.py:26
  33.7 1.1 collective-permute-start.9
  34.8 1.0 collective-permute-start.8
  36.4 2.8 %collective-permute-start.12 = (bf16[2,4,16,3072]{3,2,0,1:T(8,128)(2,1)S(1)}, bf16[2,4,16,3072]{3,2,0,1:T(8,128)(2,1)S(1)}, u32[]{:S(2)}, u32[]{:S(2)}) collective-permute-start(bf16[2,4,16,3072]{3,2,0,1:T(8,128)(2,1)S(1)} %fusion.1), channel_id=1, source_target_pairs={{16,0},{24,8},{0,16},{8,24},{48,32},{56,40},{32,48},{40,56},{80,64... | collective-permute-start | bytes 2359304 | tf_op jit(solution)/shard_map/ppermute | solution.py:26
  39.2 4.9 %collective-permute-done.10 = bf16[2,2,16,3072]{3,2,0,1:T(8,128)(2,1)S(1)} collective-permute-done((bf16[2,2,16,3072]{3,2,0,1:T(8,128)(2,1)S(1)}, bf16[2,2,16,3072]{3,2,0,1:T(8,128)(2,1)S(1)}, u32[]{:S(2)}, u32[]{:S(2)}) %collective-permute-start.10) | collective-permute-done | bytes 393248 | tf_op jit(solution)/shard_map/ppermute | solution.py:26
  44.0 7.8 %collective-permute-done.9 = bf16[2,2,16,3072]{3,2,0,1:T(8,128)(2,1)S(1)} collective-permute-done((bf16[2,2,16,3072]{3,2,0,1:T(8,128)(2,1)S(1)}, bf16[2,2,16,3072]{3,2,0,1:T(8,128)(2,1)S(1)}, u32[]{:S(2)}, u32[]{:S(2)}) %collective-permute-start.9) | collective-permute-done | bytes 393248 | tf_op jit(solution)/shard_map/ppermute | solution.py:26
  52.0 4.5 %collective-permute-done.12 = bf16[2,4,16,3072]{3,2,0,1:T(8,128)(2,1)S(1)} collective-permute-done((bf16[2,4,16,3072]{3,2,0,1:T(8,128)(2,1)S(1)}, bf16[2,4,16,3072]{3,2,0,1:T(8,128)(2,1)S(1)}, u32[]{:S(2)}, u32[]{:S(2)}) %collective-permute-start.12) | collective-permute-done | bytes 786464 | tf_op jit(solution)/shard_map/ppermute | solution.py:26
  56.9 1.5 %collective-permute-start.16 = (bf16[2,16,3072]{2,1,0:T(8,128)(2,1)S(1)}, bf16[2,16,3072]{2,1,0:T(8,128)(2,1)S(1)}, u32[]{:S(2)}, u32[]{:S(2)}) collective-permute-start(bf16[2,16,3072]{2,1,0:T(8,128)(2,1)S(1)} %get-tuple-element.53), channel_id=1, source_target_pairs={{64,0},{72,8},{80,16},{88,24},{96,32},{104,40},{112,48},{120,56},{... | collective-permute-start | bytes 589832 | tf_op jit(solution)/shard_map/ppermute | solution.py:26
  58.4 1.9 %collective-permute-start.15 = (bf16[2,16,3072]{2,1,0:T(8,128)(2,1)S(1)}, bf16[2,16,3072]{2,1,0:T(8,128)(2,1)S(1)}, u32[]{:S(2)}, u32[]{:S(2)}) collective-permute-start(bf16[2,16,3072]{2,1,0:T(8,128)(2,1)S(1)} %get-tuple-element.54), channel_id=1, source_target_pairs={{32,0},{40,8},{48,16},{56,24},{64,32},{72,40},{80,48},{88,56},{96,... | collective-permute-start | bytes 589832 | tf_op jit(solution)/shard_map/ppermute | solution.py:26
  60.5 2.8 %collective-permute-start.13 = (bf16[2,16,3072]{2,1,0:T(8,128)(2,1)S(1)}, bf16[2,16,3072]{2,1,0:T(8,128)(2,1)S(1)}, u32[]{:S(2)}, u32[]{:S(2)}) collective-permute-start(bf16[2,16,3072]{2,1,0:T(8,128)(2,1)S(1)} %fusion.21), channel_id=1, source_target_pairs={{16,0},{24,8},{0,16},{8,24},{48,32},{56,40},{32,48},{40,56},{80,64... | collective-permute-start | bytes 589832 | tf_op jit(solution)/shard_map/ppermute | solution.py:26
  63.3 2.5 %collective-permute-done.16 = bf16[2,16,3072]{2,1,0:T(8,128)(2,1)S(1)} collective-permute-done((bf16[2,16,3072]{2,1,0:T(8,128)(2,1)S(1)}, bf16[2,16,3072]{2,1,0:T(8,128)(2,1)S(1)}, u32[]{:S(2)}, u32[]{:S(2)}) %collective-permute-start.16) | collective-permute-done | bytes 196640 | tf_op jit(solution)/shard_map/ppermute | solution.py:26
  65.8 1.6 %collective-permute-done.15 = bf16[2,16,3072]{2,1,0:T(8,128)(2,1)S(1)} collective-permute-done((bf16[2,16,3072]{2,1,0:T(8,128)(2,1)S(1)}, bf16[2,16,3072]{2,1,0:T(8,128)(2,1)S(1)}, u32[]{:S(2)}, u32[]{:S(2)}) %collective-permute-start.15) | collective-permute-done | bytes 196640 | tf_op jit(solution)/shard_map/ppermute | solution.py:26
  67.4 0.8 collective-permute-done.14
  68.7 1.2 collective-permute-start.19
  69.9 2.9 %collective-permute-start.18 = (bf16[2,16,3072]{2,1,0:T(8,128)(2,1)S(1)}, bf16[2,16,3072]{2,1,0:T(8,128)(2,1)S(1)}, u32[]{:S(2)}, u32[]{:S(2)}) collective-permute-start(bf16[2,16,3072]{2,1,0:T(8,128)(2,1)S(1)} %get-tuple-element.38), channel_id=1, source_target_pairs={{64,0},{72,8},{80,16},{88,24},{96,32},{104,40},{112,48},{120,56},{... | collective-permute-start | bytes 589832 | tf_op jit(solution)/shard_map/ppermute | solution.py:26
  73.4 2.7 %collective-permute-start.20 = (bf16[2,16,3072]{2,1,0:T(8,128)(2,1)S(1)}, bf16[2,16,3072]{2,1,0:T(8,128)(2,1)S(1)}, u32[]{:S(2)}, u32[]{:S(2)}) collective-permute-start(bf16[2,16,3072]{2,1,0:T(8,128)(2,1)S(1)} %get-tuple-element.39), channel_id=1, source_target_pairs={{16,0},{24,8},{0,16},{8,24},{48,32},{56,40},{32,48},{40,56},{80,64... | collective-permute-start | bytes 589832 | tf_op jit(solution)/shard_map/ppermute | solution.py:26
  76.1 1.8 %collective-permute-done.19 = bf16[2,16,3072]{2,1,0:T(8,128)(2,1)S(1)} collective-permute-done((bf16[2,16,3072]{2,1,0:T(8,128)(2,1)S(1)}, bf16[2,16,3072]{2,1,0:T(8,128)(2,1)S(1)}, u32[]{:S(2)}, u32[]{:S(2)}) %collective-permute-start.19) | collective-permute-done | bytes 196640 | tf_op jit(solution)/shard_map/ppermute | solution.py:26
  77.9 2.4 %collective-permute-done.18 = bf16[2,16,3072]{2,1,0:T(8,128)(2,1)S(1)} collective-permute-done((bf16[2,16,3072]{2,1,0:T(8,128)(2,1)S(1)}, bf16[2,16,3072]{2,1,0:T(8,128)(2,1)S(1)}, u32[]{:S(2)}, u32[]{:S(2)}) %collective-permute-start.18) | collective-permute-done | bytes 196640 | tf_op jit(solution)/shard_map/ppermute | solution.py:26
  80.7 1.6 %collective-permute-start.25 = (bf16[2,2,16,3072]{3,2,0,1:T(8,128)(2,1)S(1)}, bf16[2,2,16,3072]{3,2,0,1:T(8,128)(2,1)S(1)}, u32[]{:S(2)}, u32[]{:S(2)}) collective-permute-start(bf16[2,2,16,3072]{3,2,0,1:T(8,128)(2,1)S(1)} %pad_maximum_fusion.7), channel_id=1, source_target_pairs={{96,0},{104,8},{112,16},{120,24},{0,32},{8,40},{16,48},{24,56},{32... | collective-permute-start | bytes 1179656 | tf_op jit(solution)/shard_map/ppermute | solution.py:26
  82.2 2.2 %collective-permute-start.24 = (bf16[2,2,16,3072]{3,2,0,1:T(8,128)(2,1)S(1)}, bf16[2,2,16,3072]{3,2,0,1:T(8,128)(2,1)S(1)}, u32[]{:S(2)}, u32[]{:S(2)}) collective-permute-start(bf16[2,2,16,3072]{3,2,0,1:T(8,128)(2,1)S(1)} %pad_maximum_fusion.7), channel_id=1, source_target_pairs={{64,0},{72,8},{80,16},{88,24},{96,32},{104,40},{112,48},{120,56},{... | collective-permute-start | bytes 1179656 | tf_op jit(solution)/shard_map/ppermute | solution.py:26
  84.5 1.1 collective-permute-start.23
  85.6 2.8 %collective-permute-start.21 = (bf16[4,2,16,3072]{3,2,0,1:T(8,128)(2,1)S(1)}, bf16[4,2,16,3072]{3,2,0,1:T(8,128)(2,1)S(1)}, u32[]{:S(2)}, u32[]{:S(2)}) collective-permute-start(bf16[4,2,16,3072]{3,2,0,1:T(8,128)(2,1)S(1)} %copy.15), channel_id=1, source_target_pairs={{16,0},{24,8},{0,16},{8,24},{48,32},{56,40},{32,48},{40,56},{80,64... | collective-permute-start | bytes 2359304 | tf_op jit(solution)/shard_map/ppermute | solution.py:26
  88.4 3.7 %collective-permute-done.25 = bf16[2,2,16,3072]{3,2,0,1:T(8,128)(2,1)S(1)} collective-permute-done((bf16[2,2,16,3072]{3,2,0,1:T(8,128)(2,1)S(1)}, bf16[2,2,16,3072]{3,2,0,1:T(8,128)(2,1)S(1)}, u32[]{:S(2)}, u32[]{:S(2)}) %collective-permute-start.25) | collective-permute-done | bytes 393248 | tf_op jit(solution)/shard_map/ppermute | solution.py:26
  92.2 8.4 %collective-permute-done.24 = bf16[2,2,16,3072]{3,2,0,1:T(8,128)(2,1)S(1)} collective-permute-done((bf16[2,2,16,3072]{3,2,0,1:T(8,128)(2,1)S(1)}, bf16[2,2,16,3072]{3,2,0,1:T(8,128)(2,1)S(1)}, u32[]{:S(2)}, u32[]{:S(2)}) %collective-permute-start.24) | collective-permute-done | bytes 393248 | tf_op jit(solution)/shard_map/ppermute | solution.py:26
  101.5 3.1 %collective-permute-done.21 = bf16[4,2,16,3072]{3,2,0,1:T(8,128)(2,1)S(1)} collective-permute-done((bf16[4,2,16,3072]{3,2,0,1:T(8,128)(2,1)S(1)}, bf16[4,2,16,3072]{3,2,0,1:T(8,128)(2,1)S(1)}, u32[]{:S(2)}, u32[]{:S(2)}) %collective-permute-start.21) | collective-permute-done | bytes 786464 | tf_op jit(solution)/shard_map/ppermute | solution.py:26
  105.5 2.0 %shard_map.73 = f32[256,768]{1,0:T(8,128)S(1)} custom-call(s32[16]{0:T(128)S(1)} %fusion.31.place_ref, bf16[4,2,16,3072]{3,2,1,0:T(8,128)(2,1)S(1)} %pad_maximum_fusion.4.refs_2_.own_ref, bf16[4,2,16,3072]{3,2,1,0:T(8,128)(2,1)S(1)} %collective-permute-done.26.refs_3_.other_ref, bf16[768,3072]{1,0:T(8,128)(2,1)S(1)} %get-tuple-element.26.in_ref.weight_ref), custom_call_target="tpu_custom_call" | custom-call | flops 1 | bytes 1 | tf_op jit(solution)/shard_map/pallas_call | solution.py:137
  107.5 2.2 %collective-permute-start.35 = (bf16[64,768]{1,0:T(8,128)(2,1)S(1)}, bf16[64,768]{1,0:T(8,128)(2,1)S(1)}, u32[]{:S(2)}, u32[]{:S(2)}) collective-permute-start(bf16[64,768]{1,0:T(8,128)(2,1)S(1)} %get-tuple-element.59), channel_id=1, source_target_pairs={{6,0},{7,1},{4,2},{5,3},{2,4},{3,5},{0,6},{1,7},{14,8},{15,9},{12,... | collective-permute-start | bytes 294920 | tf_op jit(solution)/shard_map/ppermute | solution.py:30
  109.8 2.5 %collective-permute-start.34 = (bf16[64,768]{1,0:T(8,128)(2,1)S(1)}, bf16[64,768]{1,0:T(8,128)(2,1)S(1)}, u32[]{:S(2)}, u32[]{:S(2)}) collective-permute-start(bf16[64,768]{1,0:T(8,128)(2,1)S(1)} %get-tuple-element.60), channel_id=1, source_target_pairs={{5,0},{6,1},{7,2},{4,3},{1,4},{2,5},{3,6},{0,7},{13,8},{14,9},{15,... | collective-permute-start | bytes 294920 | tf_op jit(solution)/shard_map/ppermute | solution.py:30
  112.7 2.0 %shard_map.72 = f32[256,768]{1,0:T(8,128)S(1)} custom-call(s32[16]{0:T(128)S(1)} %fusion.29.place_ref, bf16[2,4,16,3072]{3,2,1,0:T(8,128)(2,1)S(1)} %pad_maximum_fusion.3.refs_0_.own_ref, bf16[2,4,16,3072]{3,2,1,0:T(8,128)(2,1)S(1)} %collective-permute-done.22.refs_1_.other_ref, bf16[768,3072]{1,0:T(8,128)(2,1)S(1)} %get-tuple-element.26.in_ref.weight_ref), custom_call_target="tpu_custom_call" | custom-call | flops 1 | bytes 1 | tf_op jit(solution)/shard_map/pallas_call | solution.py:137
  114.8 1.6 %collective-permute-start.32 = (bf16[64,768]{1,0:T(8,128)(2,1)S(1)}, bf16[64,768]{1,0:T(8,128)(2,1)S(1)}, u32[]{:S(2)}, u32[]{:S(2)}) collective-permute-start(bf16[64,768]{1,0:T(8,128)(2,1)S(1)} %get-tuple-element.58), channel_id=1, source_target_pairs={{4,0},{5,1},{6,2},{7,3},{0,4},{1,5},{2,6},{3,7},{12,8},{13,9},{14,... | collective-permute-start | bytes 294920 | tf_op jit(solution)/shard_map/ppermute | solution.py:30
  116.4 1.4 %collective-permute-start.31 = (bf16[64,768]{1,0:T(8,128)(2,1)S(1)}, bf16[64,768]{1,0:T(8,128)(2,1)S(1)}, u32[]{:S(2)}, u32[]{:S(2)}) collective-permute-start(bf16[64,768]{1,0:T(8,128)(2,1)S(1)} %get-tuple-element.56), channel_id=1, source_target_pairs={{2,0},{3,1},{0,2},{1,3},{6,4},{7,5},{4,6},{5,7},{10,8},{11,9},{8,1... | collective-permute-start | bytes 294920 | tf_op jit(solution)/shard_map/ppermute | solution.py:30
  117.8 2.4 %collective-permute-start.30 = (bf16[64,768]{1,0:T(8,128)(2,1)S(1)}, bf16[64,768]{1,0:T(8,128)(2,1)S(1)}, u32[]{:S(2)}, u32[]{:S(2)}) collective-permute-start(bf16[64,768]{1,0:T(8,128)(2,1)S(1)} %get-tuple-element.57), channel_id=1, source_target_pairs={{1,0},{2,1},{3,2},{0,3},{5,4},{6,5},{7,6},{4,7},{9,8},{10,9},{11,1... | collective-permute-start | bytes 294920 | tf_op jit(solution)/shard_map/ppermute | solution.py:30
  120.3 3.9 %shard_map.70 = bf16[768,3072]{1,0:T(8,128)(2,1)} custom-call(bf16[2,4,16,3072]{3,2,1,0:T(8,128)(2,1)S(1)} %pad_maximum_fusion.3.refs_0_.own_ref, bf16[2,4,16,3072]{3,2,1,0:T(8,128)(2,1)S(1)} %collective-permute-done.22.refs_1_.other_ref, bf16[4,2,16,3072]{3,2,1,0:T(8,128)(2,1)S(1)} %pad_maximum_fusion.4.refs_2_.own_ref, ...), custom_call_target="tpu_custom_call" | custom-call | flops 1 | bytes 1 | tf_op jit(solution)/shard_map/pallas_call | solution.py:176
  124.2 3.6 %shard_map.71 = bf16[3072,768]{1,0:T(8,128)(2,1)} custom-call(bf16[2,4,16,3072]{3,2,1,0:T(8,128)(2,1)S(1)} %pad_maximum_fusion.5.refs_0_, bf16[2,4,16,3072]{3,2,1,0:T(8,128)(2,1)S(1)} %collective-permute-done.27.refs_1_, bf16[4,2,16,3072]{3,2,1,0:T(8,128)(2,1)S(1)} %pad_maximum_fusion.6.refs_2_, ...), custom_call_target="tpu_custom_call" | custom-call | flops 1 | bytes 1 | tf_op jit(solution)/shard_map/pallas_call | solution.py:176
  127.8 0.7 fusion.28
  (69 shorter events, 6.2 us)
Async XLA Ops:
  1.6 8.2 %collective-permute-start = (bf16[2,64,768]{2,1,0:T(8,128)(2,1)S(1)}, bf16[2,64,768]{2,1,0:T(8,128)(2,1)S(1)}, u32[]{:S(2)}, u32[]{:S(2)}) collective-permute-start(bf16[2,64,768]{2,1,0:T(8,128)(2,1)S(1)} %pad_maximum_fusion.8), channel_id=1, source_target_pairs={{4,0},{5,1},{6,2},{7,3},{0,4},{1,5},{2,6},{3,7},{12,8},{13,9},{14,... | collective-permute-start | bytes 589832 | tf_op jit(solution)/shard_map/ppermute | solution.py:30
  3.2 10.7 %collective-permute-start.3 = (bf16[2,64,768]{2,1,0:T(8,128)(2,1)S(1)}, bf16[2,64,768]{2,1,0:T(8,128)(2,1)S(1)}, u32[]{:S(2)}, u32[]{:S(2)}) collective-permute-start(bf16[2,64,768]{2,1,0:T(8,128)(2,1)S(1)} %pad_maximum_fusion.8), channel_id=1, source_target_pairs={{3,0},{0,1},{1,2},{2,3},{7,4},{4,5},{5,6},{6,7},{11,8},{8,9},{9,10... | collective-permute-start | bytes 589832 | tf_op jit(solution)/shard_map/ppermute | solution.py:30
  5.2 13.8 %collective-permute-start.2 = (bf16[2,64,768]{2,1,0:T(8,128)(2,1)S(1)}, bf16[2,64,768]{2,1,0:T(8,128)(2,1)S(1)}, u32[]{:S(2)}, u32[]{:S(2)}) collective-permute-start(bf16[2,64,768]{2,1,0:T(8,128)(2,1)S(1)} %pad_maximum_fusion.8), channel_id=1, source_target_pairs={{2,0},{3,1},{0,2},{1,3},{6,4},{7,5},{4,6},{5,7},{10,8},{11,9},{8,1... | collective-permute-start | bytes 589832 | tf_op jit(solution)/shard_map/ppermute | solution.py:30
  8.7 10.2 %collective-permute-start.1 = (bf16[2,64,768]{2,1,0:T(8,128)(2,1)S(1)}, bf16[2,64,768]{2,1,0:T(8,128)(2,1)S(1)}, u32[]{:S(2)}, u32[]{:S(2)}) collective-permute-start(bf16[2,64,768]{2,1,0:T(8,128)(2,1)S(1)} %pad_maximum_fusion.8), channel_id=1, source_target_pairs={{1,0},{2,1},{3,2},{0,3},{5,4},{6,5},{7,6},{4,7},{9,8},{10,9},{11,1... | collective-permute-start | bytes 589832 | tf_op jit(solution)/shard_map/ppermute | solution.py:30
  9.8 12.5 %collective-permute-start.6 = (bf16[2,64,768]{2,1,0:T(8,128)(2,1)S(1)}, bf16[2,64,768]{2,1,0:T(8,128)(2,1)S(1)}, u32[]{:S(2)}, u32[]{:S(2)}) collective-permute-start(bf16[2,64,768]{2,1,0:T(8,128)(2,1)S(1)} %collective-permute-done), channel_id=1, source_target_pairs={{3,0},{0,1},{1,2},{2,3},{7,4},{4,5},{5,6},{6,7},{11,8},{8,9},{9,10... | collective-permute-start | bytes 589832 | tf_op jit(solution)/shard_map/ppermute | solution.py:30
  10.8 15.0 %collective-permute-start.5 = (bf16[2,64,768]{2,1,0:T(8,128)(2,1)S(1)}, bf16[2,64,768]{2,1,0:T(8,128)(2,1)S(1)}, u32[]{:S(2)}, u32[]{:S(2)}) collective-permute-start(bf16[2,64,768]{2,1,0:T(8,128)(2,1)S(1)} %collective-permute-done), channel_id=1, source_target_pairs={{2,0},{3,1},{0,2},{1,3},{6,4},{7,5},{4,6},{5,7},{10,8},{11,9},{8,1... | collective-permute-start | bytes 589832 | tf_op jit(solution)/shard_map/ppermute | solution.py:30
  13.9 11.9 %collective-permute-start.4 = (bf16[2,64,768]{2,1,0:T(8,128)(2,1)S(1)}, bf16[2,64,768]{2,1,0:T(8,128)(2,1)S(1)}, u32[]{:S(2)}, u32[]{:S(2)}) collective-permute-start(bf16[2,64,768]{2,1,0:T(8,128)(2,1)S(1)} %collective-permute-done), channel_id=1, source_target_pairs={{1,0},{2,1},{3,2},{0,3},{5,4},{6,5},{7,6},{4,7},{9,8},{10,9},{11,1... | collective-permute-start | bytes 589832 | tf_op jit(solution)/shard_map/ppermute | solution.py:30
  25.9 3.9 %collective-permute-start.7 = (bf16[2,128,3072]{2,1,0:T(8,128)(2,1)S(1)}, bf16[2,128,3072]{2,1,0:T(8,128)(2,1)S(1)}, u32[]{:S(2)}, u32[]{:S(2)}) collective-permute-start(bf16[2,128,3072]{2,1,0:T(8,128)(2,1)S(1)} %get-tuple-element.31), channel_id=1, source_target_pairs={{8,0},{0,8},{24,16},{16,24},{40,32},{32,40},{56,48},{48,56},{72,64... | collective-permute-start | bytes 4718600 | tf_op jit(solution)/shard_map/ppermute | solution.py:26
  29.2 6.6 %collective-permute-start.11 = (bf16[2,128,3072]{2,1,0:T(8,128)(2,1)S(1)}, bf16[2,128,3072]{2,1,0:T(8,128)(2,1)S(1)}, u32[]{:S(2)}, u32[]{:S(2)}) collective-permute-start(bf16[2,128,3072]{2,1,0:T(8,128)(2,1)S(1)} %get-tuple-element.34), channel_id=1, source_target_pairs={{8,0},{0,8},{24,16},{16,24},{40,32},{32,40},{56,48},{48,56},{72,64... | collective-permute-start | bytes 4718600 | tf_op jit(solution)/shard_map/ppermute | solution.py:26
  30.4 13.6 %collective-permute-start.10 = (bf16[2,2,16,3072]{3,2,0,1:T(8,128)(2,1)S(1)}, bf16[2,2,16,3072]{3,2,0,1:T(8,128)(2,1)S(1)}, u32[]{:S(2)}, u32[]{:S(2)}) collective-permute-start(bf16[2,2,16,3072]{3,2,0,1:T(8,128)(2,1)S(1)} %get-tuple-element.48), channel_id=1, source_target_pairs={{64,0},{72,8},{80,16},{88,24},{96,32},{104,40},{112,48},{120,56},{... | collective-permute-start | bytes 1179656 | tf_op jit(solution)/shard_map/ppermute | solution.py:26
  33.7 18.2 %collective-permute-start.9 = (bf16[2,2,16,3072]{3,2,0,1:T(8,128)(2,1)S(1)}, bf16[2,2,16,3072]{3,2,0,1:T(8,128)(2,1)S(1)}, u32[]{:S(2)}, u32[]{:S(2)}) collective-permute-start(bf16[2,2,16,3072]{3,2,0,1:T(8,128)(2,1)S(1)} %get-tuple-element.49), channel_id=1, source_target_pairs={{32,0},{40,8},{48,16},{56,24},{64,32},{72,40},{80,48},{88,56},{96,... | collective-permute-start | bytes 1179656 | tf_op jit(solution)/shard_map/ppermute | solution.py:26
  34.8 17.1 %collective-permute-start.8 = (bf16[2,2,16,3072]{3,2,0,1:T(8,128)(2,1)S(1)}, bf16[2,2,16,3072]{3,2,0,1:T(8,128)(2,1)S(1)}, u32[]{:S(2)}, u32[]{:S(2)}) collective-permute-start(bf16[2,2,16,3072]{3,2,0,1:T(8,128)(2,1)S(1)} %get-tuple-element.47), channel_id=1, source_target_pairs={{96,0},{104,8},{112,16},{120,24},{0,32},{8,40},{16,48},{24,56},{32... | collective-permute-start | bytes 1179656 | tf_op jit(solution)/shard_map/ppermute | solution.py:26
  36.4 20.2 %collective-permute-start.12 = (bf16[2,4,16,3072]{3,2,0,1:T(8,128)(2,1)S(1)}, bf16[2,4,16,3072]{3,2,0,1:T(8,128)(2,1)S(1)}, u32[]{:S(2)}, u32[]{:S(2)}) collective-permute-start(bf16[2,4,16,3072]{3,2,0,1:T(8,128)(2,1)S(1)} %fusion.1), channel_id=1, source_target_pairs={{16,0},{24,8},{0,16},{8,24},{48,32},{56,40},{32,48},{40,56},{80,64... | collective-permute-start | bytes 2359304 | tf_op jit(solution)/shard_map/ppermute | solution.py:26
  56.9 8.9 %collective-permute-start.16 = (bf16[2,16,3072]{2,1,0:T(8,128)(2,1)S(1)}, bf16[2,16,3072]{2,1,0:T(8,128)(2,1)S(1)}, u32[]{:S(2)}, u32[]{:S(2)}) collective-permute-start(bf16[2,16,3072]{2,1,0:T(8,128)(2,1)S(1)} %get-tuple-element.53), channel_id=1, source_target_pairs={{64,0},{72,8},{80,16},{88,24},{96,32},{104,40},{112,48},{120,56},{... | collective-permute-start | bytes 589832 | tf_op jit(solution)/shard_map/ppermute | solution.py:26
  58.4 9.0 %collective-permute-start.15 = (bf16[2,16,3072]{2,1,0:T(8,128)(2,1)S(1)}, bf16[2,16,3072]{2,1,0:T(8,128)(2,1)S(1)}, u32[]{:S(2)}, u32[]{:S(2)}) collective-permute-start(bf16[2,16,3072]{2,1,0:T(8,128)(2,1)S(1)} %get-tuple-element.54), channel_id=1, source_target_pairs={{32,0},{40,8},{48,16},{56,24},{64,32},{72,40},{80,48},{88,56},{96,... | collective-permute-start | bytes 589832 | tf_op jit(solution)/shard_map/ppermute | solution.py:26
  60.4 7.8 %collective-permute-start.14 = (bf16[2,16,3072]{2,1,0:T(8,128)(2,1)S(1)}, bf16[2,16,3072]{2,1,0:T(8,128)(2,1)S(1)}, u32[]{:S(2)}, u32[]{:S(2)}) collective-permute-start(bf16[2,16,3072]{2,1,0:T(8,128)(2,1)S(1)} %get-tuple-element.52), channel_id=1, source_target_pairs={{96,0},{104,8},{112,16},{120,24},{0,32},{8,40},{16,48},{24,56},{32... | collective-permute-start | bytes 589832 | tf_op jit(solution)/shard_map/ppermute | solution.py:26
  60.5 8.0 %collective-permute-start.13 = (bf16[2,16,3072]{2,1,0:T(8,128)(2,1)S(1)}, bf16[2,16,3072]{2,1,0:T(8,128)(2,1)S(1)}, u32[]{:S(2)}, u32[]{:S(2)}) collective-permute-start(bf16[2,16,3072]{2,1,0:T(8,128)(2,1)S(1)} %fusion.21), channel_id=1, source_target_pairs={{16,0},{24,8},{0,16},{8,24},{48,32},{56,40},{32,48},{40,56},{80,64... | collective-permute-start | bytes 589832 | tf_op jit(solution)/shard_map/ppermute | solution.py:26
  68.7 9.2 %collective-permute-start.19 = (bf16[2,16,3072]{2,1,0:T(8,128)(2,1)S(1)}, bf16[2,16,3072]{2,1,0:T(8,128)(2,1)S(1)}, u32[]{:S(2)}, u32[]{:S(2)}) collective-permute-start(bf16[2,16,3072]{2,1,0:T(8,128)(2,1)S(1)} %get-tuple-element.38), channel_id=1, source_target_pairs={{96,0},{104,8},{112,16},{120,24},{0,32},{8,40},{16,48},{24,56},{32... | collective-permute-start | bytes 589832 | tf_op jit(solution)/shard_map/ppermute | solution.py:26
  69.9 10.4 %collective-permute-start.18 = (bf16[2,16,3072]{2,1,0:T(8,128)(2,1)S(1)}, bf16[2,16,3072]{2,1,0:T(8,128)(2,1)S(1)}, u32[]{:S(2)}, u32[]{:S(2)}) collective-permute-start(bf16[2,16,3072]{2,1,0:T(8,128)(2,1)S(1)} %get-tuple-element.38), channel_id=1, source_target_pairs={{64,0},{72,8},{80,16},{88,24},{96,32},{104,40},{112,48},{120,56},{... | collective-permute-start | bytes 589832 | tf_op jit(solution)/shard_map/ppermute | solution.py:26
  72.8 7.5 %collective-permute-start.17 = (bf16[2,16,3072]{2,1,0:T(8,128)(2,1)S(1)}, bf16[2,16,3072]{2,1,0:T(8,128)(2,1)S(1)}, u32[]{:S(2)}, u32[]{:S(2)}) collective-permute-start(bf16[2,16,3072]{2,1,0:T(8,128)(2,1)S(1)} %get-tuple-element.38), channel_id=1, source_target_pairs={{32,0},{40,8},{48,16},{56,24},{64,32},{72,40},{80,48},{88,56},{96,... | collective-permute-start | bytes 589832 | tf_op jit(solution)/shard_map/ppermute | solution.py:26
  73.4 7.2 %collective-permute-start.20 = (bf16[2,16,3072]{2,1,0:T(8,128)(2,1)S(1)}, bf16[2,16,3072]{2,1,0:T(8,128)(2,1)S(1)}, u32[]{:S(2)}, u32[]{:S(2)}) collective-permute-start(bf16[2,16,3072]{2,1,0:T(8,128)(2,1)S(1)} %get-tuple-element.39), channel_id=1, source_target_pairs={{16,0},{24,8},{0,16},{8,24},{48,32},{56,40},{32,48},{40,56},{80,64... | collective-permute-start | bytes 589832 | tf_op jit(solution)/shard_map/ppermute | solution.py:26
  80.7 11.4 %collective-permute-start.25 = (bf16[2,2,16,3072]{3,2,0,1:T(8,128)(2,1)S(1)}, bf16[2,2,16,3072]{3,2,0,1:T(8,128)(2,1)S(1)}, u32[]{:S(2)}, u32[]{:S(2)}) collective-permute-start(bf16[2,2,16,3072]{3,2,0,1:T(8,128)(2,1)S(1)} %pad_maximum_fusion.7), channel_id=1, source_target_pairs={{96,0},{104,8},{112,16},{120,24},{0,32},{8,40},{16,48},{24,56},{32... | collective-permute-start | bytes 1179656 | tf_op jit(solution)/shard_map/ppermute | solution.py:26
  82.2 18.3 %collective-permute-start.24 = (bf16[2,2,16,3072]{3,2,0,1:T(8,128)(2,1)S(1)}, bf16[2,2,16,3072]{3,2,0,1:T(8,128)(2,1)S(1)}, u32[]{:S(2)}, u32[]{:S(2)}) collective-permute-start(bf16[2,2,16,3072]{3,2,0,1:T(8,128)(2,1)S(1)} %pad_maximum_fusion.7), channel_id=1, source_target_pairs={{64,0},{72,8},{80,16},{88,24},{96,32},{104,40},{112,48},{120,56},{... | collective-permute-start | bytes 1179656 | tf_op jit(solution)/shard_map/ppermute | solution.py:26
  84.5 16.1 %collective-permute-start.23 = (bf16[2,2,16,3072]{3,2,0,1:T(8,128)(2,1)S(1)}, bf16[2,2,16,3072]{3,2,0,1:T(8,128)(2,1)S(1)}, u32[]{:S(2)}, u32[]{:S(2)}) collective-permute-start(bf16[2,2,16,3072]{3,2,0,1:T(8,128)(2,1)S(1)} %pad_maximum_fusion.7), channel_id=1, source_target_pairs={{32,0},{40,8},{48,16},{56,24},{64,32},{72,40},{80,48},{88,56},{96,... | collective-permute-start | bytes 1179656 | tf_op jit(solution)/shard_map/ppermute | solution.py:26
  85.6 19.0 %collective-permute-start.21 = (bf16[4,2,16,3072]{3,2,0,1:T(8,128)(2,1)S(1)}, bf16[4,2,16,3072]{3,2,0,1:T(8,128)(2,1)S(1)}, u32[]{:S(2)}, u32[]{:S(2)}) collective-permute-start(bf16[4,2,16,3072]{3,2,0,1:T(8,128)(2,1)S(1)} %copy.15), channel_id=1, source_target_pairs={{16,0},{24,8},{0,16},{8,24},{48,32},{56,40},{32,48},{40,56},{80,64... | collective-permute-start | bytes 2359304 | tf_op jit(solution)/shard_map/ppermute | solution.py:26
  100.7 4.7 %collective-permute-start.26 = (bf16[4,2,16,3072]{3,2,1,0:T(8,128)(2,1)S(1)}, bf16[4,2,16,3072]{3,2,1,0:T(8,128)(2,1)S(1)}, u32[]{:S(2)}, u32[]{:S(2)}) collective-permute-start(bf16[4,2,16,3072]{3,2,1,0:T(8,128)(2,1)S(1)} %pad_maximum_fusion.4.refs_2_.own_ref), channel_id=1, source_target_pairs={{8,0},{0,8},{24,16},{16,24},{40,32},{32,40},{56,48},{48,56},{72,64... | collective-permute-start | bytes 2359304 | tf_op jit(solution)/shard_map/ppermute | solution.py:26
  100.9 13.9 %collective-permute-start.28 = (bf16[4,2,16,3072]{3,2,1,0:T(8,128)(2,1)S(1)}, bf16[4,2,16,3072]{3,2,1,0:T(8,128)(2,1)S(1)}, u32[]{:S(2)}, u32[]{:S(2)}) collective-permute-start(bf16[4,2,16,3072]{3,2,1,0:T(8,128)(2,1)S(1)} %pad_maximum_fusion.6.refs_2_), channel_id=1, source_target_pairs={{8,0},{0,8},{24,16},{16,24},{40,32},{32,40},{56,48},{48,56},{72,64... | collective-permute-start | bytes 2359304 | tf_op jit(solution)/shard_map/ppermute | solution.py:26
  104.7 7.6 %collective-permute-start.22 = (bf16[2,4,16,3072]{3,2,1,0:T(8,128)(2,1)S(1)}, bf16[2,4,16,3072]{3,2,1,0:T(8,128)(2,1)S(1)}, u32[]{:S(2)}, u32[]{:S(2)}) collective-permute-start(bf16[2,4,16,3072]{3,2,1,0:T(8,128)(2,1)S(1)} %pad_maximum_fusion.3.refs_0_.own_ref), channel_id=1, source_target_pairs={{8,0},{0,8},{24,16},{16,24},{40,32},{32,40},{56,48},{48,56},{72,64... | collective-permute-start | bytes 2359304 | tf_op jit(solution)/shard_map/ppermute | solution.py:26
  104.9 15.3 %collective-permute-start.27 = (bf16[2,4,16,3072]{3,2,1,0:T(8,128)(2,1)S(1)}, bf16[2,4,16,3072]{3,2,1,0:T(8,128)(2,1)S(1)}, u32[]{:S(2)}, u32[]{:S(2)}) collective-permute-start(bf16[2,4,16,3072]{3,2,1,0:T(8,128)(2,1)S(1)} %pad_maximum_fusion.5.refs_0_), channel_id=1, source_target_pairs={{8,0},{0,8},{24,16},{16,24},{40,32},{32,40},{56,48},{48,56},{72,64... | collective-permute-start | bytes 2359304 | tf_op jit(solution)/shard_map/ppermute | solution.py:26
  107.5 8.8 %collective-permute-start.35 = (bf16[64,768]{1,0:T(8,128)(2,1)S(1)}, bf16[64,768]{1,0:T(8,128)(2,1)S(1)}, u32[]{:S(2)}, u32[]{:S(2)}) collective-permute-start(bf16[64,768]{1,0:T(8,128)(2,1)S(1)} %get-tuple-element.59), channel_id=1, source_target_pairs={{6,0},{7,1},{4,2},{5,3},{2,4},{3,5},{0,6},{1,7},{14,8},{15,9},{12,... | collective-permute-start | bytes 294920 | tf_op jit(solution)/shard_map/ppermute | solution.py:30
  109.8 8.0 %collective-permute-start.34 = (bf16[64,768]{1,0:T(8,128)(2,1)S(1)}, bf16[64,768]{1,0:T(8,128)(2,1)S(1)}, u32[]{:S(2)}, u32[]{:S(2)}) collective-permute-start(bf16[64,768]{1,0:T(8,128)(2,1)S(1)} %get-tuple-element.60), channel_id=1, source_target_pairs={{5,0},{6,1},{7,2},{4,3},{1,4},{2,5},{3,6},{0,7},{13,8},{14,9},{15,... | collective-permute-start | bytes 294920 | tf_op jit(solution)/shard_map/ppermute | solution.py:30
  112.3 15.4 %collective-permute-start.33 = (bf16[64,768]{1,0:T(8,128)(2,1)S(1)}, bf16[64,768]{1,0:T(8,128)(2,1)S(1)}, u32[]{:S(2)}, u32[]{:S(2)}) collective-permute-start(bf16[64,768]{1,0:T(8,128)(2,1)S(1)} %get-tuple-element.61), channel_id=1, source_target_pairs={{7,0},{4,1},{5,2},{6,3},{3,4},{0,5},{1,6},{2,7},{15,8},{12,9},{13,... | collective-permute-start | bytes 294920 | tf_op jit(solution)/shard_map/ppermute | solution.py:30
  114.8 13.0 %collective-permute-start.32 = (bf16[64,768]{1,0:T(8,128)(2,1)S(1)}, bf16[64,768]{1,0:T(8,128)(2,1)S(1)}, u32[]{:S(2)}, u32[]{:S(2)}) collective-permute-start(bf16[64,768]{1,0:T(8,128)(2,1)S(1)} %get-tuple-element.58), channel_id=1, source_target_pairs={{4,0},{5,1},{6,2},{7,3},{0,4},{1,5},{2,6},{3,7},{12,8},{13,9},{14,... | collective-permute-start | bytes 294920 | tf_op jit(solution)/shard_map/ppermute | solution.py:30
  116.4 11.4 %collective-permute-start.31 = (bf16[64,768]{1,0:T(8,128)(2,1)S(1)}, bf16[64,768]{1,0:T(8,128)(2,1)S(1)}, u32[]{:S(2)}, u32[]{:S(2)}) collective-permute-start(bf16[64,768]{1,0:T(8,128)(2,1)S(1)} %get-tuple-element.56), channel_id=1, source_target_pairs={{2,0},{3,1},{0,2},{1,3},{6,4},{7,5},{4,6},{5,7},{10,8},{11,9},{8,1... | collective-permute-start | bytes 294920 | tf_op jit(solution)/shard_map/ppermute | solution.py:30
  117.8 10.0 %collective-permute-start.30 = (bf16[64,768]{1,0:T(8,128)(2,1)S(1)}, bf16[64,768]{1,0:T(8,128)(2,1)S(1)}, u32[]{:S(2)}, u32[]{:S(2)}) collective-permute-start(bf16[64,768]{1,0:T(8,128)(2,1)S(1)} %get-tuple-element.57), channel_id=1, source_target_pairs={{1,0},{2,1},{3,2},{0,3},{5,4},{6,5},{7,6},{4,7},{9,8},{10,9},{11,1... | collective-permute-start | bytes 294920 | tf_op jit(solution)/shard_map/ppermute | solution.py:30
  120.2 7.6 %collective-permute-start.29 = (bf16[64,768]{1,0:T(8,128)(2,1)S(1)}, bf16[64,768]{1,0:T(8,128)(2,1)S(1)}, u32[]{:S(2)}, u32[]{:S(2)}) collective-permute-start(bf16[64,768]{1,0:T(8,128)(2,1)S(1)} %get-tuple-element.55), channel_id=1, source_target_pairs={{3,0},{0,1},{1,2},{2,3},{7,4},{4,5},{5,6},{6,7},{11,8},{8,9},{9,10... | collective-permute-start | bytes 294920 | tf_op jit(solution)/shard_map/ppermute | solution.py:30
